TPU v7x, 32 devices: a whole 2x2x4 slice. The times are simulated.
32 devices in a mesh: dp: 8 (over y, x, core), mp: 4 (over z).
Axes of the slice: x: 2, y: 2, z: 4, core: 2. Of those that a mesh axis runs over, the one named last changes fastest.
Arguments:
- patches: bfloat16 [2048, 6144], P('dp', 'mp'), may hold values from -6 to 6
- dest_group: int32 [2048], P('dp'), may hold values from 0 to 7, as said below
- dest_row: int32 [2048], P('dp'), may hold values from 0 to 255, as said below
- segment: int32 [2048], P('dp'), may hold values from 0 to 15, as said below
- ln_gain: float32 [6144], replicated, may hold values from 0.1 to 1.9
- w_qkv: bfloat16 [6144, 3, 3072], P(None, None, 'mp'), may hold values from -0.078125 to 0.078125
- qk_gain: float32 [2, 128], replicated, may hold values from 0.1 to 1.9
- w_out: bfloat16 [6144, 3072], P(None, 'mp'), may hold values from -0.4375 to 0.4375
- cotangent: bfloat16 [2048, 6144], P('dp', 'mp'), may hold values from -6 to 6
Outputs:
- output: bfloat16 [2048, 6144], P('dp', 'mp')
- input_grad: bfloat16 [2048, 6144], P('dp', 'mp')
- qkv_grad: bfloat16 [6144, 3, 3072], P('dp', None, 'mp')
- out_grad: bfloat16 [6144, 3072], P('dp', 'mp')
Inputs may be any that keep to these rules, and one draw needn't show every extreme that they name: The pairs (dest_group, dest_row) of all rows name every row of every group exactly once. The rows of one group send at most 64 rows to any one group, and in every draw some group sends exactly 64 rows to some group. `dest_row`: see dest_group. `segment`: rows of one group with equal numbers are one image and stand in consecutive rows; numbers lie between 0 and 15.
All inputs are finite; a program needn't handle non-finite values.
Results may differ from a plain program's by a relative error of at most 0.024.
Values may be sent and summed in bfloat16 or wider, within the bound.
No kernel may reach another device: no remote copies, remote signals or barrier semaphores. Data moves between devices by JAX's collectives and lax.ppermute only.
A program may use at most 192 MiB of HBM per device.

v0:
```python
import functools
import math

import jax
import jax.numpy as jnp
from jax import lax
from jax.experimental import pallas as pl
from jax.experimental.pallas import tpu as pltpu
from jax.sharding import PartitionSpec as P

DH = 128
VMEM_BYTES = 48 * 1024 * 1024


def dot_f32(left, right, left_dims, right_dims):
    return lax.dot_general(
        left, right, ((left_dims, right_dims), ((), ())), preferred_element_type=jnp.float32
    )


def params():
    return pltpu.CompilerParams(vmem_limit_bytes=VMEM_BYTES)


def project_kernel(steps, width, x_ref, w_ref, out_ref, total):
    at, t = pl.program_id(0), pl.program_id(1)
    columns = pl.ds(pl.multiple_of(t * width, width), width)
    term = jnp.dot(x_ref[0], w_ref[0], preferred_element_type=jnp.float32)

    @pl.when(at == 0)
    def _():
        total[:, columns] = term

    @pl.when(at > 0)
    def _():
        total[:, columns] += term

    @pl.when(at == steps - 1)
    def _():
        out_ref[:, columns] = total[:, columns].astype(out_ref.dtype)


def project(x, w, steps, dtype):
    _, rows, part = x.shape
    kinds, depth, width = w.shape
    return pl.pallas_call(
        functools.partial(project_kernel, steps, width),
        grid=(steps, kinds),
        in_specs=[
            pl.BlockSpec((1, rows, part), lambda at, t: (at, 0, 0)),
            pl.BlockSpec((1, part, width), lambda at, t: (t, at, 0)),
        ],
        out_specs=pl.BlockSpec((rows, kinds * width), lambda at, t: (0, 0)),
        out_shape=jax.ShapeDtypeStruct((rows, kinds * width), dtype),
        scratch_shapes=[pltpu.VMEM((rows, kinds * width), jnp.float32)],
        compiler_params=params(),
        cost_estimate=pl.CostEstimate(
            flops=2 * rows * depth * kinds * width,
            bytes_accessed=2 * kinds * depth * width + 2 * rows * depth,
            transcendentals=0,
        ),
    )(x, w)


def expand_kernel(kinds, width, x_ref, w_ref, out_ref):
    total = None
    for t in range(kinds):
        term = dot_f32(x_ref[:, t * width : (t + 1) * width], w_ref[t], (1,), (1,))
        total = term if total is None else total + term
    out_ref[0] = total.astype(jnp.bfloat16)


def expand(x, w, parts, cuts):
    rows = x.shape[0]
    kinds, depth, width = w.shape
    part = depth // parts
    piece = part // cuts
    return pl.pallas_call(
        functools.partial(expand_kernel, kinds, width),
        grid=(parts, cuts),
        in_specs=[
            pl.BlockSpec((rows, kinds * width), lambda at, cut: (0, 0)),
            pl.BlockSpec((kinds, piece, width), lambda at, cut: (0, at * cuts + cut, 0)),
        ],
        out_specs=pl.BlockSpec((1, rows, piece), lambda at, cut: (at, 0, cut)),
        out_shape=jax.ShapeDtypeStruct((parts, rows, part), jnp.bfloat16),
        compiler_params=params(),
        cost_estimate=pl.CostEstimate(
            flops=2 * rows * depth * kinds * width,
            bytes_accessed=2 * kinds * depth * width + 2 * rows * depth,
            transcendentals=0,
        ),
    )(x, w)


def unit_heads(raw):
    center = raw - jnp.mean(raw, -1, keepdims=True)
    rstd = lax.rsqrt(jnp.mean(center * center, -1, keepdims=True) + 1e-06)
    return center * rstd, rstd


def head_forward(proj_ref, same, gain_ref, heads, head):
    width = heads * DH
    q_unit, q_rstd = unit_heads(proj_ref[:, head * DH : (head + 1) * DH])
    k_unit, k_rstd = unit_heads(proj_ref[:, width + head * DH : width + (head + 1) * DH])
    values = proj_ref[:, 2 * width + head * DH : 2 * width + (head + 1) * DH].astype(jnp.bfloat16)
    queries = (q_unit * gain_ref[0:1, :]).astype(jnp.bfloat16)
    keys = (k_unit * gain_ref[1:2, :]).astype(jnp.bfloat16)
    scores = dot_f32(queries, keys, (1,), (1,)) * DH ** (-0.5)
    raised = jnp.where(same, jnp.exp(scores), 0.0)
    weights = raised / jnp.sum(raised, -1, keepdims=True)
    return q_unit, q_rstd, k_unit, k_rstd, values, queries, keys, weights


def forward_kernel(heads, proj_ref, row_ref, col_ref, gain_ref, out_ref):
    same = row_ref[...] == col_ref[...]
    for head in range(heads):
        values, _, _, weights = head_forward(proj_ref, same, gain_ref, heads, head)[4:]
        mixed = dot_f32(weights.astype(jnp.bfloat16), values, (1,), (0,))
        out_ref[:, head * DH : (head + 1) * DH] = mixed.astype(jnp.bfloat16)


def unit_backward(grad, unit, rstd, gain):
    scaled = grad.astype(jnp.bfloat16).astype(jnp.float32) * gain
    return rstd * (
        scaled
        - jnp.mean(scaled, -1, keepdims=True)
        - unit * jnp.mean(scaled * unit, -1, keepdims=True)
    )


def backward_kernel(heads, proj_ref, row_ref, col_ref, gain_ref, d_ref, out_ref):
    same = row_ref[...] == col_ref[...]
    width = heads * DH
    for head in range(heads):
        q_unit, q_rstd, k_unit, k_rstd, values, queries, keys, weights = head_forward(
            proj_ref, same, gain_ref, heads, head
        )
        at = head * DH
        weights_bf = weights.astype(jnp.bfloat16)
        d_out = d_ref[:, at : at + DH]
        mixed = dot_f32(weights_bf, values, (1,), (0,))
        out_ref[:, 3 * width + at : 3 * width + at + DH] = mixed.astype(jnp.bfloat16)
        d_values = dot_f32(weights_bf, d_out, (0,), (0,))
        out_ref[:, 2 * width + at : 2 * width + at + DH] = d_values.astype(jnp.bfloat16)
        d_weights = dot_f32(d_out, values, (1,), (1,)).astype(jnp.bfloat16).astype(jnp.float32)
        inner = jnp.sum(d_weights * weights, -1, keepdims=True)
        d_scores = (weights * (d_weights - inner) * DH ** (-0.5)).astype(jnp.bfloat16)
        d_queries = unit_backward(
            dot_f32(d_scores, keys, (1,), (0,)), q_unit, q_rstd, gain_ref[0:1, :]
        )
        d_keys = unit_backward(
            dot_f32(d_scores, queries, (0,), (0,)), k_unit, k_rstd, gain_ref[1:2, :]
        )
        out_ref[:, at : at + DH] = d_queries.astype(jnp.bfloat16)
        out_ref[:, width + at : width + at + DH] = d_keys.astype(jnp.bfloat16)


def attention(kernel, projected, segment, qk_gain, extra, kinds):
    rows, wide = projected.shape
    heads = wide // (3 * DH)
    return pl.pallas_call(
        functools.partial(kernel, heads),
        out_shape=jax.ShapeDtypeStruct((rows, kinds * heads * DH), jnp.bfloat16),
        compiler_params=params(),
        cost_estimate=pl.CostEstimate(
            flops=heads * rows * rows * DH * 16,
            bytes_accessed=rows * wide * 8,
            transcendentals=heads * rows * rows,
        ),
    )(projected, segment.reshape(rows, 1), segment.reshape(1, rows), qk_gain, *extra)


def weight_kernel(count, scale, normed_ref, cot_ref, *refs):
    b_refs, (qkv_ref, out_ref, total) = refs[:count], refs[count:]
    me, t = lax.axis_index("dp"), pl.program_id(0)

    def product(a_ref):
        for k in range(count):
            term = jnp.dot(a_ref[me ^ k], b_refs[k][...], preferred_element_type=jnp.float32)
            total[...] = term if k == 0 else total[...] + term
        return (total[...] * scale).astype(jnp.bfloat16)

    @pl.when(t < 3)
    def _():
        qkv_ref[0] = product(normed_ref)

    @pl.when(t == 3)
    def _():
        out_ref[...] = product(cot_ref)


def weight_grads(normed_cols, cot_cols, gathered, scale):
    count, depth, rows = normed_cols.shape
    width = gathered[0].shape[1] // 4
    whole = pl.BlockSpec((count, depth, rows), lambda t: (0, 0, 0))
    return pl.pallas_call(
        functools.partial(weight_kernel, count, scale),
        grid=(4,),
        in_specs=[whole, whole] + [pl.BlockSpec((rows, width), lambda t: (0, t))] * count,
        out_specs=[
            pl.BlockSpec((1, depth, width), lambda t: (jnp.minimum(t, 2), 0, 0)),
            pl.BlockSpec((depth, width), lambda t: (0, 0)),
        ],
        out_shape=[
            jax.ShapeDtypeStruct((3, depth, width), jnp.bfloat16),
            jax.ShapeDtypeStruct((depth, width), jnp.bfloat16),
        ],
        scratch_shapes=[pltpu.VMEM((depth, width), jnp.float32)],
        compiler_params=params(),
        cost_estimate=pl.CostEstimate(
            flops=8 * count * depth * rows * width,
            bytes_accessed=4 * count * depth * rows + 8 * count * rows * width,
            transcendentals=0,
        ),
    )(normed_cols, cot_cols, *gathered)


def flip(values, axis, bit):
    count = lax.axis_size(axis)
    return lax.ppermute(values, axis, [(at, at ^ bit) for at in range(count)])


def exchange_small(values, axis):
    return [values] + [flip(values, axis, bit) for bit in range(1, lax.axis_size(axis))]


def gather_xor(values, axis):
    count = lax.axis_size(axis)
    high, low = count // 2, count // 4
    over_high, over_low = flip(values, axis, high), flip(values, axis, low)
    even = lax.axis_index(axis) % 2 == 0
    onward = jnp.where(even, over_low, over_high)
    pairs = [(at, at ^ (high if at % 2 == 0 else low)) for at in range(count)]
    held = {0: values, low: over_low, high: over_high, high | low: lax.ppermute(onward, axis, pairs)}
    bit = low // 2
    while bit >= 1:
        for key in sorted(held):
            held[key | bit] = flip(held[key], axis, bit)
        bit //= 2
    return [held[key] for key in range(count)]


def line_gather(values, axis):
    count, me = lax.axis_size(axis), lax.axis_index(axis)
    zeros = (0,) * values.ndim
    held = jnp.zeros((count + 1,) + values.shape, values.dtype)
    held = lax.dynamic_update_slice(held, values[None], (me,) + zeros)
    right = left = values
    for step in range(1, count):
        right = lax.ppermute(right, axis, [(at, at + 1) for at in range(step - 1, count - 1)])
        left = lax.ppermute(left, axis, [(at, at - 1) for at in range(1, count - step + 1)])
        from_left = jnp.where(me >= step, me - step, count)
        from_right = jnp.where(me + step < count, me + step, count)
        held = lax.dynamic_update_slice(held, right[None], (from_left,) + zeros)
        held = lax.dynamic_update_slice(held, left[None], (from_right,) + zeros)
    return held


def add_bf(one, two):
    return (one.astype(jnp.float32) + two.astype(jnp.float32)).astype(jnp.bfloat16)


def line_reduce(parts, axis):
    count, me = lax.axis_size(axis), lax.axis_index(axis)

    def block(at):
        return lax.dynamic_index_in_dim(parts, jnp.clip(at, 0, count - 1), 0, keepdims=False)

    right = left = None
    for step in range(1, count):
        to_right, to_left = block(me + count - step), block(me - count + step)
        if step > 1:
            to_right, to_left = add_bf(to_right, right), add_bf(to_left, left)
        right = lax.ppermute(to_right, axis, [(at, at + 1) for at in range(step)])
        left = lax.ppermute(to_left, axis, [(at, at - 1) for at in range(count - step, count)])
    return block(me).astype(jnp.float32) + right.astype(jnp.float32) + left.astype(jnp.float32)


def columns_to_owner(whole, axis):
    count = lax.axis_size(axis)
    parts, rows, part = whole.shape
    cut = jnp.swapaxes(whole, 1, 2).reshape(count, parts * part // count, rows)
    return lax.all_to_all(cut, axis, 0, 0, tiled=True)


def shards(patches, dest_group, dest_row, segment, ln_gain, w_qkv, qk_gain, w_out, cotangent):
    group_rows, part_width = patches.shape
    groups = lax.axis_size("dp")
    parts = lax.axis_size("mp")
    slot_size = 2 * group_rows // groups
    slots = groups * slot_size
    full_width, local_width = w_out.shape
    my_group, my_index = lax.axis_index("dp"), lax.axis_index("mp")
    w_t = jnp.transpose(w_qkv, (1, 0, 2))
    w_out_t = w_out[None]

    whole_cot = lax.all_gather(cotangent, "mp", axis=0, tiled=False)

    position = jnp.arange(group_rows, dtype=jnp.int32)
    earlier = (dest_group[:, None] == dest_group[None, :]) & (position[None, :] < position[:, None])
    rank_within = jnp.sum(earlier.astype(jnp.int32), 1)
    place = dest_group * slot_size + rank_within
    to_slot = jnp.arange(slots, dtype=jnp.int32)[:, None] == place[None, :]
    outbox = dot_f32(to_slot.astype(jnp.bfloat16), patches, (1,), (0,)).astype(jnp.bfloat16)
    inbox = lax.all_to_all(
        outbox.reshape(groups, slot_size, part_width), "dp", split_axis=0, concat_axis=0, tiled=True
    ).reshape(slots, part_width)

    wide = patches.astype(jnp.float32)
    part_mean = jnp.mean(wide, -1)
    part_dev = jnp.sum(jnp.square(wide - part_mean[:, None]), -1)
    seen = exchange_small(jnp.stack([part_mean, part_dev]), "mp")
    row_mean = sum(entry[0] for entry in seen) / parts
    row_dev = sum(entry[1] + part_width * jnp.square(entry[0] - row_mean) for entry in seen)
    row_rstd = lax.rsqrt(row_dev / full_width + 1e-06)
    notes = jnp.stack([dest_row.astype(jnp.float32) + 1.0, row_mean, row_rstd])
    outnotes = jnp.sum(jnp.where(to_slot[None], notes[:, None, :], 0.0), -1)
    outnotes = outnotes.reshape(3, groups, slot_size)
    came = []
    for bit in range(groups):
        mine = lax.dynamic_index_in_dim(outnotes, my_group ^ bit, 1, keepdims=False)
        came.append(mine if bit == 0 else flip(mine, "dp", bit))
    sender = jnp.arange(groups, dtype=jnp.int32)[None, :, None]
    innotes = sum(
        jnp.where(sender == (my_group ^ bit), entry[:, None, :], 0.0)
        for bit, entry in enumerate(came)
    ).reshape(3, slots)
    arrived_at = innotes[0].astype(jnp.int32) - 1
    from_slot = position[:, None] == arrived_at[None, :]
    mean = jnp.sum(jnp.where(from_slot, innotes[1][None, :], 0.0), -1, keepdims=True)
    rstd = jnp.sum(jnp.where(from_slot, innotes[2][None, :], 0.0), -1, keepdims=True)
    packed = dot_f32(from_slot.astype(jnp.bfloat16), inbox, (1,), (0,)).astype(jnp.bfloat16)

    my_gain = lax.dynamic_slice_in_dim(ln_gain, my_index * part_width, part_width, 0)
    unit_rows = (packed.astype(jnp.float32) - mean) * rstd
    normed = line_gather((unit_rows * my_gain).astype(jnp.bfloat16), "mp")

    d_heads = project(whole_cot, w_out_t, parts, jnp.bfloat16)
    projected = project(normed, w_t, parts, jnp.float32)
    heads_out = attention(forward_kernel, projected, segment, qk_gain, (), 1)
    attn = line_reduce(expand(heads_out, w_out_t, parts, 1), "mp")
    output = (packed.astype(jnp.float32) + attn).astype(jnp.bfloat16)

    d_all = attention(backward_kernel, projected, segment, qk_gain, (d_heads,), 4)
    d_part = expand(d_all, w_t, parts, 2)
    d_normed = lax.psum_scatter(d_part, "mp", scatter_dimension=0, tiled=False)
    d_unit = d_normed.astype(jnp.float32) * my_gain
    sums = jnp.stack([jnp.sum(d_unit, -1), jnp.sum(d_unit * unit_rows, -1)])
    sums = sum(exchange_small(sums, "mp")) / full_width
    d_input = rstd * (d_unit - sums[0][:, None] - unit_rows * sums[1][:, None])
    input_grad = (cotangent.astype(jnp.float32) + d_input).astype(jnp.bfloat16)

    scale_grad = 1.0 / math.sqrt(group_rows * groups)
    cot_cols = columns_to_owner(whole_cot, "dp")
    normed_cols = columns_to_owner(normed[:parts], "dp")
    qkv_grad, out_grad = weight_grads(
        normed_cols, cot_cols, gather_xor(d_all, "dp"), scale_grad
    )
    return (output, input_grad, qkv_grad.transpose(1, 0, 2), out_grad)


def solution(mesh):
    placed = (
        P("dp", "mp"),
        P("dp"),
        P("dp"),
        P("dp"),
        P(),
        P(None, None, "mp"),
        P(),
        P(None, "mp"),
        P("dp", "mp"),
    )
    return jax.shard_map(
        shards,
        mesh=mesh,
        in_specs=placed,
        out_specs=(P("dp", "mp"), P("dp", "mp"), P("dp", None, "mp"), P("dp", "mp")),
        check_vma=False,
    )
```

profile of v0, /device:TPU:0, one launch (start us, length us, event | category | flops | bytes accessed | tf_op | source)
XLA Modules:
  0.0 351.5 jit_solution(6528152674450065203)
XLA Ops:
  10.1 5.1 %collective-permute-start.2 = (f32[2,256]{1,0:T(2,128)S(1)}, f32[2,256]{1,0:T(2,128)S(1)}, u32[]{:S(2)}, u32[]{:S(2)}) collective-permute-start(f32[2,256]{1,0:T(2,128)S(1)} %pad_maximum_fusion.1), channel_id=1, source_target_pairs={{0,3},{1,2},{2,1},{3,0},{4,7},{5,6},{6,5},{7,4},{8,11},{9,10},{10,... | collective-permute-start | bytes 6152 | tf_op jit(solution)/shard_map/ppermute | solution.py:221
  17.8 4.0 %all-to-all-start = ((bf16[8,64,1536]{2,1,0:T(8,128)(2,1)}), bf16[8,64,1536]{2,1,0:T(8,128)(2,1)S(1)}, u32[]{:S(2)}, u32[]{:S(2)}) async-start(bf16[8,64,1536]{2,1,0:T(8,128)(2,1)} %bitcast.3), calls=%async_computation | async-start | bytes 3145728 | tf_op jit(solution)/shard_map/all_to_all | solution.py:306
  29.6 12.8 %collective-permute-done.9 = f32[3,64]{1,0:T(4,128)S(1)} collective-permute-done((f32[3,64]{1,0:T(4,128)S(1)}, f32[3,64]{1,0:T(4,128)S(1)}, u32[]{:S(2)}, u32[]{:S(2)}) %collective-permute-start.9) | collective-permute-done | bytes 800 | tf_op jit(solution)/shard_map/ppermute | solution.py:221
  55.5 32.7 %collective-permute-done.10 = bf16[256,1536]{1,0:T(8,128)(2,1)S(1)} collective-permute-done((bf16[256,1536]{1,0:T(8,128)(2,1)S(1)}, bf16[256,1536]{1,0:T(8,128)(2,1)S(1)}, u32[]{:S(2)}, u32[]{:S(2)}) %collective-permute-start.10) | collective-permute-done | bytes 786464 | tf_op jit(solution)/shard_map/ppermute | solution.py:251
  88.9 15.2 %collective-permute-done.11 = bf16[256,1536]{1,0:T(8,128)(2,1)S(1)} collective-permute-done((bf16[256,1536]{1,0:T(8,128)(2,1)S(1)}, bf16[256,1536]{1,0:T(8,128)(2,1)S(1)}, u32[]{:S(2)}, u32[]{:S(2)}) %collective-permute-start.11) | collective-permute-done | bytes 786464 | tf_op jit(solution)/shard_map/ppermute | solution.py:252
  107.9 19.2 %collective-permute-done.13 = bf16[256,1536]{1,0:T(8,128)(2,1)S(1)} collective-permute-done((bf16[256,1536]{1,0:T(8,128)(2,1)S(1)}, bf16[256,1536]{1,0:T(8,128)(2,1)S(1)}, u32[]{:S(2)}, u32[]{:S(2)}) %collective-permute-start.13) | collective-permute-done | bytes 786464 | tf_op jit(solution)/shard_map/ppermute | solution.py:252
  131.4 16.0 %collective-permute-done.15 = bf16[256,1536]{1,0:T(8,128)(2,1)S(1)} collective-permute-done((bf16[256,1536]{1,0:T(8,128)(2,1)S(1)}, bf16[256,1536]{1,0:T(8,128)(2,1)S(1)}, u32[]{:S(2)}, u32[]{:S(2)}) %collective-permute-start.15) | collective-permute-done | bytes 786464 | tf_op jit(solution)/shard_map/ppermute | solution.py:252
  148.4 17.6 %shard_map.120.proj_ref = f32[256,2304]{1,0:T(8,128)S(1)} custom-call(bf16[5,256,1536]{2,1,0:T(8,128)(2,1)} %bitcast_dynamic-update-slice_fusion.x_ref, bf16[3,6144,768]{2,1,0:T(8,128)(2,1)} %bitcast.90), custom_call_target="tpu_custom_call" | custom-call | flops 7247757312 | bytes 31457280 | tf_op jit(solution)/shard_map/pallas_call | solution.py:46
  167.9 6.1 %shard_map.123.d_ref = bf16[256,768]{1,0:T(8,128)(2,1)S(1)} custom-call(bf16[4,256,1536]{2,1,0:T(8,128)(2,1)S(1)} %bitcast.86, bf16[1,6144,768]{2,1,0:T(8,128)(2,1)} %bitcast.92), custom_call_target="tpu_custom_call" | custom-call | flops 2415919104 | bytes 12582912 | tf_op jit(solution)/shard_map/pallas_call | solution.py:46
  174.0 5.3 %shard_map.124.x_ref.refs_0_ = bf16[256,3072]{1,0:T(8,128)(2,1)} custom-call(f32[256,2304]{1,0:T(8,128)S(1)} %shard_map.120.proj_ref, s32[256,1]{1,0:T(8,128)S(1)} %copy.19.row_ref, s32[1,256]{1,0:T(1,128)S(1)} %bitcast.88, f32[2,128]{1,0:T(2,128)S(1)} %copy-done.2, bf16[256,768]{1,0:T(8,128)(2,1)S(1)} %shard_map.123.d_ref), custom_call_target="tpu_custom_call" | custom-call | flops 805306368 | bytes 4718592 | tf_op jit(solution)/shard_map/pallas_call | solution.py:162
  179.3 15.9 %shard_map.125 = bf16[4,256,1536]{2,1,0:T(8,128)(2,1)} custom-call(bf16[256,3072]{1,0:T(8,128)(2,1)} %shard_map.124.x_ref.refs_0_, bf16[3,6144,768]{2,1,0:T(8,128)(2,1)} %bitcast.91), custom_call_target="tpu_custom_call" | custom-call | flops 7247757312 | bytes 31457280 | tf_op jit(solution)/shard_map/pallas_call | solution.py:78
  198.9 4.4 %slice_bitcast_fusion = bf16[4,1536,256]{1,2,0:T(8,128)(2,1)} fusion(bf16[5,256,1536]{2,1,0:T(8,128)(2,1)} %bitcast_dynamic-update-slice_fusion.x_ref), kind=kLoop, calls=%fused_computation | loop fusion | bytes 6291456 | tf_op jit(solution)/shard_map/transpose | solution.py:283
  203.4 4.7 %copy.21 = bf16[4,1536,256]{2,1,0:T(8,128)(2,1)} copy(bf16[4,1536,256]{1,2,0:T(8,128)(2,1)} %slice_bitcast_fusion) | data formatting | bytes 6291456 | tf_op jit(solution)/shard_map/transpose | solution.py:283
  208.0 4.4 %all-to-all-start.1 = ((bf16[8,768,256]{2,1,0:T(8,128)(2,1)}), bf16[8,768,256]{2,1,0:T(8,128)(2,1)}, u32[]{:S(2)}, u32[]{:S(2)}) async-start(bf16[8,768,256]{2,1,0:T(8,128)(2,1)} %bitcast.95), calls=%async_computation.2 | async-start | bytes 6291456 | tf_op jit(solution)/shard_map/all_to_all | solution.py:284
  214.2 6.0 %shard_map.122 = bf16[4,256,1536]{2,1,0:T(8,128)(2,1)S(1)} custom-call(bf16[256,768]{1,0:T(8,128)(2,1)S(1)} %shard_map.121.x_ref, bf16[1,6144,768]{2,1,0:T(8,128)(2,1)} %bitcast.93), custom_call_target="tpu_custom_call" | custom-call | flops 2415919104 | bytes 12582912 | tf_op jit(solution)/shard_map/pallas_call | solution.py:78
  224.0 9.1 %collective-permute-done.26.refs_2_ = bf16[256,3072]{1,0:T(8,128)(2,1)} collective-permute-done((bf16[256,3072]{1,0:T(8,128)(2,1)}, bf16[256,3072]{1,0:T(8,128)(2,1)}, u32[]{:S(2)}, u32[]{:S(2)}) %collective-permute-start.26) | collective-permute-done | bytes 1572896 | tf_op jit(solution)/shard_map/ppermute | solution.py:221
  239.3 17.8 %collective-permute-done.16 = bf16[256,1536]{1,0:T(8,128)(2,1)S(1)} collective-permute-done((bf16[256,1536]{1,0:T(8,128)(2,1)S(1)}, bf16[256,1536]{1,0:T(8,128)(2,1)S(1)}, u32[]{:S(2)}, u32[]{:S(2)}) %collective-permute-start.16) | collective-permute-done | bytes 786464 | tf_op jit(solution)/shard_map/ppermute | solution.py:275
  258.2 5.3 %collective-permute-start.17 = (bf16[256,1536]{1,0:T(8,128)(2,1)}, bf16[256,1536]{1,0:T(8,128)(2,1)}, u32[]{:S(2)}, u32[]{:S(2)}) collective-permute-start(bf16[256,1536]{1,0:T(8,128)(2,1)} %fusion.13), channel_id=1, source_target_pairs={{0,1},{1,2},{4,5},{5,6},{8,9},{9,10},{12,13},{13,14},{16,17},{17,1... | collective-permute-start | bytes 2359304 | tf_op jit(solution)/shard_map/ppermute | solution.py:275
  263.5 4.7 %copy.22 = bf16[4,1536,256]{2,1,0:T(8,128)(2,1)} copy(bf16[4,1536,256]{1,2,0:T(8,128)(2,1)} %bitcast.85) | data formatting | bytes 6291456 | tf_op jit(solution)/shard_map/transpose | solution.py:283
  268.4 4.5 %all-to-all-start.2 = ((bf16[8,768,256]{2,1,0:T(8,128)(2,1)}), bf16[8,768,256]{2,1,0:T(8,128)(2,1)}, u32[]{:S(2)}, u32[]{:S(2)}) async-start(bf16[8,768,256]{2,1,0:T(8,128)(2,1)} %bitcast.94), calls=%async_computation.3 | async-start | bytes 6291456 | tf_op jit(solution)/shard_map/all_to_all | solution.py:284
  272.9 11.7 %collective-permute-done.17 = bf16[256,1536]{1,0:T(8,128)(2,1)} collective-permute-done((bf16[256,1536]{1,0:T(8,128)(2,1)}, bf16[256,1536]{1,0:T(8,128)(2,1)}, u32[]{:S(2)}, u32[]{:S(2)}) %collective-permute-start.17) | collective-permute-done | bytes 786464 | tf_op jit(solution)/shard_map/ppermute | solution.py:275
  289.6 4.0 %collective-permute-done.30.refs_6_ = bf16[256,3072]{1,0:T(8,128)(2,1)} collective-permute-done((bf16[256,3072]{1,0:T(8,128)(2,1)}, bf16[256,3072]{1,0:T(8,128)(2,1)}, u32[]{:S(2)}, u32[]{:S(2)}) %collective-permute-start.30) | collective-permute-done | bytes 1572896 | tf_op jit(solution)/shard_map/ppermute | solution.py:235
  293.7 20.6 %collective-permute-start.18 = (bf16[256,1536]{1,0:T(8,128)(2,1)}, bf16[256,1536]{1,0:T(8,128)(2,1)}, u32[]{:S(2)}, u32[]{:S(2)}) collective-permute-start(bf16[256,1536]{1,0:T(8,128)(2,1)} %get-tuple-element.16), channel_id=1, source_target_pairs={{0,1},{1,2},{2,3},{4,5},{5,6},{6,7},{8,9},{9,10},{10,11},{12,13},{... | collective-permute-start | bytes 2359304 | tf_op jit(solution)/shard_map/ppermute | solution.py:275
  324.4 16.6 %shard_map.126 = (bf16[3,768,768]{2,1,0:T(8,128)(2,1)}, bf16[768,768]{1,0:T(8,128)(2,1)}) custom-call(bf16[8,768,256]{2,1,0:T(8,128)(2,1)} %all-to-all-done.1.normed_ref, bf16[8,768,256]{2,1,0:T(8,128)(2,1)} %all-to-all-done.2.cot_ref, bf16[256,3072]{1,0:T(8,128)(2,1)} %shard_map.124.x_ref.refs_0_, bf16[256,3072]{1,0:T(8,128)(2,1)} %collective-permute-done.25.refs_1_, ...), custom_call_target="tpu_custom_call" | custom-call | flops 9663676416 | bytes 18874368 | tf_op jit(solution)/shard_map/pallas_call | solution.py:197
  (133 shorter events, 73.1 us)
Async XLA Ops:
  17.8 28.7 %all-to-all-start = ((bf16[8,64,1536]{2,1,0:T(8,128)(2,1)}), bf16[8,64,1536]{2,1,0:T(8,128)(2,1)S(1)}, u32[]{:S(2)}, u32[]{:S(2)}) async-start(bf16[8,64,1536]{2,1,0:T(8,128)(2,1)} %bitcast.3), calls=%async_computation | async-start | bytes 3145728 | tf_op jit(solution)/shard_map/all_to_all | solution.py:306
  21.8 144.2 %all-gather.3.cloned.1.call-start = ((), (), s32[]{:S(2)}) async-start(), calls=%async_computation.5 | async-start | bytes 3932160 | tf_op jit(solution)/shard_map/all_gather | solution.py:298
  22.5 294.0 %reduce-scatter.2.cloned.1.call-start = ((), (), s32[]{:S(2)}) async-start(), calls=%async_computation.4 | async-start | bytes 3932160 | tf_op jit(solution)/shard_map/reduce_scatter | solution.py:347
  50.7 37.4 %collective-permute-start.10 = (bf16[256,1536]{1,0:T(8,128)(2,1)S(1)}, bf16[256,1536]{1,0:T(8,128)(2,1)S(1)}, u32[]{:S(2)}, u32[]{:S(2)}) collective-permute-start(bf16[256,1536]{1,0:T(8,128)(2,1)S(1)} %get-tuple-element.13), channel_id=1, source_target_pairs={{0,1},{1,2},{2,3},{4,5},{5,6},{6,7},{8,9},{9,10},{10,11},{12,13},{... | collective-permute-start | bytes 2359304 | tf_op jit(solution)/shard_map/ppermute | solution.py:251
  53.9 50.1 %collective-permute-start.11 = (bf16[256,1536]{1,0:T(8,128)(2,1)S(1)}, bf16[256,1536]{1,0:T(8,128)(2,1)S(1)}, u32[]{:S(2)}, u32[]{:S(2)}) collective-permute-start(bf16[256,1536]{1,0:T(8,128)(2,1)S(1)} %get-tuple-element.13), channel_id=1, source_target_pairs={{1,0},{2,1},{3,2},{5,4},{6,5},{7,6},{9,8},{10,9},{11,10},{13,12},{... | collective-permute-start | bytes 2359304 | tf_op jit(solution)/shard_map/ppermute | solution.py:252
  104.0 23.1 %collective-permute-start.13 = (bf16[256,1536]{1,0:T(8,128)(2,1)S(1)}, bf16[256,1536]{1,0:T(8,128)(2,1)S(1)}, u32[]{:S(2)}, u32[]{:S(2)}) collective-permute-start(bf16[256,1536]{1,0:T(8,128)(2,1)S(1)} %collective-permute-done.11), channel_id=1, source_target_pairs={{1,0},{2,1},{5,4},{6,5},{9,8},{10,9},{13,12},{14,13},{17,16},{18,1... | collective-permute-start | bytes 2359304 | tf_op jit(solution)/shard_map/ppermute | solution.py:252
  107.2 23.3 %collective-permute-start.14 = (bf16[256,1536]{1,0:T(8,128)(2,1)S(1)}, bf16[256,1536]{1,0:T(8,128)(2,1)S(1)}, u32[]{:S(2)}, u32[]{:S(2)}) collective-permute-start(bf16[256,1536]{1,0:T(8,128)(2,1)S(1)} %collective-permute-done.12), channel_id=1, source_target_pairs={{2,3},{6,7},{10,11},{14,15},{18,19},{22,23},{26,27},{30,31}} | collective-permute-start | bytes 2359304 | tf_op jit(solution)/shard_map/ppermute | solution.py:251
  127.1 20.3 %collective-permute-start.15 = (bf16[256,1536]{1,0:T(8,128)(2,1)S(1)}, bf16[256,1536]{1,0:T(8,128)(2,1)S(1)}, u32[]{:S(2)}, u32[]{:S(2)}) collective-permute-start(bf16[256,1536]{1,0:T(8,128)(2,1)S(1)} %collective-permute-done.13), channel_id=1, source_target_pairs={{1,0},{5,4},{9,8},{13,12},{17,16},{21,20},{25,24},{29,28}} | collective-permute-start | bytes 2359304 | tf_op jit(solution)/shard_map/ppermute | solution.py:252
  195.2 37.9 %collective-permute-start.26 = (bf16[256,3072]{1,0:T(8,128)(2,1)}, bf16[256,3072]{1,0:T(8,128)(2,1)}, u32[]{:S(2)}, u32[]{:S(2)}) collective-permute-start(bf16[256,3072]{1,0:T(8,128)(2,1)} %shard_map.124.x_ref.refs_0_), channel_id=1, source_target_pairs={{0,8},{4,12},{8,0},{12,4},{16,24},{20,28},{24,16},{28,20},{1,9},{5... | collective-permute-start | bytes 4718600 | tf_op jit(solution)/shard_map/ppermute | solution.py:221
  197.5 37.6 %collective-permute-start.28 = (bf16[256,3072]{1,0:T(8,128)(2,1)}, bf16[256,3072]{1,0:T(8,128)(2,1)}, u32[]{:S(2)}, u32[]{:S(2)}) collective-permute-start(bf16[256,3072]{1,0:T(8,128)(2,1)} %shard_map.124.x_ref.refs_0_), channel_id=1, source_target_pairs={{0,16},{4,20},{8,24},{12,28},{16,0},{20,4},{24,8},{28,12},{1,17},{... | collective-permute-start | bytes 4718600 | tf_op jit(solution)/shard_map/ppermute | solution.py:221
  208.0 60.4 %all-to-all-start.1 = ((bf16[8,768,256]{2,1,0:T(8,128)(2,1)}), bf16[8,768,256]{2,1,0:T(8,128)(2,1)}, u32[]{:S(2)}, u32[]{:S(2)}) async-start(bf16[8,768,256]{2,1,0:T(8,128)(2,1)} %bitcast.95), calls=%async_computation.2 | async-start | bytes 6291456 | tf_op jit(solution)/shard_map/all_to_all | solution.py:284
  221.1 36.0 %collective-permute-start.16 = (bf16[256,1536]{1,0:T(8,128)(2,1)S(1)}, bf16[256,1536]{1,0:T(8,128)(2,1)S(1)}, u32[]{:S(2)}, u32[]{:S(2)}) collective-permute-start(bf16[256,1536]{1,0:T(8,128)(2,1)S(1)} %get-tuple-element.18), channel_id=1, source_target_pairs={{0,1},{4,5},{8,9},{12,13},{16,17},{20,21},{24,25},{28,29}} | collective-permute-start | bytes 2359304 | tf_op jit(solution)/shard_map/ppermute | solution.py:275
  222.5 50.4 %collective-permute-start.19 = (bf16[256,1536]{1,0:T(8,128)(2,1)}, bf16[256,1536]{1,0:T(8,128)(2,1)}, u32[]{:S(2)}, u32[]{:S(2)}) collective-permute-start(bf16[256,1536]{1,0:T(8,128)(2,1)} %get-tuple-element.19), channel_id=1, source_target_pairs={{3,2},{7,6},{11,10},{15,14},{19,18},{23,22},{27,26},{31,30}} | collective-permute-start | bytes 2359304 | tf_op jit(solution)/shard_map/ppermute | solution.py:276
  237.9 55.8 %collective-permute-start.30 = (bf16[256,3072]{1,0:T(8,128)(2,1)}, bf16[256,3072]{1,0:T(8,128)(2,1)}, u32[]{:S(2)}, u32[]{:S(2)}) collective-permute-start(bf16[256,3072]{1,0:T(8,128)(2,1)} %broadcast_select_fusion), channel_id=1, source_target_pairs={{0,16},{4,12},{8,24},{12,4},{16,0},{20,28},{24,8},{28,20},{1,17},{... | collective-permute-start | bytes 4718600 | tf_op jit(solution)/shard_map/ppermute | solution.py:235
  258.2 26.4 %collective-permute-start.17 = (bf16[256,1536]{1,0:T(8,128)(2,1)}, bf16[256,1536]{1,0:T(8,128)(2,1)}, u32[]{:S(2)}, u32[]{:S(2)}) collective-permute-start(bf16[256,1536]{1,0:T(8,128)(2,1)} %fusion.13), channel_id=1, source_target_pairs={{0,1},{1,2},{4,5},{5,6},{8,9},{9,10},{12,13},{13,14},{16,17},{17,1... | collective-permute-start | bytes 2359304 | tf_op jit(solution)/shard_map/ppermute | solution.py:275
  268.4 56.0 %all-to-all-start.2 = ((bf16[8,768,256]{2,1,0:T(8,128)(2,1)}), bf16[8,768,256]{2,1,0:T(8,128)(2,1)}, u32[]{:S(2)}, u32[]{:S(2)}) async-start(bf16[8,768,256]{2,1,0:T(8,128)(2,1)} %bitcast.94), calls=%async_computation.3 | async-start | bytes 6291456 | tf_op jit(solution)/shard_map/all_to_all | solution.py:284
  289.1 29.5 %collective-permute-start.25 = (bf16[256,3072]{1,0:T(8,128)(2,1)}, bf16[256,3072]{1,0:T(8,128)(2,1)}, u32[]{:S(2)}, u32[]{:S(2)}) collective-permute-start(bf16[256,3072]{1,0:T(8,128)(2,1)} %shard_map.124.x_ref.refs_0_), channel_id=1, source_target_pairs={{0,4},{4,0},{8,12},{12,8},{16,20},{20,16},{24,28},{28,24},{1,5},{5... | collective-permute-start | bytes 4718600 | tf_op jit(solution)/shard_map/ppermute | solution.py:221
  289.1 30.8 %collective-permute-start.27 = (bf16[256,3072]{1,0:T(8,128)(2,1)}, bf16[256,3072]{1,0:T(8,128)(2,1)}, u32[]{:S(2)}, u32[]{:S(2)}) collective-permute-start(bf16[256,3072]{1,0:T(8,128)(2,1)} %collective-permute-done.26.refs_2_), channel_id=1, source_target_pairs={{0,4},{4,0},{8,12},{12,8},{16,20},{20,16},{24,28},{28,24},{1,5},{5... | collective-permute-start | bytes 4718600 | tf_op jit(solution)/shard_map/ppermute | solution.py:221
  289.6 31.7 %collective-permute-start.29 = (bf16[256,3072]{1,0:T(8,128)(2,1)}, bf16[256,3072]{1,0:T(8,128)(2,1)}, u32[]{:S(2)}, u32[]{:S(2)}) collective-permute-start(bf16[256,3072]{1,0:T(8,128)(2,1)} %collective-permute-done.28.refs_4_), channel_id=1, source_target_pairs={{0,4},{4,0},{8,12},{12,8},{16,20},{20,16},{24,28},{28,24},{1,5},{5... | collective-permute-start | bytes 4718600 | tf_op jit(solution)/shard_map/ppermute | solution.py:221
  293.7 30.4 %collective-permute-start.31 = (bf16[256,3072]{1,0:T(8,128)(2,1)}, bf16[256,3072]{1,0:T(8,128)(2,1)}, u32[]{:S(2)}, u32[]{:S(2)}) collective-permute-start(bf16[256,3072]{1,0:T(8,128)(2,1)} %collective-permute-done.30.refs_6_), channel_id=1, source_target_pairs={{0,4},{4,0},{8,12},{12,8},{16,20},{20,16},{24,28},{28,24},{1,5},{5... | collective-permute-start | bytes 4718600 | tf_op jit(solution)/shard_map/ppermute | solution.py:221
  293.7 47.4 %collective-permute-start.18 = (bf16[256,1536]{1,0:T(8,128)(2,1)}, bf16[256,1536]{1,0:T(8,128)(2,1)}, u32[]{:S(2)}, u32[]{:S(2)}) collective-permute-start(bf16[256,1536]{1,0:T(8,128)(2,1)} %get-tuple-element.16), channel_id=1, source_target_pairs={{0,1},{1,2},{2,3},{4,5},{5,6},{6,7},{8,9},{9,10},{10,11},{12,13},{... | collective-permute-start | bytes 2359304 | tf_op jit(solution)/shard_map/ppermute | solution.py:275
  318.6 22.4 %collective-permute-start.21 = (bf16[256,1536]{1,0:T(8,128)(2,1)}, bf16[256,1536]{1,0:T(8,128)(2,1)}, u32[]{:S(2)}, u32[]{:S(2)}) collective-permute-start(bf16[256,1536]{1,0:T(8,128)(2,1)} %fusion.12), channel_id=1, source_target_pairs={{1,0},{2,1},{3,2},{5,4},{6,5},{7,6},{9,8},{10,9},{11,10},{13,12},{... | collective-permute-start | bytes 2359304 | tf_op jit(solution)/shard_map/ppermute | solution.py:276
  319.9 21.1 %collective-permute-start.24 = (f32[2,256]{1,0:T(2,128)S(1)}, f32[2,256]{1,0:T(2,128)S(1)}, u32[]{:S(2)}, u32[]{:S(2)}) collective-permute-start(f32[2,256]{1,0:T(2,128)S(1)} %pad_maximum_fusion.2), channel_id=1, source_target_pairs={{0,3},{1,2},{2,1},{3,0},{4,7},{5,6},{6,5},{7,4},{8,11},{9,10},{10,... | collective-permute-start | bytes 6152 | tf_op jit(solution)/shard_map/ppermute | solution.py:221
  321.3 19.7 %collective-permute-start.23 = (f32[2,256]{1,0:T(2,128)S(1)}, f32[2,256]{1,0:T(2,128)S(1)}, u32[]{:S(2)}, u32[]{:S(2)}) collective-permute-start(f32[2,256]{1,0:T(2,128)S(1)} %pad_maximum_fusion.2), channel_id=1, source_target_pairs={{0,2},{1,3},{2,0},{3,1},{4,6},{5,7},{6,4},{7,5},{8,10},{9,11},{10,... | collective-permute-start | bytes 6152 | tf_op jit(solution)/shard_map/ppermute | solution.py:221
  (22 other events, 249.9 us)
Sparse Core Ops, SparseCore 0:
  24.2 78.0 all-gather.2
  195.3 77.9 reduce-scatter.1
where the time goes:
time: 353 us; the launch traced here: 351 us
  waiting for transfers between devices  143 us (41%)
  starting transfers between devices  76.5 us (22%)
  Pallas kernels  69.1 us (20%)
  local copies, waits for them, and re-layouts  25.8 us (7%)
  other arithmetic  18.4 us (5%)
  between operations  14.7 us (4%)
  matrix products  3.75 us (1%)
    ppermute x3, waiting for transfers between devices, line_gather(): lax.ppermute(left, axis, [(at, at - 1) for at in range(1, count - step +...  50.4 us
    ppermute x3, waiting for transfers between devices, line_gather(): lax.ppermute(right, axis, [(at, at + 1) for at in range(step - 1, count -...  32.7 us
    ppermute x3, waiting for transfers between devices, line_reduce(): right = lax.ppermute(to_right, axis, [(at, at + 1) for at in range(step)])  29.6 us
    ppermute x3, starting transfers between devices, line_reduce(): right = lax.ppermute(to_right, axis, [(at, at + 1) for at in range(step)])  27.2 us
    ppermute x19, waiting for transfers between devices, flip(): return lax.ppermute(values, axis, [(at, at ^ bit) for at in range(count)])  25.6 us
    pallas_call x2, Pallas kernels, project(): pl.pallas_call(functools.partial(project_kernel, steps, width), grid=(ste...  23.7 us
    pallas_call x2, Pallas kernels, expand(): pl.pallas_call(functools.partial(expand_kernel, kinds, width), grid=(part...  21.9 us
    ppermute x19, starting transfers between devices, flip(): return lax.ppermute(values, axis, [(at, at ^ bit) for at in range(count)])  21.8 us
  transfers between devices with their start and end apart: 37, of which 12 were waited for; matrix products, arithmetic and copies ran while one was open for 11% of the time, Pallas kernels for 12%

commit v1 on v0

--- a/solution.py
+++ b/solution.py
@@ -60,6 +60,40 @@
             transcendentals=0,
         ),
     )(x, w)
+
+
+def add_block_kernel(first, width, at_ref, x_ref, w_ref, *refs):
+    out_ref = refs[-1]
+    term = jnp.dot(x_ref[...], w_ref[0], preferred_element_type=jnp.float32)
+    out_ref[...] = term if first else refs[0][...] + term
+
+
+def add_block(total, x, w, at):
+    rows, part = x.shape
+    kinds, _, width = w.shape
+    sums = pl.BlockSpec((rows, width), lambda t, at_ref: (0, t))
+    before = [] if total is None else [total]
+    return pl.pallas_call(
+        functools.partial(add_block_kernel, total is None, width),
+        grid_spec=pltpu.PrefetchScalarGridSpec(
+            num_scalar_prefetch=1,
+            grid=(kinds,),
+            in_specs=[
+                pl.BlockSpec((rows, part), lambda t, at_ref: (0, 0)),
+                pl.BlockSpec((1, part, width), lambda t, at_ref: (t, at_ref[0], 0)),
+            ]
+            + [sums] * len(before),
+            out_specs=sums,
+        ),
+        out_shape=jax.ShapeDtypeStruct((rows, kinds * width), jnp.float32),
+        input_output_aliases={} if total is None else {3: 0},
+        compiler_params=params(),
+        cost_estimate=pl.CostEstimate(
+            flops=2 * rows * part * kinds * width,
+            bytes_accessed=2 * kinds * part * width + 8 * rows * kinds * width,
+            transcendentals=0,
+        ),
+    )(at.reshape(1).astype(jnp.int32), x, w, *before)
 
 
 def expand_kernel(kinds, width, x_ref, w_ref, out_ref):
@@ -129,7 +163,7 @@
     )
 
 
-def backward_kernel(heads, proj_ref, row_ref, col_ref, gain_ref, d_ref, out_ref):
+def backward_kernel(heads, proj_ref, row_ref, col_ref, gain_ref, d_one_ref, d_two_ref, out_ref):
     same = row_ref[...] == col_ref[...]
     width = heads * DH
     for head in range(heads):
@@ -138,7 +172,7 @@
         )
         at = head * DH
         weights_bf = weights.astype(jnp.bfloat16)
-        d_out = d_ref[:, at : at + DH]
+        d_out = jnp.concatenate([d_one_ref[:, at : at + DH], d_two_ref[:, at : at + DH]], 0)
         mixed = dot_f32(weights_bf, values, (1,), (0,))
         out_ref[:, 3 * width + at : 3 * width + at + DH] = mixed.astype(jnp.bfloat16)
         d_values = dot_f32(weights_bf, d_out, (0,), (0,))
@@ -171,49 +205,76 @@
     )(projected, segment.reshape(rows, 1), segment.reshape(1, rows), qk_gain, *extra)
 
 
-def weight_kernel(count, scale, normed_ref, cot_ref, *refs):
-    b_refs, (qkv_ref, out_ref, total) = refs[:count], refs[count:]
+def weight_kernel(keys, scale, normed_ref, one_ref, two_ref, *refs):
+    b_refs, refs = refs[: len(keys)], refs[len(keys) :]
     me, t = lax.axis_index("dp"), pl.program_id(0)
 
-    def product(a_ref):
-        for k in range(count):
-            term = jnp.dot(a_ref[me ^ k], b_refs[k][...], preferred_element_type=jnp.float32)
-            total[...] = term if k == 0 else total[...] + term
-        return (total[...] * scale).astype(jnp.bfloat16)
+    def product(load, total):
+        for order, key in enumerate(keys):
+            term = jnp.dot(load(me ^ key), b_refs[order][...], preferred_element_type=jnp.float32)
+            if scale is None and order == 0:
+                total[...] = term
+            else:
+                total[...] += term
+
+    def normed(at):
+        return normed_ref[at]
+
+    def cot(at):
+        return jnp.concatenate([one_ref[at], two_ref[at]], 1)
+
+    if scale is None:
+        total = refs[0].at[0]
+    else:
+        before_ref, qkv_ref, out_ref, total = refs
+        total[...] = before_ref[0]
 
     @pl.when(t < 3)
     def _():
-        qkv_ref[0] = product(normed_ref)
+        product(normed, total)
+        if scale is not None:
+            qkv_ref[0] = (total[...] * scale).astype(jnp.bfloat16)
 
     @pl.when(t == 3)
     def _():
-        out_ref[...] = product(cot_ref)
-
-
-def weight_grads(normed_cols, cot_cols, gathered, scale):
+        product(cot, total)
+        if scale is not None:
+            out_ref[...] = (total[...] * scale).astype(jnp.bfloat16)
+
+
+def weight_grads(normed_cols, cot_one, cot_two, gathered, keys, before, scale):
     count, depth, rows = normed_cols.shape
     width = gathered[0].shape[1] // 4
     whole = pl.BlockSpec((count, depth, rows), lambda t: (0, 0, 0))
+    half = pl.BlockSpec((count, depth, rows // 2), lambda t: (0, 0, 0))
+    sums = pl.BlockSpec((1, depth, width), lambda t: (t, 0, 0))
+    sums_shape = jax.ShapeDtypeStruct((4, depth, width), jnp.float32)
     return pl.pallas_call(
-        functools.partial(weight_kernel, count, scale),
+        functools.partial(weight_kernel, keys, scale),
         grid=(4,),
-        in_specs=[whole, whole] + [pl.BlockSpec((rows, width), lambda t: (0, t))] * count,
-        out_specs=[
+        in_specs=[whole, half, half]
+        + [pl.BlockSpec((rows, width), lambda t: (0, t))] * len(keys)
+        + ([] if before is None else [sums]),
+        out_specs=sums
+        if before is None
+        else [
             pl.BlockSpec((1, depth, width), lambda t: (jnp.minimum(t, 2), 0, 0)),
             pl.BlockSpec((depth, width), lambda t: (0, 0)),
         ],
-        out_shape=[
+        out_shape=sums_shape
+        if before is None
+        else [
             jax.ShapeDtypeStruct((3, depth, width), jnp.bfloat16),
             jax.ShapeDtypeStruct((depth, width), jnp.bfloat16),
         ],
-        scratch_shapes=[pltpu.VMEM((depth, width), jnp.float32)],
+        scratch_shapes=[] if before is None else [pltpu.VMEM((depth, width), jnp.float32)],
         compiler_params=params(),
         cost_estimate=pl.CostEstimate(
-            flops=8 * count * depth * rows * width,
-            bytes_accessed=4 * count * depth * rows + 8 * count * rows * width,
+            flops=8 * len(keys) * depth * rows * width,
+            bytes_accessed=4 * count * depth * rows + 8 * len(keys) * rows * width,
             transcendentals=0,
         ),
-    )(normed_cols, cot_cols, *gathered)
+    )(normed_cols, cot_one, cot_two, *gathered, *([] if before is None else [before]))
 
 
 def flip(values, axis, bit):
@@ -228,33 +289,48 @@
 def gather_xor(values, axis):
     count = lax.axis_size(axis)
     high, low = count // 2, count // 4
+
+    def spread(held):
+        bit = low // 2
+        while bit >= 1:
+            for key in sorted(held):
+                held[key | bit] = flip(held[key], axis, bit)
+            bit //= 2
+        return held
+
     over_high, over_low = flip(values, axis, high), flip(values, axis, low)
+    own = spread({0: values})
+    keys = sorted(own)
+    spread_own, over_high, over_low = lax.optimization_barrier(
+        ([own[key] for key in keys], over_high, over_low)
+    )
     even = lax.axis_index(axis) % 2 == 0
     onward = jnp.where(even, over_low, over_high)
     pairs = [(at, at ^ (high if at % 2 == 0 else low)) for at in range(count)]
-    held = {0: values, low: over_low, high: over_high, high | low: lax.ppermute(onward, axis, pairs)}
-    bit = low // 2
-    while bit >= 1:
-        for key in sorted(held):
-            held[key | bit] = flip(held[key], axis, bit)
-        bit //= 2
-    return [held[key] for key in range(count)]
-
-
-def line_gather(values, axis):
+    far = lax.ppermute(onward, axis, pairs)
+    near = dict(zip(keys, spread_own))
+    near.update(spread({high: over_high}))
+    near.update(spread({low: over_low}))
+    return near, spread({high | low: far})
+
+
+def line_blocks(values, axis, between):
     count, me = lax.axis_size(axis), lax.axis_index(axis)
-    zeros = (0,) * values.ndim
-    held = jnp.zeros((count + 1,) + values.shape, values.dtype)
-    held = lax.dynamic_update_slice(held, values[None], (me,) + zeros)
+    blocks = [(me, None, values)]
     right = left = values
     for step in range(1, count):
         right = lax.ppermute(right, axis, [(at, at + 1) for at in range(step - 1, count - 1)])
         left = lax.ppermute(left, axis, [(at, at - 1) for at in range(1, count - step + 1)])
-        from_left = jnp.where(me >= step, me - step, count)
-        from_right = jnp.where(me + step < count, me + step, count)
-        held = lax.dynamic_update_slice(held, right[None], (from_left,) + zeros)
-        held = lax.dynamic_update_slice(held, left[None], (from_right,) + zeros)
-    return held
+        if step == count // 2:
+            right, left = between(right, left)
+        over, under = me >= step, me + step < count
+        if 2 * step >= count:
+            at = jnp.where(over, me - step, jnp.minimum(me + step, count - 1))
+            blocks.append((at, over | under, right + left))
+        else:
+            blocks.append((jnp.maximum(me - step, 0), over, right))
+            blocks.append((jnp.minimum(me + step, count - 1), under, left))
+    return blocks
 
 
 def add_bf(one, two):
@@ -267,20 +343,28 @@
     def block(at):
         return lax.dynamic_index_in_dim(parts, jnp.clip(at, 0, count - 1), 0, keepdims=False)
 
-    right = left = None
-    for step in range(1, count):
-        to_right, to_left = block(me + count - step), block(me - count + step)
-        if step > 1:
-            to_right, to_left = add_bf(to_right, right), add_bf(to_left, left)
-        right = lax.ppermute(to_right, axis, [(at, at + 1) for at in range(step)])
-        left = lax.ppermute(to_left, axis, [(at, at - 1) for at in range(count - step, count)])
-    return block(me).astype(jnp.float32) + right.astype(jnp.float32) + left.astype(jnp.float32)
-
-
-def columns_to_owner(whole, axis):
+    def send(step, to_right, to_left):
+        return (
+            lax.ppermute(to_right, axis, [(at, at + 1) for at in range(step)]),
+            lax.ppermute(to_left, axis, [(at, at - 1) for at in range(count - step, count)]),
+        )
+
+    def go_on(right, left):
+        for step in range(2, count):
+            right, left = send(
+                step,
+                add_bf(block(me + count - step), right),
+                add_bf(block(me - count + step), left),
+            )
+        return block(me).astype(jnp.float32) + right.astype(jnp.float32) + left.astype(jnp.float32)
+
+    return send(1, block(me + count - 1), block(me - count + 1)), go_on
+
+
+def columns_to_owner(turned, axis):
     count = lax.axis_size(axis)
-    parts, rows, part = whole.shape
-    cut = jnp.swapaxes(whole, 1, 2).reshape(count, parts * part // count, rows)
+    parts, part, rows = turned.shape
+    cut = turned.reshape(count, parts * part // count, rows)
     return lax.all_to_all(cut, axis, 0, 0, tiled=True)
 
 
@@ -295,7 +379,9 @@
     w_t = jnp.transpose(w_qkv, (1, 0, 2))
     w_out_t = w_out[None]
 
-    whole_cot = lax.all_gather(cotangent, "mp", axis=0, tiled=False)
+    half = group_rows // 2
+    first_rows, dest_group = lax.optimization_barrier((cotangent[:half], dest_group))
+    cot_one = lax.all_gather(first_rows, "mp", axis=0, tiled=False)
 
     position = jnp.arange(group_rows, dtype=jnp.int32)
     earlier = (dest_group[:, None] == dest_group[None, :]) & (position[None, :] < position[:, None])
@@ -307,7 +393,8 @@
         outbox.reshape(groups, slot_size, part_width), "dp", split_axis=0, concat_axis=0, tiled=True
     ).reshape(slots, part_width)
 
-    wide = patches.astype(jnp.float32)
+    outbox, late_patches = lax.optimization_barrier((outbox, patches))
+    wide = late_patches.astype(jnp.float32)
     part_mean = jnp.mean(wide, -1)
     part_dev = jnp.sum(jnp.square(wide - part_mean[:, None]), -1)
     seen = exchange_small(jnp.stack([part_mean, part_dev]), "mp")
@@ -334,15 +421,44 @@
 
     my_gain = lax.dynamic_slice_in_dim(ln_gain, my_index * part_width, part_width, 0)
     unit_rows = (packed.astype(jnp.float32) - mean) * rstd
-    normed = line_gather((unit_rows * my_gain).astype(jnp.bfloat16), "mp")
-
-    d_heads = project(whole_cot, w_out_t, parts, jnp.bfloat16)
-    projected = project(normed, w_t, parts, jnp.float32)
+    normed_part = (unit_rows * my_gain).astype(jnp.bfloat16)
+    normed_part, cot_one = lax.optimization_barrier((normed_part, cot_one))
+
+    late = [None]
+
+    def between(right, left):
+        right, left, late[0] = lax.optimization_barrier((right, left, cotangent[half:]))
+        return right, left
+
+    blocks = line_blocks(normed_part, "mp", between)
+    cot_two = lax.all_gather(late[0], "mp", axis=0, tiled=False)
+    cot_cols_one = columns_to_owner(jnp.swapaxes(cot_one, 1, 2), "dp")
+    d_heads_one = project(cot_one, w_out_t, parts, jnp.bfloat16)
+    projected = None
+    turned = jnp.zeros((parts, part_width, group_rows), jnp.bfloat16)
+    for order, (at, there, block) in enumerate(blocks):
+        if order == len(blocks) - 1:
+            block, cot_cols_one, d_heads_one, projected = lax.optimization_barrier(
+                (block, cot_cols_one, d_heads_one, projected)
+            )
+        projected = add_block(projected, block, w_t, at)
+        block_t = block.T
+        if there is not None:
+            held = lax.dynamic_index_in_dim(turned, at, 0, keepdims=False)
+            block_t = jnp.where(there, block_t, held)
+        turned = lax.dynamic_update_index_in_dim(turned, block_t, at, 0)
+    normed_cols = columns_to_owner(turned, "dp")
+
     heads_out = attention(forward_kernel, projected, segment, qk_gain, (), 1)
-    attn = line_reduce(expand(heads_out, w_out_t, parts, 1), "mp")
+    first_step, go_on = line_reduce(expand(heads_out, w_out_t, parts, 1), "mp")
+    d_heads_two = project(cot_two, w_out_t, parts, jnp.bfloat16)
+    first_step, normed_cols, d_heads_one, d_heads_two = lax.optimization_barrier(
+        (first_step, normed_cols, d_heads_one, d_heads_two)
+    )
+    attn = go_on(*first_step)
     output = (packed.astype(jnp.float32) + attn).astype(jnp.bfloat16)
 
-    d_all = attention(backward_kernel, projected, segment, qk_gain, (d_heads,), 4)
+    d_all = attention(backward_kernel, projected, segment, qk_gain, (d_heads_one, d_heads_two), 4)
     d_part = expand(d_all, w_t, parts, 2)
     d_normed = lax.psum_scatter(d_part, "mp", scatter_dimension=0, tiled=False)
     d_unit = d_normed.astype(jnp.float32) * my_gain
@@ -352,11 +468,14 @@
     input_grad = (cotangent.astype(jnp.float32) + d_input).astype(jnp.bfloat16)
 
     scale_grad = 1.0 / math.sqrt(group_rows * groups)
-    cot_cols = columns_to_owner(whole_cot, "dp")
-    normed_cols = columns_to_owner(normed[:parts], "dp")
-    qkv_grad, out_grad = weight_grads(
-        normed_cols, cot_cols, gather_xor(d_all, "dp"), scale_grad
-    )
+    cot_cols_two = columns_to_owner(jnp.swapaxes(cot_two, 1, 2), "dp")
+    columns = (normed_cols, cot_cols_one, cot_cols_two)
+    sums_near = None
+    near, far = gather_xor(d_all, "dp")
+    for held, scale in ((near, None), (far, scale_grad)):
+        keys = sorted(held)
+        sums_near = weight_grads(*columns, [held[key] for key in keys], keys, sums_near, scale)
+    qkv_grad, out_grad = sums_near
     return (output, input_grad, qkv_grad.transpose(1, 0, 2), out_grad)
 
 

time: 353 us -> 381 us (1.079)
  waiting for transfers between devices: 143 us -> 117 us
  local copies, waits for them, and re-layouts: 25.8 us -> 47.6 us
  Pallas kernels: 69.1 us -> 86.7 us
  other arithmetic: 18.4 us -> 27.1 us
  starting transfers between devices: 76.5 us -> 81.8 us
    ppermute x13, waiting for transfers between devices: 117 us -> 28.8 us  [the longest x1 16.9 us: gather_xor(): far = lax.ppermute(onward, axis, pairs)]
    all_gather x1 -> x2, waiting for transfers between devices: 0.02 us -> 46.5 us  [the longest x1 31.1 us: shards(): cot_two = lax.all_gather(late[0], 'mp', axis=0, tiled=False)]
    pallas_call x1 -> x7, Pallas kernels: 16.6 us -> 49.9 us  [the longest x5 25.6 us: add_block(): pl.pallas_call(functools.partial(add_block_kernel, total is None, width),...]
    ppermute x19, waiting for transfers between devices: 25.6 us -> 40.8 us  [flip(): return lax.ppermute(values, axis, [(at, at ^ bit) for at in range(count)])]
    pallas_call x2, Pallas kernels: 23.7 us -> 10.6 us  [project(): pl.pallas_call(functools.partial(project_kernel, steps, width), grid=(ste...]
    dynamic_slice x0 -> x8, local copies, waits for them, and re-layouts: none -> 12.2 us  [shards(): held = lax.dynamic_index_in_dim(turned, at, 0, keepdims=False)]
    ppermute x19, starting transfers between devices: 21.8 us -> 32.6 us  [flip(): return lax.ppermute(values, axis, [(at, at ^ bit) for at in range(count)])]
    ppermute x13, starting transfers between devices: 41.8 us -> 31.7 us  [the longest x3 16.5 us: send(): lax.ppermute(to_right, axis, [(at, at + 1) for at in range(step)])]
  transfers between devices with their start and end apart: 37 -> 39, of which waited for: 12 -> 9; matrix products, arithmetic and copies ran while one was open for 11% -> 15% of each run, Pallas kernels for 12% -> 18%
where the time goes in v1:
time: 381 us; the launch traced here: 379 us
  waiting for transfers between devices  117 us (31%)
  Pallas kernels  86.7 us (23%)
  starting transfers between devices  81.8 us (21%)
  local copies, waits for them, and re-layouts  47.6 us (12%)
  other arithmetic  27.1 us (7%)
  between operations  14.5 us (4%)
    ppermute x19, waiting for transfers between devices, flip(): return lax.ppermute(values, axis, [(at, at ^ bit) for at in range(count)])  40.8 us
    ppermute x19, starting transfers between devices, flip(): return lax.ppermute(values, axis, [(at, at ^ bit) for at in range(count)])  32.6 us
    all_gather x1, waiting for transfers between devices, shards(): cot_two = lax.all_gather(late[0], 'mp', axis=0, tiled=False)  31.1 us
    pallas_call x5, Pallas kernels, add_block(): pl.pallas_call(functools.partial(add_block_kernel, total is None, width),...  25.6 us
    pallas_call x2, Pallas kernels, weight_grads(): pl.pallas_call(functools.partial(weight_kernel, keys, scale), grid=(4,),...  24.3 us
    pallas_call x2, Pallas kernels, expand(): pl.pallas_call(functools.partial(expand_kernel, kinds, width), grid=(part...  20.5 us
    ppermute x1, waiting for transfers between devices, gather_xor(): far = lax.ppermute(onward, axis, pairs)  16.9 us
    ppermute x3, starting transfers between devices, send(): lax.ppermute(to_right, axis, [(at, at + 1) for at in range(step)])  16.5 us
  transfers between devices with their start and end apart: 39, of which 9 were waited for; matrix products, arithmetic and copies ran while one was open for 15% of the time, Pallas kernels for 18%

profile of v1, /device:TPU:0, one launch (start us, length us, event | category | flops | bytes accessed | tf_op | source)
XLA Modules:
  0.0 378.5 jit_solution(14291380454901709842)
XLA Ops:
  11.8 5.1 %collective-permute-start.2 = (f32[2,256]{1,0:T(2,128)S(1)}, f32[2,256]{1,0:T(2,128)S(1)}, u32[]{:S(2)}, u32[]{:S(2)}) collective-permute-start(f32[2,256]{1,0:T(2,128)S(1)} %pad_maximum_fusion.1), channel_id=1, source_target_pairs={{0,3},{1,2},{2,1},{3,0},{4,7},{5,6},{6,5},{7,4},{8,11},{9,10},{10,... | collective-permute-start | bytes 6152 | tf_op jit(solution)/shard_map/ppermute | solution.py:282
  29.3 12.8 %collective-permute-done.9 = f32[3,64]{1,0:T(4,128)S(1)} collective-permute-done((f32[3,64]{1,0:T(4,128)S(1)}, f32[3,64]{1,0:T(4,128)S(1)}, u32[]{:S(2)}, u32[]{:S(2)}) %collective-permute-start.9) | collective-permute-done | bytes 800 | tf_op jit(solution)/shard_map/ppermute | solution.py:282
  48.0 15.3 %all-gather.5.cloned.1.call-done = bf16[512,1536]{1,0:T(8,128)(2,1)} async-done(((bf16[128,1536]{1,0:T(8,128)(2,1)}), bf16[512,1536]{1,0:T(8,128)(2,1)}) %all-gather.5.cloned.1.call-update) | async-done | bytes 1572880 | tf_op jit(solution)/shard_map/all_gather | solution.py:384
  70.5 4.3 %all-to-all-start.1 = ((bf16[8,768,128]{2,1,0:T(8,128)(2,1)}), bf16[8,768,128]{2,1,0:T(8,128)(2,1)}, u32[]{:S(2)}, u32[]{:S(2)}) async-start(bf16[8,768,128]{2,1,0:T(8,128)(2,1)} %bitcast.8), calls=%async_computation.1 | async-start | bytes 3145728 | tf_op jit(solution)/shard_map/all_to_all | solution.py:368
  78.7 5.3 %shard_map.120.d_one_ref = bf16[128,768]{1,0:T(8,128)(2,1)S(1)} custom-call(bf16[4,128,1536]{2,1,0:T(8,128)(2,1)S(1)} %bitcast.114, bf16[1,6144,768]{2,1,0:T(8,128)(2,1)} %bitcast.126), custom_call_target="tpu_custom_call" | custom-call | flops 1207959552 | bytes 11010048 | tf_op jit(solution)/shard_map/pallas_call | solution.py:46
  84.0 5.1 %shard_map.121.refs_0_ = f32[256,2304]{1,0:T(8,128)S(1)} custom-call(s32[1]{0:T(128)} %bitcast.14.at_ref, bf16[256,1536]{1,0:T(8,128)(2,1)S(1)} %get-tuple-element.30.x_ref, bf16[3,6144,768]{2,1,0:T(8,128)(2,1)} %bitcast.120), custom_call_target="tpu_custom_call" | custom-call | flops 1811939328 | bytes 11796480 | tf_op jit(solution)/shard_map/pallas_call | solution.py:76
  109.8 5.2 %shard_map.122.refs_0_ = f32[256,2304]{1,0:T(8,128)S(1)} custom-call(s32[1]{0:T(128)} %bitcast.13.at_ref, bf16[256,1536]{1,0:T(8,128)(2,1)} %collective-permute-done.10.x_ref, bf16[3,6144,768]{2,1,0:T(8,128)(2,1)} %bitcast.121, f32[256,2304]{1,0:T(8,128)S(1)} %shard_map.121.refs_0_), custom_call_target="tpu_custom_call", output_to_operand_aliasing={{}: (3, {})} | custom-call | flops 1811939328 | bytes 11796480 | tf_op jit(solution)/shard_map/pallas_call | solution.py:76
  115.0 5.2 %shard_map.123.refs_0_ = f32[256,2304]{1,0:T(8,128)S(1)} custom-call(s32[1]{0:T(128)} %bitcast.12.at_ref, bf16[256,1536]{1,0:T(8,128)(2,1)} %collective-permute-done.12.x_ref, bf16[3,6144,768]{2,1,0:T(8,128)(2,1)} %bitcast.122, f32[256,2304]{1,0:T(8,128)S(1)} %shard_map.122.refs_0_), custom_call_target="tpu_custom_call", output_to_operand_aliasing={{}: (3, {})} | custom-call | flops 1811939328 | bytes 11796480 | tf_op jit(solution)/shard_map/pallas_call | solution.py:76
  120.3 8.3 %collective-permute-done.13 = bf16[256,1536]{1,0:T(8,128)(2,1)} collective-permute-done((bf16[256,1536]{1,0:T(8,128)(2,1)}, bf16[256,1536]{1,0:T(8,128)(2,1)}, u32[]{:S(2)}, u32[]{:S(2)}) %collective-permute-start.13) | collective-permute-done | bytes 786464 | tf_op jit(solution)/shard_map/ppermute | solution.py:323
  142.7 5.0 %shard_map.124.refs_0_ = f32[256,2304]{1,0:T(8,128)S(1)} custom-call(s32[1]{0:T(128)} %bitcast.10.at_ref, bf16[256,1536]{1,0:T(8,128)(2,1)S(1)} %get-tuple-element.55.x_ref, bf16[3,6144,768]{2,1,0:T(8,128)(2,1)} %bitcast.123, f32[256,2304]{1,0:T(8,128)S(1)} %shard_map.123.refs_0_), custom_call_target="tpu_custom_call", output_to_operand_aliasing={{}: (3, {})} | custom-call | flops 1811939328 | bytes 11796480 | tf_op jit(solution)/shard_map/pallas_call | solution.py:76
  159.3 4.8 %all-to-all-start.2 = ((bf16[8,768,256]{2,1,0:T(8,128)(2,1)}), bf16[8,768,256]{2,1,0:T(8,128)(2,1)}, u32[]{:S(2)}, u32[]{:S(2)}) async-start(bf16[8,768,256]{2,1,0:T(8,128)(2,1)} %bitcast.129), calls=%async_computation.2 | async-start | bytes 6291456 | tf_op jit(solution)/shard_map/all_to_all | solution.py:368
  165.1 5.0 %shard_map.125.proj_ref = f32[256,2304]{1,0:T(8,128)S(1)} custom-call(s32[1]{0:T(128)} %bitcast.5.at_ref, bf16[256,1536]{1,0:T(8,128)(2,1)S(1)} %add.255.x_ref, bf16[3,6144,768]{2,1,0:T(8,128)(2,1)} %bitcast.124, f32[256,2304]{1,0:T(8,128)S(1)} %shard_map.124.refs_0_), custom_call_target="tpu_custom_call", output_to_operand_aliasing={{}: (3, {})} | custom-call | flops 1811939328 | bytes 11796480 | tf_op jit(solution)/shard_map/pallas_call | solution.py:76
  171.8 6.1 %shard_map.127 = bf16[4,256,1536]{2,1,0:T(8,128)(2,1)S(1)} custom-call(bf16[256,768]{1,0:T(8,128)(2,1)S(1)} %shard_map.126.x_ref, bf16[1,6144,768]{2,1,0:T(8,128)(2,1)} %bitcast.127), custom_call_target="tpu_custom_call" | custom-call | flops 2415919104 | bytes 12582912 | tf_op jit(solution)/shard_map/pallas_call | solution.py:112
  184.4 31.1 %all-gather.7.cloned.1.call-done = bf16[512,1536]{1,0:T(8,128)(2,1)} async-done(((bf16[128,1536]{1,0:T(8,128)(2,1)}), bf16[512,1536]{1,0:T(8,128)(2,1)}) %all-gather.7.cloned.1.call-update) | async-done | bytes 1572880 | tf_op jit(solution)/shard_map/all_gather | solution.py:434
  217.0 5.3 %shard_map.128.d_two_ref = bf16[128,768]{1,0:T(8,128)(2,1)S(1)} custom-call(bf16[4,128,1536]{2,1,0:T(8,128)(2,1)S(1)} %bitcast.116, bf16[1,6144,768]{2,1,0:T(8,128)(2,1)} %bitcast.128), custom_call_target="tpu_custom_call" | custom-call | flops 1207959552 | bytes 11010048 | tf_op jit(solution)/shard_map/pallas_call | solution.py:46
  226.4 14.4 %shard_map.130 = bf16[4,256,1536]{2,1,0:T(8,128)(2,1)S(1)} custom-call(bf16[256,3072]{1,0:T(8,128)(2,1)S(1)} %shard_map.129.x_ref.refs_0_, bf16[3,6144,768]{2,1,0:T(8,128)(2,1)} %bitcast.125), custom_call_target="tpu_custom_call" | custom-call | flops 7247757312 | bytes 31457280 | tf_op jit(solution)/shard_map/pallas_call | solution.py:112
  249.4 6.9 %collective-permute-start.18 = (bf16[256,1536]{1,0:T(8,128)(2,1)}, bf16[256,1536]{1,0:T(8,128)(2,1)}, u32[]{:S(2)}, u32[]{:S(2)}) collective-permute-start(bf16[256,1536]{1,0:T(8,128)(2,1)} %fusion.13), channel_id=1, source_target_pairs={{0,1},{1,2},{4,5},{5,6},{8,9},{9,10},{12,13},{13,14},{16,17},{17,1... | collective-permute-start | bytes 2359304 | tf_op jit(solution)/shard_map/ppermute | solution.py:348
  256.2 24.7 %collective-permute-done.26.refs_4_ = bf16[256,3072]{1,0:T(8,128)(2,1)} collective-permute-done((bf16[256,3072]{1,0:T(8,128)(2,1)}, bf16[256,3072]{1,0:T(8,128)(2,1)}, u32[]{:S(2)}, u32[]{:S(2)}) %collective-permute-start.26) | collective-permute-done | bytes 1572896 | tf_op jit(solution)/shard_map/ppermute | solution.py:282
  288.1 4.3 %all-to-all-start.3 = ((bf16[8,768,128]{2,1,0:T(8,128)(2,1)}), bf16[8,768,128]{2,1,0:T(8,128)(2,1)}, u32[]{:S(2)}, u32[]{:S(2)}) async-start(bf16[8,768,128]{2,1,0:T(8,128)(2,1)} %bitcast.131), calls=%async_computation.4 | async-start | bytes 3145728 | tf_op jit(solution)/shard_map/all_to_all | solution.py:368
  297.4 16.9 %collective-permute-done.28.refs_0_ = bf16[256,3072]{1,0:T(8,128)(2,1)} collective-permute-done((bf16[256,3072]{1,0:T(8,128)(2,1)}, bf16[256,3072]{1,0:T(8,128)(2,1)}, u32[]{:S(2)}, u32[]{:S(2)}) %collective-permute-start.28) | collective-permute-done | bytes 1572896 | tf_op jit(solution)/shard_map/ppermute | solution.py:310
  314.3 6.8 %collective-permute-start.19 = (bf16[256,1536]{1,0:T(8,128)(2,1)}, bf16[256,1536]{1,0:T(8,128)(2,1)}, u32[]{:S(2)}, u32[]{:S(2)}) collective-permute-start(bf16[256,1536]{1,0:T(8,128)(2,1)} %get-tuple-element.58), channel_id=1, source_target_pairs={{0,1},{1,2},{2,3},{4,5},{5,6},{6,7},{8,9},{9,10},{10,11},{12,13},{... | collective-permute-start | bytes 2359304 | tf_op jit(solution)/shard_map/ppermute | solution.py:348
  326.4 13.4 %shard_map.131.refs_2_ = f32[4,768,768]{2,1,0:T(8,128)} custom-call(bf16[8,768,256]{2,1,0:T(8,128)(2,1)} %all-to-all-done.2.normed_ref, bf16[8,768,128]{2,1,0:T(8,128)(2,1)} %all-to-all-done.1.one_ref, bf16[8,768,128]{2,1,0:T(8,128)(2,1)} %all-to-all-done.3.two_ref, bf16[256,3072]{1,0:T(8,128)(2,1)S(1)} %copy-done.4, ...), custom_call_target="tpu_custom_call" | custom-call | flops 7247757312 | bytes 15728640 | tf_op jit(solution)/shard_map/pallas_call | solution.py:252
  341.9 14.9 %collective-permute-start.24 = (f32[2,256]{1,0:T(2,128)S(1)}, f32[2,256]{1,0:T(2,128)S(1)}, u32[]{:S(2)}, u32[]{:S(2)}) collective-permute-start(f32[2,256]{1,0:T(2,128)S(1)} %pad_maximum_fusion.2), channel_id=1, source_target_pairs={{0,3},{1,2},{2,1},{3,0},{4,7},{5,6},{6,5},{7,4},{8,11},{9,10},{10,... | collective-permute-start | bytes 6152 | tf_op jit(solution)/shard_map/ppermute | solution.py:282
  357.4 10.9 %shard_map.132 = (bf16[3,768,768]{2,1,0:T(8,128)(2,1)}, bf16[768,768]{1,0:T(8,128)(2,1)}) custom-call(bf16[8,768,256]{2,1,0:T(8,128)(2,1)} %all-to-all-done.2.normed_ref, bf16[8,768,128]{2,1,0:T(8,128)(2,1)} %all-to-all-done.1.one_ref, bf16[8,768,128]{2,1,0:T(8,128)(2,1)} %all-to-all-done.3.two_ref, bf16[256,3072]{1,0:T(8,128)(2,1)} %collective-permute-done.28.refs_0_, ...), custom_call_target="tpu_custom_call" | custom-call | flops 2415919104 | bytes 9437184 | tf_op jit(solution)/shard_map/pallas_call | solution.py:252
  (177 shorter events, 126.7 us)
Async XLA Ops:
  17.5 28.7 %all-to-all-start = ((bf16[8,64,1536]{2,1,0:T(8,128)(2,1)}), bf16[8,64,1536]{2,1,0:T(8,128)(2,1)S(1)}, u32[]{:S(2)}, u32[]{:S(2)}) async-start(bf16[8,64,1536]{2,1,0:T(8,128)(2,1)} %bitcast.3), calls=%async_computation | async-start | bytes 3145728 | tf_op jit(solution)/shard_map/all_to_all | solution.py:392
  21.5 41.8 %all-gather.5.cloned.1.call-start = ((), (), s32[]{:S(2)}) async-start(), calls=%async_computation.6 | async-start | bytes 1966080 | tf_op jit(solution)/shard_map/all_gather | solution.py:384
  63.4 25.8 %collective-permute-start.10 = (bf16[256,1536]{1,0:T(8,128)(2,1)S(1)}, bf16[256,1536]{1,0:T(8,128)(2,1)}, u32[]{:S(2)}, u32[]{:S(2)}) collective-permute-start(bf16[256,1536]{1,0:T(8,128)(2,1)S(1)} %get-tuple-element.30.x_ref), channel_id=1, source_target_pairs={{0,1},{1,2},{2,3},{4,5},{5,6},{6,7},{8,9},{9,10},{10,11},{12,13},{... | collective-permute-start | bytes 2359304 | tf_op jit(solution)/shard_map/ppermute | solution.py:322
  66.6 33.3 %collective-permute-start.12 = (bf16[256,1536]{1,0:T(8,128)(2,1)S(1)}, bf16[256,1536]{1,0:T(8,128)(2,1)}, u32[]{:S(2)}, u32[]{:S(2)}) collective-permute-start(bf16[256,1536]{1,0:T(8,128)(2,1)S(1)} %get-tuple-element.30.x_ref), channel_id=1, source_target_pairs={{1,0},{2,1},{3,2},{5,4},{6,5},{7,6},{9,8},{10,9},{11,10},{13,12},{... | collective-permute-start | bytes 2359304 | tf_op jit(solution)/shard_map/ppermute | solution.py:323
  70.5 82.4 %all-to-all-start.1 = ((bf16[8,768,128]{2,1,0:T(8,128)(2,1)}), bf16[8,768,128]{2,1,0:T(8,128)(2,1)}, u32[]{:S(2)}, u32[]{:S(2)}) async-start(bf16[8,768,128]{2,1,0:T(8,128)(2,1)} %bitcast.8), calls=%async_computation.1 | async-start | bytes 3145728 | tf_op jit(solution)/shard_map/all_to_all | solution.py:368
  104.1 24.4 %collective-permute-start.13 = (bf16[256,1536]{1,0:T(8,128)(2,1)}, bf16[256,1536]{1,0:T(8,128)(2,1)}, u32[]{:S(2)}, u32[]{:S(2)}) collective-permute-start(bf16[256,1536]{1,0:T(8,128)(2,1)} %collective-permute-done.12.x_ref), channel_id=1, source_target_pairs={{1,0},{2,1},{5,4},{6,5},{9,8},{10,9},{13,12},{14,13},{17,16},{18,1... | collective-permute-start | bytes 2359304 | tf_op jit(solution)/shard_map/ppermute | solution.py:323
  130.1 21.2 %collective-permute-start.15 = (bf16[256,1536]{1,0:T(8,128)(2,1)}, bf16[256,1536]{1,0:T(8,128)(2,1)}, u32[]{:S(2)}, u32[]{:S(2)}) collective-permute-start(bf16[256,1536]{1,0:T(8,128)(2,1)} %collective-permute-done.13), channel_id=1, source_target_pairs={{1,0},{5,4},{9,8},{13,12},{17,16},{21,20},{25,24},{29,28}} | collective-permute-start | bytes 2359304 | tf_op jit(solution)/shard_map/ppermute | solution.py:323
  159.3 62.9 %all-to-all-start.2 = ((bf16[8,768,256]{2,1,0:T(8,128)(2,1)}), bf16[8,768,256]{2,1,0:T(8,128)(2,1)}, u32[]{:S(2)}, u32[]{:S(2)}) async-start(bf16[8,768,256]{2,1,0:T(8,128)(2,1)} %bitcast.129), calls=%async_computation.2 | async-start | bytes 6291456 | tf_op jit(solution)/shard_map/all_to_all | solution.py:368
  164.1 51.4 %all-gather.7.cloned.1.call-start = ((), (), s32[]{:S(2)}) async-start(), calls=%async_computation.7 | async-start | bytes 1966080 | tf_op jit(solution)/shard_map/all_gather | solution.py:434
  164.9 174.9 %reduce-scatter.2.cloned.1.call-start = ((), (), s32[]{:S(2)}) async-start(), calls=%async_computation.5 | async-start | bytes 3932160 | tf_op jit(solution)/shard_map/reduce_scatter | solution.py:463
  180.1 42.2 %collective-permute-start.16 = (bf16[256,1536]{1,0:T(8,128)(2,1)}, bf16[256,1536]{1,0:T(8,128)(2,1)}, u32[]{:S(2)}, u32[]{:S(2)}) collective-permute-start(bf16[256,1536]{1,0:T(8,128)(2,1)} %get-tuple-element.61), channel_id=1, source_target_pairs={{0,1},{4,5},{8,9},{12,13},{16,17},{20,21},{24,25},{28,29}} | collective-permute-start | bytes 2359304 | tf_op jit(solution)/shard_map/ppermute | solution.py:348
  182.8 39.4 %collective-permute-start.17 = (bf16[256,1536]{1,0:T(8,128)(2,1)}, bf16[256,1536]{1,0:T(8,128)(2,1)}, u32[]{:S(2)}, u32[]{:S(2)}) collective-permute-start(bf16[256,1536]{1,0:T(8,128)(2,1)} %get-tuple-element.60), channel_id=1, source_target_pairs={{3,2},{7,6},{11,10},{15,14},{19,18},{23,22},{27,26},{31,30}} | collective-permute-start | bytes 2359304 | tf_op jit(solution)/shard_map/ppermute | solution.py:349
  243.7 37.2 %collective-permute-start.26 = (bf16[256,3072]{1,0:T(8,128)(2,1)}, bf16[256,3072]{1,0:T(8,128)(2,1)}, u32[]{:S(2)}, u32[]{:S(2)}) collective-permute-start(bf16[256,3072]{1,0:T(8,128)(2,1)} %copy-done.3), channel_id=1, source_target_pairs={{0,16},{4,20},{8,24},{12,28},{16,0},{20,4},{24,8},{28,12},{1,17},{... | collective-permute-start | bytes 4718600 | tf_op jit(solution)/shard_map/ppermute | solution.py:282
  245.7 36.8 %collective-permute-start.27 = (bf16[256,3072]{1,0:T(8,128)(2,1)}, bf16[256,3072]{1,0:T(8,128)(2,1)}, u32[]{:S(2)}, u32[]{:S(2)}) collective-permute-start(bf16[256,3072]{1,0:T(8,128)(2,1)} %copy-done.3), channel_id=1, source_target_pairs={{0,8},{4,12},{8,0},{12,4},{16,24},{20,28},{24,16},{28,20},{1,9},{5... | collective-permute-start | bytes 4718600 | tf_op jit(solution)/shard_map/ppermute | solution.py:282
  249.4 43.6 %collective-permute-start.18 = (bf16[256,1536]{1,0:T(8,128)(2,1)}, bf16[256,1536]{1,0:T(8,128)(2,1)}, u32[]{:S(2)}, u32[]{:S(2)}) collective-permute-start(bf16[256,1536]{1,0:T(8,128)(2,1)} %fusion.13), channel_id=1, source_target_pairs={{0,1},{1,2},{4,5},{5,6},{8,9},{9,10},{12,13},{13,14},{16,17},{17,1... | collective-permute-start | bytes 2359304 | tf_op jit(solution)/shard_map/ppermute | solution.py:348
  285.2 29.2 %collective-permute-start.28 = (bf16[256,3072]{1,0:T(8,128)(2,1)}, bf16[256,3072]{1,0:T(8,128)(2,1)}, u32[]{:S(2)}, u32[]{:S(2)}) collective-permute-start(bf16[256,3072]{1,0:T(8,128)(2,1)} %broadcast_select_fusion), channel_id=1, source_target_pairs={{0,16},{4,12},{8,24},{12,4},{16,0},{20,28},{24,8},{28,20},{1,17},{... | collective-permute-start | bytes 4718600 | tf_op jit(solution)/shard_map/ppermute | solution.py:310
  288.1 36.8 %all-to-all-start.3 = ((bf16[8,768,128]{2,1,0:T(8,128)(2,1)}), bf16[8,768,128]{2,1,0:T(8,128)(2,1)}, u32[]{:S(2)}, u32[]{:S(2)}) async-start(bf16[8,768,128]{2,1,0:T(8,128)(2,1)} %bitcast.131), calls=%async_computation.4 | async-start | bytes 3145728 | tf_op jit(solution)/shard_map/all_to_all | solution.py:368
  292.4 32.6 %collective-permute-start.30 = (bf16[256,3072]{1,0:T(8,128)(2,1)}, bf16[256,3072]{1,0:T(8,128)(2,1)}, u32[]{:S(2)}, u32[]{:S(2)}) collective-permute-start(bf16[256,3072]{1,0:T(8,128)(2,1)} %collective-permute-done.27.refs_2_), channel_id=1, source_target_pairs={{0,4},{4,0},{8,12},{12,8},{16,20},{20,16},{24,28},{28,24},{1,5},{5... | collective-permute-start | bytes 4718600 | tf_op jit(solution)/shard_map/ppermute | solution.py:282
  292.8 32.2 %collective-permute-start.31 = (bf16[256,3072]{1,0:T(8,128)(2,1)}, bf16[256,3072]{1,0:T(8,128)(2,1)}, u32[]{:S(2)}, u32[]{:S(2)}) collective-permute-start(bf16[256,3072]{1,0:T(8,128)(2,1)} %collective-permute-done.26.refs_4_), channel_id=1, source_target_pairs={{0,4},{4,0},{8,12},{12,8},{16,20},{20,16},{24,28},{28,24},{1,5},{5... | collective-permute-start | bytes 4718600 | tf_op jit(solution)/shard_map/ppermute | solution.py:282
  295.8 25.4 %collective-permute-start.20 = (bf16[256,1536]{1,0:T(8,128)(2,1)}, bf16[256,1536]{1,0:T(8,128)(2,1)}, u32[]{:S(2)}, u32[]{:S(2)}) collective-permute-start(bf16[256,1536]{1,0:T(8,128)(2,1)} %get-tuple-element.59), channel_id=1, source_target_pairs={{2,1},{3,2},{6,5},{7,6},{10,9},{11,10},{14,13},{15,14},{18,17},{19... | collective-permute-start | bytes 2359304 | tf_op jit(solution)/shard_map/ppermute | solution.py:349
  314.3 42.5 %collective-permute-start.29 = (bf16[256,3072]{1,0:T(8,128)(2,1)}, bf16[256,3072]{1,0:T(8,128)(2,1)}, u32[]{:S(2)}, u32[]{:S(2)}) collective-permute-start(bf16[256,3072]{1,0:T(8,128)(2,1)} %collective-permute-done.28.refs_0_), channel_id=1, source_target_pairs={{0,4},{4,0},{8,12},{12,8},{16,20},{20,16},{24,28},{28,24},{1,5},{5... | collective-permute-start | bytes 4718600 | tf_op jit(solution)/shard_map/ppermute | solution.py:282
  314.3 54.1 %collective-permute-start.19 = (bf16[256,1536]{1,0:T(8,128)(2,1)}, bf16[256,1536]{1,0:T(8,128)(2,1)}, u32[]{:S(2)}, u32[]{:S(2)}) collective-permute-start(bf16[256,1536]{1,0:T(8,128)(2,1)} %get-tuple-element.58), channel_id=1, source_target_pairs={{0,1},{1,2},{2,3},{4,5},{5,6},{6,7},{8,9},{9,10},{10,11},{12,13},{... | collective-permute-start | bytes 2359304 | tf_op jit(solution)/shard_map/ppermute | solution.py:348
  323.4 45.0 %collective-permute-start.21 = (bf16[256,1536]{1,0:T(8,128)(2,1)}, bf16[256,1536]{1,0:T(8,128)(2,1)}, u32[]{:S(2)}, u32[]{:S(2)}) collective-permute-start(bf16[256,1536]{1,0:T(8,128)(2,1)} %fusion.12), channel_id=1, source_target_pairs={{1,0},{2,1},{3,2},{5,4},{6,5},{7,6},{9,8},{10,9},{11,10},{13,12},{... | collective-permute-start | bytes 2359304 | tf_op jit(solution)/shard_map/ppermute | solution.py:349
  341.9 26.5 %collective-permute-start.24 = (f32[2,256]{1,0:T(2,128)S(1)}, f32[2,256]{1,0:T(2,128)S(1)}, u32[]{:S(2)}, u32[]{:S(2)}) collective-permute-start(f32[2,256]{1,0:T(2,128)S(1)} %pad_maximum_fusion.2), channel_id=1, source_target_pairs={{0,3},{1,2},{2,1},{3,0},{4,7},{5,6},{6,5},{7,4},{8,11},{9,10},{10,... | collective-permute-start | bytes 6152 | tf_op jit(solution)/shard_map/ppermute | solution.py:282
  (32 other events, 307.0 us)
Sparse Core Ops, SparseCore 0:
  24.5 38.7 all-gather.4
  167.1 48.3 all-gather.6
  243.8 77.6 reduce-scatter.1

commit v2 on v1

--- a/solution.py
+++ b/solution.py
@@ -62,44 +62,10 @@
     )(x, w)
 
 
-def add_block_kernel(first, width, at_ref, x_ref, w_ref, *refs):
-    out_ref = refs[-1]
-    term = jnp.dot(x_ref[...], w_ref[0], preferred_element_type=jnp.float32)
-    out_ref[...] = term if first else refs[0][...] + term
-
-
-def add_block(total, x, w, at):
-    rows, part = x.shape
-    kinds, _, width = w.shape
-    sums = pl.BlockSpec((rows, width), lambda t, at_ref: (0, t))
-    before = [] if total is None else [total]
-    return pl.pallas_call(
-        functools.partial(add_block_kernel, total is None, width),
-        grid_spec=pltpu.PrefetchScalarGridSpec(
-            num_scalar_prefetch=1,
-            grid=(kinds,),
-            in_specs=[
-                pl.BlockSpec((rows, part), lambda t, at_ref: (0, 0)),
-                pl.BlockSpec((1, part, width), lambda t, at_ref: (t, at_ref[0], 0)),
-            ]
-            + [sums] * len(before),
-            out_specs=sums,
-        ),
-        out_shape=jax.ShapeDtypeStruct((rows, kinds * width), jnp.float32),
-        input_output_aliases={} if total is None else {3: 0},
-        compiler_params=params(),
-        cost_estimate=pl.CostEstimate(
-            flops=2 * rows * part * kinds * width,
-            bytes_accessed=2 * kinds * part * width + 8 * rows * kinds * width,
-            transcendentals=0,
-        ),
-    )(at.reshape(1).astype(jnp.int32), x, w, *before)
-
-
 def expand_kernel(kinds, width, x_ref, w_ref, out_ref):
     total = None
     for t in range(kinds):
-        term = dot_f32(x_ref[:, t * width : (t + 1) * width], w_ref[t], (1,), (1,))
+        term = dot_f32(w_ref[t], x_ref[:, t * width : (t + 1) * width], (1,), (1,))
         total = term if total is None else total + term
     out_ref[0] = total.astype(jnp.bfloat16)
 
@@ -116,8 +82,8 @@
             pl.BlockSpec((rows, kinds * width), lambda at, cut: (0, 0)),
             pl.BlockSpec((kinds, piece, width), lambda at, cut: (0, at * cuts + cut, 0)),
         ],
-        out_specs=pl.BlockSpec((1, rows, piece), lambda at, cut: (at, 0, cut)),
-        out_shape=jax.ShapeDtypeStruct((parts, rows, part), jnp.bfloat16),
+        out_specs=pl.BlockSpec((1, piece, rows), lambda at, cut: (at, cut, 0)),
+        out_shape=jax.ShapeDtypeStruct((parts, part, rows), jnp.bfloat16),
         compiler_params=params(),
         cost_estimate=pl.CostEstimate(
             flops=2 * rows * depth * kinds * width,
@@ -135,9 +101,14 @@
 
 def head_forward(proj_ref, same, gain_ref, heads, head):
     width = heads * DH
-    q_unit, q_rstd = unit_heads(proj_ref[:, head * DH : (head + 1) * DH])
-    k_unit, k_rstd = unit_heads(proj_ref[:, width + head * DH : width + (head + 1) * DH])
-    values = proj_ref[:, 2 * width + head * DH : 2 * width + (head + 1) * DH].astype(jnp.bfloat16)
+
+    def load(kind):
+        start = kind * width + head * DH
+        return proj_ref[:, start : start + DH]
+
+    q_unit, q_rstd = unit_heads(load(0))
+    k_unit, k_rstd = unit_heads(load(1))
+    values = load(2).astype(jnp.bfloat16)
     queries = (q_unit * gain_ref[0:1, :]).astype(jnp.bfloat16)
     keys = (k_unit * gain_ref[1:2, :]).astype(jnp.bfloat16)
     scores = dot_f32(queries, keys, (1,), (1,)) * DH ** (-0.5)
@@ -205,7 +176,7 @@
     )(projected, segment.reshape(rows, 1), segment.reshape(1, rows), qk_gain, *extra)
 
 
-def weight_kernel(keys, scale, normed_ref, one_ref, two_ref, *refs):
+def weight_kernel(keys, scale, normed_ref, cot_ref, *refs):
     b_refs, refs = refs[: len(keys)], refs[len(keys) :]
     me, t = lax.axis_index("dp"), pl.program_id(0)
 
@@ -221,7 +192,7 @@
         return normed_ref[at]
 
     def cot(at):
-        return jnp.concatenate([one_ref[at], two_ref[at]], 1)
+        return cot_ref[at]
 
     if scale is None:
         total = refs[0].at[0]
@@ -242,17 +213,16 @@
             out_ref[...] = (total[...] * scale).astype(jnp.bfloat16)
 
 
-def weight_grads(normed_cols, cot_one, cot_two, gathered, keys, before, scale):
+def weight_grads(normed_cols, cot_cols, gathered, keys, before, scale):
     count, depth, rows = normed_cols.shape
     width = gathered[0].shape[1] // 4
     whole = pl.BlockSpec((count, depth, rows), lambda t: (0, 0, 0))
-    half = pl.BlockSpec((count, depth, rows // 2), lambda t: (0, 0, 0))
     sums = pl.BlockSpec((1, depth, width), lambda t: (t, 0, 0))
     sums_shape = jax.ShapeDtypeStruct((4, depth, width), jnp.float32)
     return pl.pallas_call(
         functools.partial(weight_kernel, keys, scale),
         grid=(4,),
-        in_specs=[whole, half, half]
+        in_specs=[whole, whole]
         + [pl.BlockSpec((rows, width), lambda t: (0, t))] * len(keys)
         + ([] if before is None else [sums]),
         out_specs=sums
@@ -274,7 +244,7 @@
             bytes_accessed=4 * count * depth * rows + 8 * len(keys) * rows * width,
             transcendentals=0,
         ),
-    )(normed_cols, cot_one, cot_two, *gathered, *([] if before is None else [before]))
+    )(normed_cols, cot_cols, *gathered, *([] if before is None else [before]))
 
 
 def flip(values, axis, bit):
@@ -312,25 +282,6 @@
     near.update(spread({high: over_high}))
     near.update(spread({low: over_low}))
     return near, spread({high | low: far})
-
-
-def line_blocks(values, axis, between):
-    count, me = lax.axis_size(axis), lax.axis_index(axis)
-    blocks = [(me, None, values)]
-    right = left = values
-    for step in range(1, count):
-        right = lax.ppermute(right, axis, [(at, at + 1) for at in range(step - 1, count - 1)])
-        left = lax.ppermute(left, axis, [(at, at - 1) for at in range(1, count - step + 1)])
-        if step == count // 2:
-            right, left = between(right, left)
-        over, under = me >= step, me + step < count
-        if 2 * step >= count:
-            at = jnp.where(over, me - step, jnp.minimum(me + step, count - 1))
-            blocks.append((at, over | under, right + left))
-        else:
-            blocks.append((jnp.maximum(me - step, 0), over, right))
-            blocks.append((jnp.minimum(me + step, count - 1), under, left))
-    return blocks
 
 
 def add_bf(one, two):
@@ -379,8 +330,8 @@
     w_t = jnp.transpose(w_qkv, (1, 0, 2))
     w_out_t = w_out[None]
 
-    half = group_rows // 2
-    first_rows, dest_group = lax.optimization_barrier((cotangent[:half], dest_group))
+    early = group_rows // 4
+    first_rows, dest_group = lax.optimization_barrier((cotangent[:early], dest_group))
     cot_one = lax.all_gather(first_rows, "mp", axis=0, tiled=False)
 
     position = jnp.arange(group_rows, dtype=jnp.int32)
@@ -422,54 +373,38 @@
     my_gain = lax.dynamic_slice_in_dim(ln_gain, my_index * part_width, part_width, 0)
     unit_rows = (packed.astype(jnp.float32) - mean) * rstd
     normed_part = (unit_rows * my_gain).astype(jnp.bfloat16)
+
     normed_part, cot_one = lax.optimization_barrier((normed_part, cot_one))
-
-    late = [None]
-
-    def between(right, left):
-        right, left, late[0] = lax.optimization_barrier((right, left, cotangent[half:]))
-        return right, left
-
-    blocks = line_blocks(normed_part, "mp", between)
-    cot_two = lax.all_gather(late[0], "mp", axis=0, tiled=False)
-    cot_cols_one = columns_to_owner(jnp.swapaxes(cot_one, 1, 2), "dp")
+    normed = lax.all_gather(normed_part, "mp", axis=0, tiled=False)
     d_heads_one = project(cot_one, w_out_t, parts, jnp.bfloat16)
-    projected = None
-    turned = jnp.zeros((parts, part_width, group_rows), jnp.bfloat16)
-    for order, (at, there, block) in enumerate(blocks):
-        if order == len(blocks) - 1:
-            block, cot_cols_one, d_heads_one, projected = lax.optimization_barrier(
-                (block, cot_cols_one, d_heads_one, projected)
-            )
-        projected = add_block(projected, block, w_t, at)
-        block_t = block.T
-        if there is not None:
-            held = lax.dynamic_index_in_dim(turned, at, 0, keepdims=False)
-            block_t = jnp.where(there, block_t, held)
-        turned = lax.dynamic_update_index_in_dim(turned, block_t, at, 0)
-    normed_cols = columns_to_owner(turned, "dp")
+    normed, d_heads_one, late_cot = lax.optimization_barrier(
+        (normed, d_heads_one, cotangent[early:])
+    )
+    cot_two = lax.all_gather(late_cot, "mp", axis=0, tiled=False)
+    projected = project(normed, w_t, parts, jnp.float32)
 
     heads_out = attention(forward_kernel, projected, segment, qk_gain, (), 1)
     first_step, go_on = line_reduce(expand(heads_out, w_out_t, parts, 1), "mp")
+    normed_cols = columns_to_owner(jnp.swapaxes(normed, 1, 2), "dp")
     d_heads_two = project(cot_two, w_out_t, parts, jnp.bfloat16)
     first_step, normed_cols, d_heads_one, d_heads_two = lax.optimization_barrier(
         (first_step, normed_cols, d_heads_one, d_heads_two)
     )
-    attn = go_on(*first_step)
+    attn = go_on(*first_step).T
     output = (packed.astype(jnp.float32) + attn).astype(jnp.bfloat16)
 
     d_all = attention(backward_kernel, projected, segment, qk_gain, (d_heads_one, d_heads_two), 4)
     d_part = expand(d_all, w_t, parts, 2)
     d_normed = lax.psum_scatter(d_part, "mp", scatter_dimension=0, tiled=False)
-    d_unit = d_normed.astype(jnp.float32) * my_gain
+    d_unit = d_normed.T.astype(jnp.float32) * my_gain
     sums = jnp.stack([jnp.sum(d_unit, -1), jnp.sum(d_unit * unit_rows, -1)])
     sums = sum(exchange_small(sums, "mp")) / full_width
     d_input = rstd * (d_unit - sums[0][:, None] - unit_rows * sums[1][:, None])
     input_grad = (cotangent.astype(jnp.float32) + d_input).astype(jnp.bfloat16)
 
     scale_grad = 1.0 / math.sqrt(group_rows * groups)
-    cot_cols_two = columns_to_owner(jnp.swapaxes(cot_two, 1, 2), "dp")
-    columns = (normed_cols, cot_cols_one, cot_cols_two)
+    cot_turned = jnp.swapaxes(jnp.concatenate([cot_one, cot_two], 1), 1, 2)
+    columns = (normed_cols, columns_to_owner(cot_turned, "dp"))
     sums_near = None
     near, far = gather_xor(d_all, "dp")
     for held, scale in ((near, None), (far, scale_grad)):

time: 381 us -> 353 us (0.927)
  blocking collectives: 0 us -> 19.8 us
  waiting for transfers between devices: 117 us -> 104 us
  local copies, waits for them, and re-layouts: 47.6 us -> 35.6 us
  starting transfers between devices: 81.8 us -> 71.8 us
  Pallas kernels: 86.7 us -> 78.3 us
  other arithmetic: 27.1 us -> 23 us
    pallas_call x5 -> x0, Pallas kernels: 25.6 us -> none  [add_block(): pl.pallas_call(functools.partial(add_block_kernel, total is None, width),...]
    ppermute x19, waiting for transfers between devices: 40.8 us -> 18.1 us  [flip(): return lax.ppermute(values, axis, [(at, at ^ bit) for at in range(count)])]
    all_gather x0 -> x1, blocking collectives: none -> 19.8 us  [shards(): cot_one = lax.all_gather(first_rows, 'mp', axis=0, tiled=False)]
    pallas_call x2 -> x3, Pallas kernels: 10.6 us -> 27.9 us  [project(): pl.pallas_call(functools.partial(project_kernel, steps, width), grid=(ste...]
    all_gather x2, waiting for transfers between devices: 46.5 us -> 62.3 us  [the longest x1 56.1 us: shards(): normed = lax.all_gather(normed_part, 'mp', axis=0, tiled=False)]
    dynamic_slice x8 -> x0, local copies, waits for them, and re-layouts: 12.2 us -> none  [shards(): held = lax.dynamic_index_in_dim(turned, at, 0, keepdims=False)]
    ppermute x6 -> x0, waiting for transfers between devices: 11.8 us -> none  [the longest x3 11.8 us: line_blocks(): lax.ppermute(left, axis, [(at, at - 1) for at in range(1, count - step +...]
    ppermute x3, starting transfers between devices: 16.5 us -> 28.1 us  [send(): lax.ppermute(to_right, axis, [(at, at + 1) for at in range(step)])]
  transfers between devices with their start and end apart: 39 -> 32, of which waited for: 9 -> 9; matrix products, arithmetic and copies ran while one was open for 15% -> 10% of each run, Pallas kernels for 18% -> 17%
where the time goes in v2:
time: 353 us; the launch traced here: 352 us
  waiting for transfers between devices  104 us (29%)
  Pallas kernels  78.3 us (22%)
  starting transfers between devices  71.8 us (20%)
  local copies, waits for them, and re-layouts  35.6 us (10%)
  other arithmetic  23 us (7%)
  blocking collectives  19.8 us (6%)
  between operations  14.4 us (4%)
  matrix products  5.11 us (1%)
    all_gather x1, waiting for transfers between devices, shards(): normed = lax.all_gather(normed_part, 'mp', axis=0, tiled=False)  56.1 us
    ppermute x3, starting transfers between devices, send(): lax.ppermute(to_right, axis, [(at, at + 1) for at in range(step)])  28.1 us
    pallas_call x3, Pallas kernels, project(): pl.pallas_call(functools.partial(project_kernel, steps, width), grid=(ste...  27.9 us
    ppermute x19, starting transfers between devices, flip(): return lax.ppermute(values, axis, [(at, at ^ bit) for at in range(count)])  25.7 us
    pallas_call x2, Pallas kernels, weight_grads(): pl.pallas_call(functools.partial(weight_kernel, keys, scale), grid=(4,),...  24.4 us
    pallas_call x2, Pallas kernels, expand(): pl.pallas_call(functools.partial(expand_kernel, kinds, width), grid=(part...  20.2 us
    all_gather x1, blocking collectives, shards(): cot_one = lax.all_gather(first_rows, 'mp', axis=0, tiled=False)  19.8 us
    ppermute x19, waiting for transfers between devices, flip(): return lax.ppermute(values, axis, [(at, at ^ bit) for at in range(count)])  18.1 us
  transfers between devices with their start and end apart: 32, of which 9 were waited for; matrix products, arithmetic and copies ran while one was open for 10% of the time, Pallas kernels for 17%

profile of v2, /device:TPU:0, one launch (start us, length us, event | category | flops | bytes accessed | tf_op | source)
XLA Modules:
  0.0 351.7 jit_solution(1813763787547731578)
XLA Ops:
  12.2 5.1 %collective-permute-start.2 = (f32[2,256]{1,0:T(2,128)S(1)}, f32[2,256]{1,0:T(2,128)S(1)}, u32[]{:S(2)}, u32[]{:S(2)}) collective-permute-start(f32[2,256]{1,0:T(2,128)S(1)} %pad_maximum_fusion.1), channel_id=1, source_target_pairs={{0,3},{1,2},{2,1},{3,0},{4,7},{5,6},{6,5},{7,4},{8,11},{9,10},{10,... | collective-permute-start | bytes 6152 | tf_op jit(solution)/shard_map/ppermute | solution.py:252
  18.0 4.0 %all-to-all-start = ((bf16[8,64,1536]{2,1,0:T(8,128)(2,1)}), bf16[8,64,1536]{2,1,0:T(8,128)(2,1)S(1)}, u32[]{:S(2)}, u32[]{:S(2)}) async-start(bf16[8,64,1536]{2,1,0:T(8,128)(2,1)} %bitcast.3), calls=%async_computation | async-start | bytes 3145728 | tf_op jit(solution)/shard_map/all_to_all | solution.py:343
  22.2 19.8 %all-gather = bf16[256,1536]{1,0:T(8,128)(2,1)S(1)} all-gather(bf16[64,1536]{1,0:T(8,128)(2,1)S(1)} %slice-done), channel_id=2, replica_groups=mesh['dp'=8,'mp'=4] {'mp'}, dimensions={0}, use_global_device_ids=true | all-gather | bytes 983040 | tf_op jit(solution)/shard_map/all_gather | solution.py:335
  55.7 5.4 %shard_map.120.d_one_ref = bf16[64,768]{1,0:T(8,128)(2,1)S(1)} custom-call(bf16[4,64,1536]{2,1,0:T(8,128)(2,1)S(1)} %bitcast.98, bf16[1,6144,768]{2,1,0:T(8,128)(2,1)} %bitcast.105), custom_call_target="tpu_custom_call" | custom-call | flops 603979776 | bytes 10223616 | tf_op jit(solution)/shard_map/pallas_call | solution.py:46
  61.1 56.1 %all-gather.6.cloned.1.call-done = bf16[1024,1536]{0,1:T(8,128)(2,1)} async-done(((bf16[256,1536]{0,1:T(8,128)(2,1)}), bf16[1024,1536]{0,1:T(8,128)(2,1)}) %all-gather.6.cloned.1.call-update) | async-done | bytes 3145744 | tf_op jit(solution)/shard_map/all_gather | solution.py:378
  117.1 4.8 %reshape.164 = bf16[4,256,1536]{1,0,2:T(4,128)(2,1)S(1)} reshape(bf16[1024,1536]{0,1:T(8,128)(2,1)} %all-gather.6.cloned.1.call-done) | data formatting | bytes 6291456 | tf_op jit(solution)/shard_map/all_gather | solution.py:378
  124.7 4.5 %all-to-all-start.1 = ((bf16[8,768,256]{2,1,0:T(8,128)(2,1)}), bf16[8,768,256]{2,1,0:T(8,128)(2,1)}, u32[]{:S(2)}, u32[]{:S(2)}) async-start(bf16[8,768,256]{2,1,0:T(8,128)(2,1)} %bitcast.109), calls=%async_computation.1 | async-start | bytes 6291456 | tf_op jit(solution)/shard_map/all_to_all | solution.py:319
  129.4 4.4 %copy.30.x_ref = bf16[4,256,1536]{2,1,0:T(8,128)(2,1)S(1)} copy(bf16[4,256,1536]{1,0,2:T(4,128)(2,1)} %copy-done.12) | data formatting | bytes 6291456 | tf_op jit(solution)/shard_map/optimization_barrier | solution.py:380
  133.8 16.9 %shard_map.121.proj_ref = f32[256,2304]{1,0:T(8,128)S(1)} custom-call(bf16[4,256,1536]{2,1,0:T(8,128)(2,1)S(1)} %copy.30.x_ref, bf16[3,6144,768]{2,1,0:T(8,128)(2,1)} %bitcast.103), custom_call_target="tpu_custom_call" | custom-call | flops 7247757312 | bytes 31457280 | tf_op jit(solution)/shard_map/pallas_call | solution.py:46
  153.7 6.0 %shard_map.123 = bf16[4,1536,256]{2,1,0:T(8,128)(2,1)S(1)} custom-call(bf16[256,768]{1,0:T(8,128)(2,1)S(1)} %shard_map.122.x_ref, bf16[1,6144,768]{2,1,0:T(8,128)(2,1)} %bitcast.106), custom_call_target="tpu_custom_call" | custom-call | flops 2415919104 | bytes 12582912 | tf_op jit(solution)/shard_map/pallas_call | solution.py:78
  164.7 6.2 %all-gather.8.cloned.1.call-done = bf16[768,1536]{1,0:T(8,128)(2,1)} async-done(((bf16[192,1536]{1,0:T(8,128)(2,1)}), bf16[768,1536]{1,0:T(8,128)(2,1)}) %all-gather.8.cloned.1.call-update) | async-done | bytes 2359312 | tf_op jit(solution)/shard_map/all_gather | solution.py:383
  172.6 5.6 %shard_map.124.d_two_ref = bf16[192,768]{1,0:T(8,128)(2,1)S(1)} custom-call(bf16[4,192,1536]{2,1,0:T(8,128)(2,1)S(1)} %bitcast.96, bf16[1,6144,768]{2,1,0:T(8,128)(2,1)} %bitcast.107), custom_call_target="tpu_custom_call" | custom-call | flops 1811939328 | bytes 11796480 | tf_op jit(solution)/shard_map/pallas_call | solution.py:46
  178.2 5.7 %collective-permute-done.10 = bf16[1536,256]{1,0:T(8,128)(2,1)} collective-permute-done((bf16[1536,256]{1,0:T(8,128)(2,1)}, bf16[1536,256]{1,0:T(8,128)(2,1)}, u32[]{:S(2)}, u32[]{:S(2)}) %collective-permute-start.10) | collective-permute-done | bytes 786464 | tf_op jit(solution)/shard_map/ppermute | solution.py:299
  186.5 4.1 %shard_map.125.x_ref.refs_0_ = bf16[256,3072]{1,0:T(8,128)(2,1)S(1)} custom-call(f32[256,2304]{1,0:T(8,128)S(1)} %copy-done.2, s32[256,1]{1,0:T(8,128)S(1)} %copy-done.9, s32[1,256]{1,0:T(1,128)S(1)} %bitcast.102, f32[2,128]{1,0:T(2,128)S(1)} %copy-done.11, bf16[64,768]{1,0:T(8,128)(2,1)S(1)} %shard_map.120.d_one_ref, bf16[192,768]{1,0:T(8,128)(2,1)S(1)} %shard_map.124.d_two_ref), custom_call_target="tpu_custom_call" | custom-call | flops 805306368 | bytes 4718592 | tf_op jit(solution)/shard_map/pallas_call | solution.py:167
  190.7 14.2 %shard_map.126 = bf16[4,1536,256]{2,1,0:T(8,128)(2,1)S(1)} custom-call(bf16[256,3072]{1,0:T(8,128)(2,1)S(1)} %shard_map.125.x_ref.refs_0_, bf16[3,6144,768]{2,1,0:T(8,128)(2,1)} %bitcast.104), custom_call_target="tpu_custom_call" | custom-call | flops 7247757312 | bytes 31457280 | tf_op jit(solution)/shard_map/pallas_call | solution.py:78
  213.5 5.3 %collective-permute-start.12 = (bf16[1536,256]{1,0:T(8,128)(2,1)}, bf16[1536,256]{1,0:T(8,128)(2,1)}, u32[]{:S(2)}, u32[]{:S(2)}) collective-permute-start(bf16[1536,256]{1,0:T(8,128)(2,1)} %fusion.14), channel_id=1, source_target_pairs={{0,1},{1,2},{4,5},{5,6},{8,9},{9,10},{12,13},{13,14},{16,17},{17,1... | collective-permute-start | bytes 2359304 | tf_op jit(solution)/shard_map/ppermute | solution.py:299
  221.8 4.6 %copy.35 = bf16[4,1536,256]{2,1,0:T(8,128)(2,1)} copy(bf16[4,1536,256]{1,2,0:T(8,128)(2,1)} %maximum_bitcast_fusion) | data formatting | bytes 6291456 | tf_op jit(solution)/shard_map/transpose | solution.py:406
  226.5 4.5 %all-to-all-start.2 = ((bf16[8,768,256]{2,1,0:T(8,128)(2,1)}), bf16[8,768,256]{2,1,0:T(8,128)(2,1)}, u32[]{:S(2)}, u32[]{:S(2)}) async-start(bf16[8,768,256]{2,1,0:T(8,128)(2,1)} %bitcast.108), calls=%async_computation.3 | async-start | bytes 6291456 | tf_op jit(solution)/shard_map/all_to_all | solution.py:319
  230.9 14.5 %collective-permute-done.20.refs_4_ = bf16[256,3072]{1,0:T(8,128)(2,1)} collective-permute-done((bf16[256,3072]{1,0:T(8,128)(2,1)}, bf16[256,3072]{1,0:T(8,128)(2,1)}, u32[]{:S(2)}, u32[]{:S(2)}) %collective-permute-start.20) | collective-permute-done | bytes 1572896 | tf_op jit(solution)/shard_map/ppermute | solution.py:252
  259.3 20.6 %collective-permute-start.13 = (bf16[1536,256]{1,0:T(8,128)(2,1)}, bf16[1536,256]{1,0:T(8,128)(2,1)}, u32[]{:S(2)}, u32[]{:S(2)}) collective-permute-start(bf16[1536,256]{1,0:T(8,128)(2,1)} %get-tuple-element.58), channel_id=1, source_target_pairs={{0,1},{1,2},{2,3},{4,5},{5,6},{6,7},{8,9},{9,10},{10,11},{12,13},{... | collective-permute-start | bytes 2359304 | tf_op jit(solution)/shard_map/ppermute | solution.py:299
  279.9 15.7 %collective-permute-done.22.refs_0_ = bf16[256,3072]{1,0:T(8,128)(2,1)} collective-permute-done((bf16[256,3072]{1,0:T(8,128)(2,1)}, bf16[256,3072]{1,0:T(8,128)(2,1)}, u32[]{:S(2)}, u32[]{:S(2)}) %collective-permute-start.22) | collective-permute-done | bytes 1572896 | tf_op jit(solution)/shard_map/ppermute | solution.py:280
  302.1 13.5 %shard_map.127.refs_2_ = f32[4,768,768]{2,1,0:T(8,128)} custom-call(bf16[8,768,256]{2,1,0:T(8,128)(2,1)} %all-to-all-done.1.normed_ref, bf16[8,768,256]{2,1,0:T(8,128)(2,1)} %all-to-all-done.2.cot_ref, bf16[256,3072]{1,0:T(8,128)(2,1)S(1)} %copy-done.7, bf16[256,3072]{1,0:T(8,128)(2,1)} %collective-permute-done.19.refs_1_, ...), custom_call_target="tpu_custom_call" | custom-call | flops 7247757312 | bytes 15728640 | tf_op jit(solution)/shard_map/pallas_call | solution.py:222
  319.0 7.5 %collective-permute-start.18 = (f32[2,256]{1,0:T(2,128)S(1)}, f32[2,256]{1,0:T(2,128)S(1)}, u32[]{:S(2)}, u32[]{:S(2)}) collective-permute-start(f32[2,256]{1,0:T(2,128)S(1)} %pad_maximum_fusion.2), channel_id=1, source_target_pairs={{0,3},{1,2},{2,1},{3,0},{4,7},{5,6},{6,5},{7,4},{8,11},{9,10},{10,... | collective-permute-start | bytes 6152 | tf_op jit(solution)/shard_map/ppermute | solution.py:252
  327.2 10.9 %shard_map.128 = (bf16[3,768,768]{2,1,0:T(8,128)(2,1)}, bf16[768,768]{1,0:T(8,128)(2,1)}) custom-call(bf16[8,768,256]{2,1,0:T(8,128)(2,1)} %all-to-all-done.1.normed_ref, bf16[8,768,256]{2,1,0:T(8,128)(2,1)} %all-to-all-done.2.cot_ref, bf16[256,3072]{1,0:T(8,128)(2,1)} %collective-permute-done.22.refs_0_, bf16[256,3072]{1,0:T(8,128)(2,1)} %collective-permute-done.23.refs_1_, ...), custom_call_target="tpu_custom_call" | custom-call | flops 2415919104 | bytes 9437184 | tf_op jit(solution)/shard_map/pallas_call | solution.py:222
  (159 shorter events, 77.3 us)
Async XLA Ops:
  12.2 29.9 %collective-permute-start.2 = (f32[2,256]{1,0:T(2,128)S(1)}, f32[2,256]{1,0:T(2,128)S(1)}, u32[]{:S(2)}, u32[]{:S(2)}) collective-permute-start(f32[2,256]{1,0:T(2,128)S(1)} %pad_maximum_fusion.1), channel_id=1, source_target_pairs={{0,3},{1,2},{2,1},{3,0},{4,7},{5,6},{6,5},{7,4},{8,11},{9,10},{10,... | collective-permute-start | bytes 6152 | tf_op jit(solution)/shard_map/ppermute | solution.py:252
  17.3 24.8 %collective-permute-start.1 = (f32[2,256]{1,0:T(2,128)S(1)}, f32[2,256]{1,0:T(2,128)S(1)}, u32[]{:S(2)}, u32[]{:S(2)}) collective-permute-start(f32[2,256]{1,0:T(2,128)S(1)} %pad_maximum_fusion.1), channel_id=1, source_target_pairs={{0,2},{1,3},{2,0},{3,1},{4,6},{5,7},{6,4},{7,5},{8,10},{9,11},{10,... | collective-permute-start | bytes 6152 | tf_op jit(solution)/shard_map/ppermute | solution.py:252
  17.3 24.8 %collective-permute-start = (f32[2,256]{1,0:T(2,128)S(1)}, f32[2,256]{1,0:T(2,128)S(1)}, u32[]{:S(2)}, u32[]{:S(2)}) collective-permute-start(f32[2,256]{1,0:T(2,128)S(1)} %pad_maximum_fusion.1), channel_id=1, source_target_pairs={{0,1},{1,0},{2,3},{3,2},{4,5},{5,4},{6,7},{7,6},{8,9},{9,8},{10,11... | collective-permute-start | bytes 6152 | tf_op jit(solution)/shard_map/ppermute | solution.py:252
  18.0 34.4 %all-to-all-start = ((bf16[8,64,1536]{2,1,0:T(8,128)(2,1)}), bf16[8,64,1536]{2,1,0:T(8,128)(2,1)S(1)}, u32[]{:S(2)}, u32[]{:S(2)}) async-start(bf16[8,64,1536]{2,1,0:T(8,128)(2,1)} %bitcast.3), calls=%async_computation | async-start | bytes 3145728 | tf_op jit(solution)/shard_map/all_to_all | solution.py:343
  22.0 95.2 %all-gather.6.cloned.1.call-start = ((), (), s32[]{:S(2)}) async-start(), calls=%async_computation.5 | async-start | bytes 3932160 | tf_op jit(solution)/shard_map/all_gather | solution.py:378
  54.7 116.2 %all-gather.8.cloned.1.call-start = ((), (), s32[]{:S(2)}) async-start(), calls=%async_computation.6 | async-start | bytes 2949120 | tf_op jit(solution)/shard_map/all_gather | solution.py:383
  124.7 59.3 %all-to-all-start.1 = ((bf16[8,768,256]{2,1,0:T(8,128)(2,1)}), bf16[8,768,256]{2,1,0:T(8,128)(2,1)}, u32[]{:S(2)}, u32[]{:S(2)}) async-start(bf16[8,768,256]{2,1,0:T(8,128)(2,1)} %bitcast.109), calls=%async_computation.1 | async-start | bytes 6291456 | tf_op jit(solution)/shard_map/all_to_all | solution.py:319
  129.2 186.4 %reduce-scatter.2.cloned.1.call-start = ((), (), s32[]{:S(2)}) async-start(), calls=%async_computation.4 | async-start | bytes 3932160 | tf_op jit(solution)/shard_map/reduce_scatter | solution.py:398
  161.0 23.0 %collective-permute-start.10 = (bf16[1536,256]{1,0:T(8,128)(2,1)}, bf16[1536,256]{1,0:T(8,128)(2,1)}, u32[]{:S(2)}, u32[]{:S(2)}) collective-permute-start(bf16[1536,256]{1,0:T(8,128)(2,1)} %get-tuple-element.61), channel_id=1, source_target_pairs={{0,1},{4,5},{8,9},{12,13},{16,17},{20,21},{24,25},{28,29}} | collective-permute-start | bytes 2359304 | tf_op jit(solution)/shard_map/ppermute | solution.py:299
  163.1 20.8 %collective-permute-start.11 = (bf16[1536,256]{1,0:T(8,128)(2,1)}, bf16[1536,256]{1,0:T(8,128)(2,1)}, u32[]{:S(2)}, u32[]{:S(2)}) collective-permute-start(bf16[1536,256]{1,0:T(8,128)(2,1)} %get-tuple-element.60), channel_id=1, source_target_pairs={{3,2},{7,6},{11,10},{15,14},{19,18},{23,22},{27,26},{31,30}} | collective-permute-start | bytes 2359304 | tf_op jit(solution)/shard_map/ppermute | solution.py:300
  207.8 23.1 %collective-permute-start.19 = (bf16[256,3072]{1,0:T(8,128)(2,1)}, bf16[256,3072]{1,0:T(8,128)(2,1)}, u32[]{:S(2)}, u32[]{:S(2)}) collective-permute-start(bf16[256,3072]{1,0:T(8,128)(2,1)} %copy-done.6), channel_id=1, source_target_pairs={{0,4},{4,0},{8,12},{12,8},{16,20},{20,16},{24,28},{28,24},{1,5},{5... | collective-permute-start | bytes 4718600 | tf_op jit(solution)/shard_map/ppermute | solution.py:252
  207.9 37.6 %collective-permute-start.20 = (bf16[256,3072]{1,0:T(8,128)(2,1)}, bf16[256,3072]{1,0:T(8,128)(2,1)}, u32[]{:S(2)}, u32[]{:S(2)}) collective-permute-start(bf16[256,3072]{1,0:T(8,128)(2,1)} %copy-done.6), channel_id=1, source_target_pairs={{0,16},{4,20},{8,24},{12,28},{16,0},{20,4},{24,8},{28,12},{1,17},{... | collective-permute-start | bytes 4718600 | tf_op jit(solution)/shard_map/ppermute | solution.py:252
  209.7 37.6 %collective-permute-start.21 = (bf16[256,3072]{1,0:T(8,128)(2,1)}, bf16[256,3072]{1,0:T(8,128)(2,1)}, u32[]{:S(2)}, u32[]{:S(2)}) collective-permute-start(bf16[256,3072]{1,0:T(8,128)(2,1)} %copy-done.6), channel_id=1, source_target_pairs={{0,8},{4,12},{8,0},{12,4},{16,24},{20,28},{24,16},{28,20},{1,9},{5... | collective-permute-start | bytes 4718600 | tf_op jit(solution)/shard_map/ppermute | solution.py:252
  213.5 39.1 %collective-permute-start.12 = (bf16[1536,256]{1,0:T(8,128)(2,1)}, bf16[1536,256]{1,0:T(8,128)(2,1)}, u32[]{:S(2)}, u32[]{:S(2)}) collective-permute-start(bf16[1536,256]{1,0:T(8,128)(2,1)} %fusion.14), channel_id=1, source_target_pairs={{0,1},{1,2},{4,5},{5,6},{8,9},{9,10},{12,13},{13,14},{16,17},{17,1... | collective-permute-start | bytes 2359304 | tf_op jit(solution)/shard_map/ppermute | solution.py:299
  226.5 74.2 %all-to-all-start.2 = ((bf16[8,768,256]{2,1,0:T(8,128)(2,1)}), bf16[8,768,256]{2,1,0:T(8,128)(2,1)}, u32[]{:S(2)}, u32[]{:S(2)}) async-start(bf16[8,768,256]{2,1,0:T(8,128)(2,1)} %bitcast.108), calls=%async_computation.3 | async-start | bytes 6291456 | tf_op jit(solution)/shard_map/all_to_all | solution.py:319
  250.0 45.6 %collective-permute-start.22 = (bf16[256,3072]{1,0:T(8,128)(2,1)}, bf16[256,3072]{1,0:T(8,128)(2,1)}, u32[]{:S(2)}, u32[]{:S(2)}) collective-permute-start(bf16[256,3072]{1,0:T(8,128)(2,1)} %broadcast_select_fusion), channel_id=1, source_target_pairs={{0,16},{4,12},{8,24},{12,4},{16,0},{20,28},{24,8},{28,20},{1,17},{... | collective-permute-start | bytes 4718600 | tf_op jit(solution)/shard_map/ppermute | solution.py:280
  250.3 50.4 %collective-permute-start.24 = (bf16[256,3072]{1,0:T(8,128)(2,1)}, bf16[256,3072]{1,0:T(8,128)(2,1)}, u32[]{:S(2)}, u32[]{:S(2)}) collective-permute-start(bf16[256,3072]{1,0:T(8,128)(2,1)} %collective-permute-done.21.refs_2_), channel_id=1, source_target_pairs={{0,4},{4,0},{8,12},{12,8},{16,20},{20,16},{24,28},{28,24},{1,5},{5... | collective-permute-start | bytes 4718600 | tf_op jit(solution)/shard_map/ppermute | solution.py:252
  250.3 50.4 %collective-permute-start.25 = (bf16[256,3072]{1,0:T(8,128)(2,1)}, bf16[256,3072]{1,0:T(8,128)(2,1)}, u32[]{:S(2)}, u32[]{:S(2)}) collective-permute-start(bf16[256,3072]{1,0:T(8,128)(2,1)} %collective-permute-done.20.refs_4_), channel_id=1, source_target_pairs={{0,4},{4,0},{8,12},{12,8},{16,20},{20,16},{24,28},{28,24},{1,5},{5... | collective-permute-start | bytes 4718600 | tf_op jit(solution)/shard_map/ppermute | solution.py:252
  255.4 41.5 %collective-permute-start.14 = (bf16[1536,256]{1,0:T(8,128)(2,1)}, bf16[1536,256]{1,0:T(8,128)(2,1)}, u32[]{:S(2)}, u32[]{:S(2)}) collective-permute-start(bf16[1536,256]{1,0:T(8,128)(2,1)} %get-tuple-element.59), channel_id=1, source_target_pairs={{2,1},{3,2},{6,5},{7,6},{10,9},{11,10},{14,13},{15,14},{18,17},{19... | collective-permute-start | bytes 2359304 | tf_op jit(solution)/shard_map/ppermute | solution.py:300
  259.3 78.9 %collective-permute-start.13 = (bf16[1536,256]{1,0:T(8,128)(2,1)}, bf16[1536,256]{1,0:T(8,128)(2,1)}, u32[]{:S(2)}, u32[]{:S(2)}) collective-permute-start(bf16[1536,256]{1,0:T(8,128)(2,1)} %get-tuple-element.58), channel_id=1, source_target_pairs={{0,1},{1,2},{2,3},{4,5},{5,6},{6,7},{8,9},{9,10},{10,11},{12,13},{... | collective-permute-start | bytes 2359304 | tf_op jit(solution)/shard_map/ppermute | solution.py:299
  295.6 31.0 %collective-permute-start.23 = (bf16[256,3072]{1,0:T(8,128)(2,1)}, bf16[256,3072]{1,0:T(8,128)(2,1)}, u32[]{:S(2)}, u32[]{:S(2)}) collective-permute-start(bf16[256,3072]{1,0:T(8,128)(2,1)} %collective-permute-done.22.refs_0_), channel_id=1, source_target_pairs={{0,4},{4,0},{8,12},{12,8},{16,20},{20,16},{24,28},{28,24},{1,5},{5... | collective-permute-start | bytes 4718600 | tf_op jit(solution)/shard_map/ppermute | solution.py:252
  299.1 39.0 %collective-permute-start.15 = (bf16[1536,256]{1,0:T(8,128)(2,1)}, bf16[1536,256]{1,0:T(8,128)(2,1)}, u32[]{:S(2)}, u32[]{:S(2)}) collective-permute-start(bf16[1536,256]{1,0:T(8,128)(2,1)} %fusion.13), channel_id=1, source_target_pairs={{1,0},{2,1},{3,2},{5,4},{6,5},{7,6},{9,8},{10,9},{11,10},{13,12},{... | collective-permute-start | bytes 2359304 | tf_op jit(solution)/shard_map/ppermute | solution.py:300
  319.0 19.1 %collective-permute-start.18 = (f32[2,256]{1,0:T(2,128)S(1)}, f32[2,256]{1,0:T(2,128)S(1)}, u32[]{:S(2)}, u32[]{:S(2)}) collective-permute-start(f32[2,256]{1,0:T(2,128)S(1)} %pad_maximum_fusion.2), channel_id=1, source_target_pairs={{0,3},{1,2},{2,1},{3,0},{4,7},{5,6},{6,5},{7,4},{8,11},{9,10},{10,... | collective-permute-start | bytes 6152 | tf_op jit(solution)/shard_map/ppermute | solution.py:252
  326.5 11.6 %collective-permute-start.16 = (f32[2,256]{1,0:T(2,128)S(1)}, f32[2,256]{1,0:T(2,128)S(1)}, u32[]{:S(2)}, u32[]{:S(2)}) collective-permute-start(f32[2,256]{1,0:T(2,128)S(1)} %pad_maximum_fusion.2), channel_id=1, source_target_pairs={{0,1},{1,0},{2,3},{3,2},{4,5},{5,4},{6,7},{7,6},{8,9},{9,8},{10,11... | collective-permute-start | bytes 6152 | tf_op jit(solution)/shard_map/ppermute | solution.py:252
  (33 other events, 238.3 us)
Sparse Core Ops, SparseCore 0:
  54.9 62.2 all-gather.5
  122.1 48.7 all-gather.7
  207.9 81.0 reduce-scatter.1

commit v3 on v2

--- a/solution.py
+++ b/solution.py
@@ -22,10 +22,32 @@
     return pltpu.CompilerParams(vmem_limit_bytes=VMEM_BYTES)
 
 
-def project_kernel(steps, width, x_ref, w_ref, out_ref, total):
+def turn_kernel(x_ref, one_ref, two_ref):
+    half = one_ref.shape[1]
+    one_ref[...] = x_ref[:half, :].T
+    two_ref[...] = x_ref[half:, :].T
+
+
+def turn_halves(x):
+    rows, part = x.shape
+    shape = jax.ShapeDtypeStruct((part, rows // 2), x.dtype)
+    return pl.pallas_call(
+        turn_kernel,
+        out_shape=[shape, shape],
+        compiler_params=params(),
+        cost_estimate=pl.CostEstimate(flops=0, bytes_accessed=4 * rows * part, transcendentals=0),
+    )(x)
+
+
+def project_kernel(steps, width, x_ref, w_ref, out_ref, total, block):
     at, t = pl.program_id(0), pl.program_id(1)
     columns = pl.ds(pl.multiple_of(t * width, width), width)
-    term = jnp.dot(x_ref[0], w_ref[0], preferred_element_type=jnp.float32)
+
+    @pl.when(t == 0)
+    def _():
+        block[...] = x_ref[0].T
+
+    term = jnp.dot(block[...], w_ref[0], preferred_element_type=jnp.float32)
 
     @pl.when(at == 0)
     def _():
@@ -40,19 +62,22 @@
         out_ref[:, columns] = total[:, columns].astype(out_ref.dtype)
 
 
-def project(x, w, steps, dtype):
-    _, rows, part = x.shape
+def project(x, w, dtype):
+    steps, part, rows = x.shape
     kinds, depth, width = w.shape
     return pl.pallas_call(
         functools.partial(project_kernel, steps, width),
         grid=(steps, kinds),
         in_specs=[
-            pl.BlockSpec((1, rows, part), lambda at, t: (at, 0, 0)),
+            pl.BlockSpec((1, part, rows), lambda at, t: (at, 0, 0)),
             pl.BlockSpec((1, part, width), lambda at, t: (t, at, 0)),
         ],
         out_specs=pl.BlockSpec((rows, kinds * width), lambda at, t: (0, 0)),
         out_shape=jax.ShapeDtypeStruct((rows, kinds * width), dtype),
-        scratch_shapes=[pltpu.VMEM((rows, kinds * width), jnp.float32)],
+        scratch_shapes=[
+            pltpu.VMEM((rows, kinds * width), jnp.float32),
+            pltpu.VMEM((rows, part), jnp.bfloat16),
+        ],
         compiler_params=params(),
         cost_estimate=pl.CostEstimate(
             flops=2 * rows * depth * kinds * width,
@@ -62,35 +87,52 @@
     )(x, w)
 
 
-def expand_kernel(kinds, width, x_ref, w_ref, out_ref):
+def expand_kernel(kinds, width, x_ref, w_ref, *refs):
     total = None
     for t in range(kinds):
         term = dot_f32(w_ref[t], x_ref[:, t * width : (t + 1) * width], (1,), (1,))
         total = term if total is None else total + term
+    if len(refs) == 1:
+        (out_ref,) = refs
+    else:
+        gain_ref, normed_ref, out_ref, sums_ref = refs
+
+        @pl.when((pl.program_id(0) == 0) & (pl.program_id(1) == 0))
+        def _():
+            sums_ref[...] = jnp.zeros_like(sums_ref)
+
+        sums_ref[0:1, :] += jnp.sum(total * gain_ref[...], 0, keepdims=True)
+        sums_ref[1:2, :] += jnp.sum(total * normed_ref[0].astype(jnp.float32), 0, keepdims=True)
     out_ref[0] = total.astype(jnp.bfloat16)
 
 
-def expand(x, w, parts, cuts):
+def expand(x, w, parts, cuts, gain=None, normed=None):
     rows = x.shape[0]
     kinds, depth, width = w.shape
     part = depth // parts
     piece = part // cuts
+    turned = pl.BlockSpec((1, piece, rows), lambda at, cut: (at, cut, 0))
+    turned_shape = jax.ShapeDtypeStruct((parts, part, rows), jnp.bfloat16)
+    more = [] if gain is None else [gain, normed]
     return pl.pallas_call(
         functools.partial(expand_kernel, kinds, width),
         grid=(parts, cuts),
         in_specs=[
             pl.BlockSpec((rows, kinds * width), lambda at, cut: (0, 0)),
             pl.BlockSpec((kinds, piece, width), lambda at, cut: (0, at * cuts + cut, 0)),
-        ],
-        out_specs=pl.BlockSpec((1, piece, rows), lambda at, cut: (at, cut, 0)),
-        out_shape=jax.ShapeDtypeStruct((parts, part, rows), jnp.bfloat16),
+        ]
+        + ([pl.BlockSpec((piece, 1), lambda at, cut: (at * cuts + cut, 0)), turned] if more else []),
+        out_specs=[turned, pl.BlockSpec((2, rows), lambda at, cut: (0, 0))] if more else turned,
+        out_shape=[turned_shape, jax.ShapeDtypeStruct((2, rows), jnp.float32)]
+        if more
+        else turned_shape,
         compiler_params=params(),
         cost_estimate=pl.CostEstimate(
             flops=2 * rows * depth * kinds * width,
             bytes_accessed=2 * kinds * depth * width + 2 * rows * depth,
             transcendentals=0,
         ),
-    )(x, w)
+    )(x, w, *more)
 
 
 def unit_heads(raw):
@@ -176,7 +218,7 @@
     )(projected, segment.reshape(rows, 1), segment.reshape(1, rows), qk_gain, *extra)
 
 
-def weight_kernel(keys, scale, normed_ref, cot_ref, *refs):
+def weight_kernel(keys, scale, normed_ref, one_ref, two_ref, *refs):
     b_refs, refs = refs[: len(keys)], refs[len(keys) :]
     me, t = lax.axis_index("dp"), pl.program_id(0)
 
@@ -192,7 +234,7 @@
         return normed_ref[at]
 
     def cot(at):
-        return cot_ref[at]
+        return jnp.concatenate([one_ref[at], two_ref[at]], 1)
 
     if scale is None:
         total = refs[0].at[0]
@@ -213,16 +255,17 @@
             out_ref[...] = (total[...] * scale).astype(jnp.bfloat16)
 
 
-def weight_grads(normed_cols, cot_cols, gathered, keys, before, scale):
+def weight_grads(normed_cols, cot_one, cot_two, gathered, keys, before, scale):
     count, depth, rows = normed_cols.shape
     width = gathered[0].shape[1] // 4
     whole = pl.BlockSpec((count, depth, rows), lambda t: (0, 0, 0))
+    half = pl.BlockSpec((count, depth, rows // 2), lambda t: (0, 0, 0))
     sums = pl.BlockSpec((1, depth, width), lambda t: (t, 0, 0))
     sums_shape = jax.ShapeDtypeStruct((4, depth, width), jnp.float32)
     return pl.pallas_call(
         functools.partial(weight_kernel, keys, scale),
         grid=(4,),
-        in_specs=[whole, whole]
+        in_specs=[whole, half, half]
         + [pl.BlockSpec((rows, width), lambda t: (0, t))] * len(keys)
         + ([] if before is None else [sums]),
         out_specs=sums
@@ -244,7 +287,7 @@
             bytes_accessed=4 * count * depth * rows + 8 * len(keys) * rows * width,
             transcendentals=0,
         ),
-    )(normed_cols, cot_cols, *gathered, *([] if before is None else [before]))
+    )(normed_cols, cot_one, cot_two, *gathered, *([] if before is None else [before]))
 
 
 def flip(values, axis, bit):
@@ -282,34 +325,6 @@
     near.update(spread({high: over_high}))
     near.update(spread({low: over_low}))
     return near, spread({high | low: far})
-
-
-def add_bf(one, two):
-    return (one.astype(jnp.float32) + two.astype(jnp.float32)).astype(jnp.bfloat16)
-
-
-def line_reduce(parts, axis):
-    count, me = lax.axis_size(axis), lax.axis_index(axis)
-
-    def block(at):
-        return lax.dynamic_index_in_dim(parts, jnp.clip(at, 0, count - 1), 0, keepdims=False)
-
-    def send(step, to_right, to_left):
-        return (
-            lax.ppermute(to_right, axis, [(at, at + 1) for at in range(step)]),
-            lax.ppermute(to_left, axis, [(at, at - 1) for at in range(count - step, count)]),
-        )
-
-    def go_on(right, left):
-        for step in range(2, count):
-            right, left = send(
-                step,
-                add_bf(block(me + count - step), right),
-                add_bf(block(me - count + step), left),
-            )
-        return block(me).astype(jnp.float32) + right.astype(jnp.float32) + left.astype(jnp.float32)
-
-    return send(1, block(me + count - 1), block(me - count + 1)), go_on
 
 
 def columns_to_owner(turned, axis):
@@ -330,9 +345,8 @@
     w_t = jnp.transpose(w_qkv, (1, 0, 2))
     w_out_t = w_out[None]
 
-    early = group_rows // 4
-    first_rows, dest_group = lax.optimization_barrier((cotangent[:early], dest_group))
-    cot_one = lax.all_gather(first_rows, "mp", axis=0, tiled=False)
+    first_cot, second_cot = turn_halves(cotangent)
+    cot_one = lax.all_gather(first_cot, "mp", axis=0, tiled=False)
 
     position = jnp.arange(group_rows, dtype=jnp.int32)
     earlier = (dest_group[:, None] == dest_group[None, :]) & (position[None, :] < position[:, None])
@@ -365,52 +379,51 @@
         for bit, entry in enumerate(came)
     ).reshape(3, slots)
     arrived_at = innotes[0].astype(jnp.int32) - 1
-    from_slot = position[:, None] == arrived_at[None, :]
-    mean = jnp.sum(jnp.where(from_slot, innotes[1][None, :], 0.0), -1, keepdims=True)
-    rstd = jnp.sum(jnp.where(from_slot, innotes[2][None, :], 0.0), -1, keepdims=True)
-    packed = dot_f32(from_slot.astype(jnp.bfloat16), inbox, (1,), (0,)).astype(jnp.bfloat16)
-
-    my_gain = lax.dynamic_slice_in_dim(ln_gain, my_index * part_width, part_width, 0)
+    at_row = arrived_at[:, None] == position[None, :]
+    mean = jnp.sum(jnp.where(at_row, innotes[1][:, None], 0.0), 0, keepdims=True)
+    rstd = jnp.sum(jnp.where(at_row, innotes[2][:, None], 0.0), 0, keepdims=True)
+    packed = dot_f32(inbox, at_row.astype(jnp.bfloat16), (0,), (0,)).astype(jnp.bfloat16)
+    gain_column = ln_gain[:, None]
+    my_gain = lax.dynamic_slice_in_dim(gain_column, my_index * part_width, part_width, 0)
     unit_rows = (packed.astype(jnp.float32) - mean) * rstd
     normed_part = (unit_rows * my_gain).astype(jnp.bfloat16)
 
     normed_part, cot_one = lax.optimization_barrier((normed_part, cot_one))
     normed = lax.all_gather(normed_part, "mp", axis=0, tiled=False)
-    d_heads_one = project(cot_one, w_out_t, parts, jnp.bfloat16)
-    normed, d_heads_one, late_cot = lax.optimization_barrier(
-        (normed, d_heads_one, cotangent[early:])
+    d_heads_one = project(cot_one, w_out_t, jnp.bfloat16)
+    cot_cols_one = columns_to_owner(cot_one, "dp")
+    normed, d_heads_one, cot_cols_one, late_cot = lax.optimization_barrier(
+        (normed, d_heads_one, cot_cols_one, second_cot)
     )
     cot_two = lax.all_gather(late_cot, "mp", axis=0, tiled=False)
-    projected = project(normed, w_t, parts, jnp.float32)
+    projected = project(normed, w_t, jnp.float32)
+    normed_cols = columns_to_owner(normed, "dp")
 
     heads_out = attention(forward_kernel, projected, segment, qk_gain, (), 1)
-    first_step, go_on = line_reduce(expand(heads_out, w_out_t, parts, 1), "mp")
-    normed_cols = columns_to_owner(jnp.swapaxes(normed, 1, 2), "dp")
-    d_heads_two = project(cot_two, w_out_t, parts, jnp.bfloat16)
-    first_step, normed_cols, d_heads_one, d_heads_two = lax.optimization_barrier(
-        (first_step, normed_cols, d_heads_one, d_heads_two)
-    )
-    attn = go_on(*first_step).T
-    output = (packed.astype(jnp.float32) + attn).astype(jnp.bfloat16)
-
+    attn_part = expand(heads_out, w_out_t, parts, 1)
+    attn_part, cot_two = lax.optimization_barrier((attn_part, cot_two))
+    attn = lax.psum_scatter(attn_part, "mp", scatter_dimension=0, tiled=False)
+    output = (packed.astype(jnp.float32) + attn.astype(jnp.float32)).astype(jnp.bfloat16).T
+
+    d_heads_two = project(cot_two, w_out_t, jnp.bfloat16)
+    normed_cols, d_heads_two = lax.optimization_barrier((normed_cols, d_heads_two))
     d_all = attention(backward_kernel, projected, segment, qk_gain, (d_heads_one, d_heads_two), 4)
-    d_part = expand(d_all, w_t, parts, 2)
+    d_part, sums = expand(d_all, w_t, parts, 2, gain_column, normed)
     d_normed = lax.psum_scatter(d_part, "mp", scatter_dimension=0, tiled=False)
-    d_unit = d_normed.T.astype(jnp.float32) * my_gain
-    sums = jnp.stack([jnp.sum(d_unit, -1), jnp.sum(d_unit * unit_rows, -1)])
     sums = sum(exchange_small(sums, "mp")) / full_width
-    d_input = rstd * (d_unit - sums[0][:, None] - unit_rows * sums[1][:, None])
-    input_grad = (cotangent.astype(jnp.float32) + d_input).astype(jnp.bfloat16)
-
     scale_grad = 1.0 / math.sqrt(group_rows * groups)
-    cot_turned = jnp.swapaxes(jnp.concatenate([cot_one, cot_two], 1), 1, 2)
-    columns = (normed_cols, columns_to_owner(cot_turned, "dp"))
+    columns = (normed_cols, cot_cols_one, columns_to_owner(cot_two, "dp"))
     sums_near = None
     near, far = gather_xor(d_all, "dp")
     for held, scale in ((near, None), (far, scale_grad)):
         keys = sorted(held)
         sums_near = weight_grads(*columns, [held[key] for key in keys], keys, sums_near, scale)
+    d_normed, sums_near = lax.optimization_barrier((d_normed, sums_near))
     qkv_grad, out_grad = sums_near
+
+    d_unit = d_normed.astype(jnp.float32) * my_gain
+    d_input = rstd * (d_unit - sums[0:1] - unit_rows * sums[1:2])
+    input_grad = (cotangent.astype(jnp.float32) + d_input.T).astype(jnp.bfloat16)
     return (output, input_grad, qkv_grad.transpose(1, 0, 2), out_grad)
 
 

time: 353 us -> 347 us (0.983)
  waiting for transfers between devices: 104 us -> 187 us
  starting transfers between devices: 71.8 us -> 34.8 us
  local copies, waits for them, and re-layouts: 35.6 us -> 9.82 us
  blocking collectives: 19.8 us -> 0 us
  other arithmetic: 23 us -> 9.32 us
  Pallas kernels: 78.3 us -> 86.1 us
    all_to_all x2 -> x3, waiting for transfers between devices: 0.01 us -> 44.8 us  [columns_to_owner(): return lax.all_to_all(cut, axis, 0, 0, tiled=True)]
    ppermute x19, waiting for transfers between devices: 18.1 us -> 55 us  [flip(): return lax.ppermute(values, axis, [(at, at ^ bit) for at in range(count)])]
    ppermute x6 -> x0, starting transfers between devices: 32.7 us -> none  [the longest x3 28.1 us: send(): lax.ppermute(to_right, axis, [(at, at + 1) for at in range(step)])]
    all_gather x1 -> x0, blocking collectives: 19.8 us -> none  [shards(): cot_one = lax.all_gather(first_rows, 'mp', axis=0, tiled=False)]
    all_gather x1, waiting for transfers between devices: 56.1 us -> 38.5 us  [shards(): normed = lax.all_gather(normed_part, 'mp', axis=0, tiled=False)]
    all_gather x0 -> x1, waiting for transfers between devices: none -> 14.8 us  [shards(): cot_one = lax.all_gather(first_cot, 'mp', axis=0, tiled=False)]
    convert_element_type x4 -> x1, other arithmetic: 10.9 us -> 1.7 us  [shards(): (cotangent.astype(jnp.float32) + d_input.T).astype(jnp.bfloat16)]
    unnamed x59 -> x37, local copies, waits for them, and re-layouts: 16.2 us -> 7.07 us
  transfers between devices with their start and end apart: 32 -> 29, of which waited for: 9 -> 12; matrix products, arithmetic and copies ran while one was open for 10% -> 4% of each run, Pallas kernels for 17% -> 25%
where the time goes in v3:
time: 347 us; the launch traced here: 346 us
  waiting for transfers between devices  187 us (54%)
  Pallas kernels  86.1 us (25%)
  starting transfers between devices  34.8 us (10%)
  between operations  14.2 us (4%)
  local copies, waits for them, and re-layouts  9.82 us (3%)
  other arithmetic  9.32 us (3%)
  matrix products  5.06 us (1%)
    ppermute x19, waiting for transfers between devices, flip(): return lax.ppermute(values, axis, [(at, at ^ bit) for at in range(count)])  55 us
    all_to_all x3, waiting for transfers between devices, columns_to_owner(): return lax.all_to_all(cut, axis, 0, 0, tiled=True)  44.8 us
    all_gather x1, waiting for transfers between devices, shards(): normed = lax.all_gather(normed_part, 'mp', axis=0, tiled=False)  38.5 us
    pallas_call x3, Pallas kernels, project(): pl.pallas_call(functools.partial(project_kernel, steps, width), grid=(ste...  30 us
    pallas_call x2, Pallas kernels, expand(): pl.pallas_call(functools.partial(expand_kernel, kinds, width), grid=(part...  24.8 us
    pallas_call x2, Pallas kernels, weight_grads(): pl.pallas_call(functools.partial(weight_kernel, keys, scale), grid=(4,),...  23.4 us
    ppermute x1, waiting for transfers between devices, gather_xor(): far = lax.ppermute(onward, axis, pairs)  23.3 us
    ppermute x19, starting transfers between devices, flip(): return lax.ppermute(values, axis, [(at, at ^ bit) for at in range(count)])  16.9 us
  transfers between devices with their start and end apart: 29, of which 12 were waited for; matrix products, arithmetic and copies ran while one was open for 4% of the time, Pallas kernels for 25%

profile of v3, /device:TPU:0, one launch (start us, length us, event | category | flops | bytes accessed | tf_op | source)
XLA Modules:
  0.0 346.2 jit_solution(11681966134544448012)
XLA Ops:
  8.8 2.9 convolution_convert_fusion
  12.2 5.1 %collective-permute-start.2 = (f32[2,256]{1,0:T(2,128)S(1)}, f32[2,256]{1,0:T(2,128)S(1)}, u32[]{:S(2)}, u32[]{:S(2)}) collective-permute-start(f32[2,256]{1,0:T(2,128)S(1)} %pad_maximum_fusion.1), channel_id=1, source_target_pairs={{0,3},{1,2},{2,1},{3,0},{4,7},{5,6},{6,5},{7,4},{8,11},{9,10},{10,... | collective-permute-start | bytes 6152 | tf_op jit(solution)/shard_map/ppermute | solution.py:295
  18.0 4.0 %all-to-all-start = ((bf16[8,64,1536]{2,1,0:T(8,128)(2,1)}), bf16[8,64,1536]{2,1,0:T(8,128)(2,1)S(1)}, u32[]{:S(2)}, u32[]{:S(2)}) async-start(bf16[8,64,1536]{2,1,0:T(8,128)(2,1)} %bitcast), calls=%async_computation | async-start | bytes 3145728 | tf_op jit(solution)/shard_map/all_to_all | solution.py:357
  30.8 11.8 %collective-permute-done.9 = f32[3,64]{1,0:T(4,128)S(1)} collective-permute-done((f32[3,64]{1,0:T(4,128)S(1)}, f32[3,64]{1,0:T(4,128)S(1)}, u32[]{:S(2)}, u32[]{:S(2)}) %collective-permute-start.9) | collective-permute-done | bytes 800 | tf_op jit(solution)/shard_map/ppermute | solution.py:295
  49.0 14.8 %all-gather.7.cloned.1.call-done = bf16[6144,128]{1,0:T(8,128)(2,1)} async-done(((bf16[1536,128]{1,0:T(8,128)(2,1)}), bf16[6144,128]{1,0:T(8,128)(2,1)}) %all-gather.7.cloned.1.call-update) | async-done | bytes 1572880 | tf_op jit(solution)/shard_map/all_gather | solution.py:349
  63.8 3.8 %all-to-all-start.1 = ((bf16[8,768,128]{2,1,0:T(8,128)(2,1)}), bf16[8,768,128]{2,1,0:T(8,128)(2,1)S(1)}, u32[]{:S(2)}, u32[]{:S(2)}) async-start(bf16[8,768,128]{2,1,0:T(8,128)(2,1)} %bitcast.55), calls=%async_computation.1 | async-start | bytes 3145728 | tf_op jit(solution)/shard_map/all_to_all | solution.py:334
  67.7 5.6 %shard_map.121.d_one_ref = bf16[128,768]{1,0:T(8,128)(2,1)S(1)} custom-call(bf16[4,1536,128]{2,1,0:T(8,128)(2,1)S(1)} %bitcast.56, bf16[1,6144,768]{2,1,0:T(8,128)(2,1)} %bitcast.62), custom_call_target="tpu_custom_call" | custom-call | flops 1207959552 | bytes 11010048 | tf_op jit(solution)/shard_map/pallas_call | solution.py:68
  73.4 15.3 %all-to-all-done.1.one_ref = bf16[8,768,128]{2,1,0:T(8,128)(2,1)S(1)} async-done(((bf16[8,768,128]{2,1,0:T(8,128)(2,1)}), bf16[8,768,128]{2,1,0:T(8,128)(2,1)S(1)}, u32[]{:S(2)}, u32[]{:S(2)}) %all-to-all-start.1) | async-done | bytes 1572896 | tf_op jit(solution)/shard_map/all_to_all | solution.py:334
  89.8 38.5 %all-gather.9.cloned.1.call-done = bf16[6144,256]{1,0:T(8,128)(2,1)} async-done(((bf16[1536,256]{1,0:T(8,128)(2,1)}), bf16[6144,256]{1,0:T(8,128)(2,1)}) %all-gather.9.cloned.1.call-update) | async-done | bytes 3145744 | tf_op jit(solution)/shard_map/all_gather | solution.py:392
  128.6 18.4 %shard_map.122.proj_ref = f32[256,2304]{1,0:T(8,128)S(1)} custom-call(bf16[4,1536,256]{2,1,0:T(8,128)(2,1)} %bitcast.6.x_ref.refs_1_, bf16[3,6144,768]{2,1,0:T(8,128)(2,1)} %bitcast.60), custom_call_target="tpu_custom_call" | custom-call | flops 7247757312 | bytes 31457280 | tf_op jit(solution)/shard_map/pallas_call | solution.py:68
  148.7 7.3 %shard_map.124 = bf16[4,1536,256]{2,1,0:T(8,128)(2,1)} custom-call(bf16[256,768]{1,0:T(8,128)(2,1)S(1)} %shard_map.123.x_ref, bf16[1,6144,768]{2,1,0:T(8,128)(2,1)} %bitcast.63), custom_call_target="tpu_custom_call" | custom-call | flops 2415919104 | bytes 12582912 | tf_op jit(solution)/shard_map/pallas_call | solution.py:117
  155.9 10.3 %all-gather.11.cloned.1.call-done = bf16[6144,128]{1,0:T(8,128)(2,1)} async-done(((bf16[1536,128]{1,0:T(8,128)(2,1)}), bf16[6144,128]{1,0:T(8,128)(2,1)}) %all-gather.11.cloned.1.call-update) | async-done | bytes 1572880 | tf_op jit(solution)/shard_map/all_gather | solution.py:398
  166.3 4.5 %all-to-all-start.2 = ((bf16[8,768,256]{2,1,0:T(8,128)(2,1)}), bf16[8,768,256]{2,1,0:T(8,128)(2,1)}, u32[]{:S(2)}, u32[]{:S(2)}) async-start(bf16[8,768,256]{2,1,0:T(8,128)(2,1)} %bitcast.15), calls=%async_computation.3 | async-start | bytes 6291456 | tf_op jit(solution)/shard_map/all_to_all | solution.py:334
  173.2 5.9 %shard_map.125.d_two_ref = bf16[128,768]{1,0:T(8,128)(2,1)S(1)} custom-call(bf16[4,1536,128]{2,1,0:T(8,128)(2,1)} %bitcast.12.x_ref, bf16[1,6144,768]{2,1,0:T(8,128)(2,1)} %bitcast.64), custom_call_target="tpu_custom_call" | custom-call | flops 1207959552 | bytes 11010048 | tf_op jit(solution)/shard_map/pallas_call | solution.py:68
  179.1 29.5 %all-to-all-done.2.normed_ref = bf16[8,768,256]{2,1,0:T(8,128)(2,1)} async-done(((bf16[8,768,256]{2,1,0:T(8,128)(2,1)}), bf16[8,768,256]{2,1,0:T(8,128)(2,1)}, u32[]{:S(2)}, u32[]{:S(2)}) %all-to-all-start.2) | async-done | bytes 3145760 | tf_op jit(solution)/shard_map/all_to_all | solution.py:334
  208.7 5.4 %shard_map.126.x_ref.refs_0_ = bf16[256,3072]{1,0:T(8,128)(2,1)} custom-call(f32[256,2304]{1,0:T(8,128)S(1)} %shard_map.122.proj_ref, s32[256,1]{1,0:T(8,128)S(1)} %copy.22.row_ref, s32[1,256]{1,0:T(1,128)S(1)} %bitcast.59, f32[2,128]{1,0:T(2,128)S(1)} %copy-done.6, bf16[128,768]{1,0:T(8,128)(2,1)S(1)} %shard_map.121.d_one_ref, ...), custom_call_target="tpu_custom_call" | custom-call | flops 805306368 | bytes 4718592 | tf_op jit(solution)/shard_map/pallas_call | solution.py:209
  214.6 17.5 %shard_map.127 = (bf16[4,1536,256]{2,1,0:T(8,128)(2,1)}, f32[2,256]{1,0:T(2,128)S(1)}) custom-call(bf16[256,3072]{1,0:T(8,128)(2,1)} %shard_map.126.x_ref.refs_0_, bf16[3,6144,768]{2,1,0:T(8,128)(2,1)} %bitcast.61, f32[6144,1]{1,0:T(8,128)} %copy.25.refs_0_, bf16[4,1536,256]{2,1,0:T(8,128)(2,1)} %bitcast.6.x_ref.refs_1_), custom_call_target="tpu_custom_call" | custom-call | flops 7247757312 | bytes 31457280 | tf_op jit(solution)/shard_map/pallas_call | solution.py:117
  232.9 18.3 %collective-permute-done.11.refs_4_ = bf16[256,3072]{1,0:T(8,128)(2,1)} collective-permute-done((bf16[256,3072]{1,0:T(8,128)(2,1)}, bf16[256,3072]{1,0:T(8,128)(2,1)}, u32[]{:S(2)}, u32[]{:S(2)}) %collective-permute-start.11) | collective-permute-done | bytes 1572896 | tf_op jit(solution)/shard_map/ppermute | solution.py:295
  251.2 17.8 %collective-permute-done.12.refs_2_ = bf16[256,3072]{1,0:T(8,128)(2,1)} collective-permute-done((bf16[256,3072]{1,0:T(8,128)(2,1)}, bf16[256,3072]{1,0:T(8,128)(2,1)}, u32[]{:S(2)}, u32[]{:S(2)}) %collective-permute-start.12) | collective-permute-done | bytes 1572896 | tf_op jit(solution)/shard_map/ppermute | solution.py:295
  273.7 3.8 %all-to-all-start.3 = ((bf16[8,768,128]{2,1,0:T(8,128)(2,1)}), bf16[8,768,128]{2,1,0:T(8,128)(2,1)S(1)}, u32[]{:S(2)}, u32[]{:S(2)}) async-start(bf16[8,768,128]{2,1,0:T(8,128)(2,1)} %bitcast.18), calls=%async_computation.5 | async-start | bytes 3145728 | tf_op jit(solution)/shard_map/all_to_all | solution.py:334
  277.5 23.3 %collective-permute-done.13.refs_0_ = bf16[256,3072]{1,0:T(8,128)(2,1)} collective-permute-done((bf16[256,3072]{1,0:T(8,128)(2,1)}, bf16[256,3072]{1,0:T(8,128)(2,1)}, u32[]{:S(2)}, u32[]{:S(2)}) %collective-permute-start.13) | collective-permute-done | bytes 1572896 | tf_op jit(solution)/shard_map/ppermute | solution.py:323
  302.8 3.4 collective-permute-done.19
  309.8 13.2 %shard_map.128.refs_2_ = f32[4,768,768]{2,1,0:T(8,128)} custom-call(bf16[8,768,256]{2,1,0:T(8,128)(2,1)} %all-to-all-done.2.normed_ref, bf16[8,768,128]{2,1,0:T(8,128)(2,1)S(1)} %copy-done.1, bf16[8,768,128]{2,1,0:T(8,128)(2,1)S(1)} %all-to-all-done.3.two_ref, bf16[256,3072]{1,0:T(8,128)(2,1)} %shard_map.126.x_ref.refs_0_, bf16[256,3072]{1,0:T(8,128)(2,1)} %copy-done.12, ...), custom_call_target="tpu_custom_call" | custom-call | flops 7247757312 | bytes 15728640 | tf_op jit(solution)/shard_map/pallas_call | solution.py:265
  323.0 10.2 %shard_map.129 = (bf16[3,768,768]{2,1,0:T(8,128)(2,1)}, bf16[768,768]{1,0:T(8,128)(2,1)}) custom-call(bf16[8,768,256]{2,1,0:T(8,128)(2,1)} %all-to-all-done.2.normed_ref, bf16[8,768,128]{2,1,0:T(8,128)(2,1)S(1)} %copy-done.1, bf16[8,768,128]{2,1,0:T(8,128)(2,1)S(1)} %all-to-all-done.3.two_ref, bf16[256,3072]{1,0:T(8,128)(2,1)} %collective-permute-done.13.refs_0_, ...), custom_call_target="tpu_custom_call" | custom-call | flops 2415919104 | bytes 9437184 | tf_op jit(solution)/shard_map/pallas_call | solution.py:265
  (120 shorter events, 41.4 us)
Async XLA Ops:
  12.2 11.8 %collective-permute-start.2 = (f32[2,256]{1,0:T(2,128)S(1)}, f32[2,256]{1,0:T(2,128)S(1)}, u32[]{:S(2)}, u32[]{:S(2)}) collective-permute-start(f32[2,256]{1,0:T(2,128)S(1)} %pad_maximum_fusion.1), channel_id=1, source_target_pairs={{0,3},{1,2},{2,1},{3,0},{4,7},{5,6},{6,5},{7,4},{8,11},{9,10},{10,... | collective-permute-start | bytes 6152 | tf_op jit(solution)/shard_map/ppermute | solution.py:295
  17.3 6.7 %collective-permute-start.1 = (f32[2,256]{1,0:T(2,128)S(1)}, f32[2,256]{1,0:T(2,128)S(1)}, u32[]{:S(2)}, u32[]{:S(2)}) collective-permute-start(f32[2,256]{1,0:T(2,128)S(1)} %pad_maximum_fusion.1), channel_id=1, source_target_pairs={{0,2},{1,3},{2,0},{3,1},{4,6},{5,7},{6,4},{7,5},{8,10},{9,11},{10,... | collective-permute-start | bytes 6152 | tf_op jit(solution)/shard_map/ppermute | solution.py:295
  17.3 6.7 %collective-permute-start = (f32[2,256]{1,0:T(2,128)S(1)}, f32[2,256]{1,0:T(2,128)S(1)}, u32[]{:S(2)}, u32[]{:S(2)}) collective-permute-start(f32[2,256]{1,0:T(2,128)S(1)} %pad_maximum_fusion.1), channel_id=1, source_target_pairs={{0,1},{1,0},{2,3},{3,2},{4,5},{5,4},{6,7},{7,6},{8,9},{9,8},{10,11... | collective-permute-start | bytes 6152 | tf_op jit(solution)/shard_map/ppermute | solution.py:295
  18.0 28.8 %all-to-all-start = ((bf16[8,64,1536]{2,1,0:T(8,128)(2,1)}), bf16[8,64,1536]{2,1,0:T(8,128)(2,1)S(1)}, u32[]{:S(2)}, u32[]{:S(2)}) async-start(bf16[8,64,1536]{2,1,0:T(8,128)(2,1)} %bitcast), calls=%async_computation | async-start | bytes 3145728 | tf_op jit(solution)/shard_map/all_to_all | solution.py:357
  22.0 41.8 %all-gather.7.cloned.1.call-start = ((), (), s32[]{:S(2)}) async-start(), calls=%async_computation.8 | async-start | bytes 1966080 | tf_op jit(solution)/shard_map/all_gather | solution.py:349
  23.7 104.6 %all-gather.9.cloned.1.call-start = ((), (), s32[]{:S(2)}) async-start(), calls=%async_computation.9 | async-start | bytes 3932160 | tf_op jit(solution)/shard_map/all_gather | solution.py:392
  24.6 18.0 %collective-permute-start.9 = (f32[3,64]{1,0:T(4,128)S(1)}, f32[3,64]{1,0:T(4,128)S(1)}, u32[]{:S(2)}, u32[]{:S(2)}) collective-permute-start(f32[3,64]{1,0:T(4,128)S(1)} %bitcast.82), channel_id=1, source_target_pairs={{0,28},{4,24},{8,20},{12,16},{16,12},{20,8},{24,4},{28,0},{1,29},{... | collective-permute-start | bytes 2312 | tf_op jit(solution)/shard_map/ppermute | solution.py:295
  27.2 15.9 %collective-permute-start.8 = (f32[3,64]{1,0:T(4,128)S(1)}, f32[3,64]{1,0:T(4,128)S(1)}, u32[]{:S(2)}, u32[]{:S(2)}) collective-permute-start(f32[3,64]{1,0:T(4,128)S(1)} %bitcast.81), channel_id=1, source_target_pairs={{0,24},{4,28},{8,16},{12,20},{16,8},{20,12},{24,0},{28,4},{1,25},{... | collective-permute-start | bytes 2312 | tf_op jit(solution)/shard_map/ppermute | solution.py:295
  27.6 16.1 %collective-permute-start.7 = (f32[3,64]{1,0:T(4,128)S(1)}, f32[3,64]{1,0:T(4,128)S(1)}, u32[]{:S(2)}, u32[]{:S(2)}) collective-permute-start(f32[3,64]{1,0:T(4,128)S(1)} %bitcast.76), channel_id=1, source_target_pairs={{0,20},{4,16},{8,28},{12,24},{16,4},{20,0},{24,12},{28,8},{1,21},{... | collective-permute-start | bytes 2312 | tf_op jit(solution)/shard_map/ppermute | solution.py:295
  29.0 14.8 %collective-permute-start.6 = (f32[3,64]{1,0:T(4,128)S(1)}, f32[3,64]{1,0:T(4,128)S(1)}, u32[]{:S(2)}, u32[]{:S(2)}) collective-permute-start(f32[3,64]{1,0:T(4,128)S(1)} %bitcast.77), channel_id=1, source_target_pairs={{0,16},{4,20},{8,24},{12,28},{16,0},{20,4},{24,8},{28,12},{1,17},{... | collective-permute-start | bytes 2312 | tf_op jit(solution)/shard_map/ppermute | solution.py:295
  29.3 14.4 %collective-permute-start.5 = (f32[3,64]{1,0:T(4,128)S(1)}, f32[3,64]{1,0:T(4,128)S(1)}, u32[]{:S(2)}, u32[]{:S(2)}) collective-permute-start(f32[3,64]{1,0:T(4,128)S(1)} %bitcast.78), channel_id=1, source_target_pairs={{0,12},{4,8},{8,4},{12,0},{16,28},{20,24},{24,20},{28,16},{1,13},{... | collective-permute-start | bytes 2312 | tf_op jit(solution)/shard_map/ppermute | solution.py:295
  63.8 24.8 %all-to-all-start.1 = ((bf16[8,768,128]{2,1,0:T(8,128)(2,1)}), bf16[8,768,128]{2,1,0:T(8,128)(2,1)S(1)}, u32[]{:S(2)}, u32[]{:S(2)}) async-start(bf16[8,768,128]{2,1,0:T(8,128)(2,1)} %bitcast.55), calls=%async_computation.1 | async-start | bytes 3145728 | tf_op jit(solution)/shard_map/all_to_all | solution.py:334
  67.6 98.6 %all-gather.11.cloned.1.call-start = ((), (), s32[]{:S(2)}) async-start(), calls=%async_computation.10 | async-start | bytes 1966080 | tf_op jit(solution)/shard_map/all_gather | solution.py:398
  128.4 204.9 %reduce-scatter.3.cloned.1.call-start = ((), (), s32[]{:S(2)}) async-start(), calls=%async_computation.6 | async-start | bytes 3932160 | tf_op jit(solution)/shard_map/reduce_scatter | solution.py:405
  166.3 42.4 %all-to-all-start.2 = ((bf16[8,768,256]{2,1,0:T(8,128)(2,1)}), bf16[8,768,256]{2,1,0:T(8,128)(2,1)}, u32[]{:S(2)}, u32[]{:S(2)}) async-start(bf16[8,768,256]{2,1,0:T(8,128)(2,1)} %bitcast.15), calls=%async_computation.3 | async-start | bytes 6291456 | tf_op jit(solution)/shard_map/all_to_all | solution.py:334
  170.8 165.5 %reduce-scatter.5.cloned.1.call-start = ((), (), s32[]{:S(2)}) async-start(), calls=%async_computation.7 | async-start | bytes 3932160 | tf_op jit(solution)/shard_map/reduce_scatter | solution.py:412
  214.0 18.9 %collective-permute-start.10 = (bf16[256,3072]{1,0:T(8,128)(2,1)}, bf16[256,3072]{1,0:T(8,128)(2,1)S(1)}, u32[]{:S(2)}, u32[]{:S(2)}) collective-permute-start(bf16[256,3072]{1,0:T(8,128)(2,1)} %shard_map.126.x_ref.refs_0_), channel_id=1, source_target_pairs={{0,4},{4,0},{8,12},{12,8},{16,20},{20,16},{24,28},{28,24},{1,5},{5... | collective-permute-start | bytes 4718600 | tf_op jit(solution)/shard_map/ppermute | solution.py:295
  214.0 37.1 %collective-permute-start.11 = (bf16[256,3072]{1,0:T(8,128)(2,1)}, bf16[256,3072]{1,0:T(8,128)(2,1)}, u32[]{:S(2)}, u32[]{:S(2)}) collective-permute-start(bf16[256,3072]{1,0:T(8,128)(2,1)} %shard_map.126.x_ref.refs_0_), channel_id=1, source_target_pairs={{0,16},{4,20},{8,24},{12,28},{16,0},{20,4},{24,8},{28,12},{1,17},{... | collective-permute-start | bytes 4718600 | tf_op jit(solution)/shard_map/ppermute | solution.py:295
  232.1 36.8 %collective-permute-start.12 = (bf16[256,3072]{1,0:T(8,128)(2,1)}, bf16[256,3072]{1,0:T(8,128)(2,1)}, u32[]{:S(2)}, u32[]{:S(2)}) collective-permute-start(bf16[256,3072]{1,0:T(8,128)(2,1)} %shard_map.126.x_ref.refs_0_), channel_id=1, source_target_pairs={{0,8},{4,12},{8,0},{12,4},{16,24},{20,28},{24,16},{28,20},{1,9},{5... | collective-permute-start | bytes 4718600 | tf_op jit(solution)/shard_map/ppermute | solution.py:295
  271.7 29.2 %collective-permute-start.13 = (bf16[256,3072]{1,0:T(8,128)(2,1)}, bf16[256,3072]{1,0:T(8,128)(2,1)}, u32[]{:S(2)}, u32[]{:S(2)}) collective-permute-start(bf16[256,3072]{1,0:T(8,128)(2,1)} %broadcast_select_fusion), channel_id=1, source_target_pairs={{0,16},{4,12},{8,24},{12,4},{16,0},{20,28},{24,8},{28,20},{1,17},{... | collective-permute-start | bytes 4718600 | tf_op jit(solution)/shard_map/ppermute | solution.py:323
  273.1 36.7 %collective-permute-start.15 = (bf16[256,3072]{1,0:T(8,128)(2,1)}, bf16[256,3072]{1,0:T(8,128)(2,1)}, u32[]{:S(2)}, u32[]{:S(2)}) collective-permute-start(bf16[256,3072]{1,0:T(8,128)(2,1)} %collective-permute-done.12.refs_2_), channel_id=1, source_target_pairs={{0,4},{4,0},{8,12},{12,8},{16,20},{20,16},{24,28},{28,24},{1,5},{5... | collective-permute-start | bytes 4718600 | tf_op jit(solution)/shard_map/ppermute | solution.py:295
  273.1 36.7 %collective-permute-start.16 = (bf16[256,3072]{1,0:T(8,128)(2,1)}, bf16[256,3072]{1,0:T(8,128)(2,1)}, u32[]{:S(2)}, u32[]{:S(2)}) collective-permute-start(bf16[256,3072]{1,0:T(8,128)(2,1)} %collective-permute-done.11.refs_4_), channel_id=1, source_target_pairs={{0,4},{4,0},{8,12},{12,8},{16,20},{20,16},{24,28},{28,24},{1,5},{5... | collective-permute-start | bytes 4718600 | tf_op jit(solution)/shard_map/ppermute | solution.py:295
  273.7 36.2 %all-to-all-start.3 = ((bf16[8,768,128]{2,1,0:T(8,128)(2,1)}), bf16[8,768,128]{2,1,0:T(8,128)(2,1)S(1)}, u32[]{:S(2)}, u32[]{:S(2)}) async-start(bf16[8,768,128]{2,1,0:T(8,128)(2,1)} %bitcast.18), calls=%async_computation.5 | async-start | bytes 3145728 | tf_op jit(solution)/shard_map/all_to_all | solution.py:334
  300.8 22.2 %collective-permute-start.14 = (bf16[256,3072]{1,0:T(8,128)(2,1)}, bf16[256,3072]{1,0:T(8,128)(2,1)}, u32[]{:S(2)}, u32[]{:S(2)}) collective-permute-start(bf16[256,3072]{1,0:T(8,128)(2,1)} %collective-permute-done.13.refs_0_), channel_id=1, source_target_pairs={{0,4},{4,0},{8,12},{12,8},{16,20},{20,16},{24,28},{28,24},{1,5},{5... | collective-permute-start | bytes 4718600 | tf_op jit(solution)/shard_map/ppermute | solution.py:295
  (18 other events, 218.6 us)
Sparse Core Ops, SparseCore 0:
  25.0 38.7 all-gather.6
  65.9 62.3 all-gather.8
  130.5 35.7 all-gather.10
  168.4 59.1 reduce-scatter.2
  232.2 58.3 reduce-scatter.4

commit v4 on v3

--- a/solution.py
+++ b/solution.py
@@ -10,6 +10,7 @@
 
 DH = 128
 VMEM_BYTES = 48 * 1024 * 1024
+STREAMS = 4
 
 
 def dot_f32(left, right, left_dims, right_dims):
@@ -39,7 +40,8 @@
     )(x)
 
 
-def project_kernel(steps, width, x_ref, w_ref, out_ref, total, block):
+def project_kernel(steps, width, x_ref, *refs):
+    w_refs, (out_ref, total, block) = refs[:STREAMS], refs[STREAMS:]
     at, t = pl.program_id(0), pl.program_id(1)
     columns = pl.ds(pl.multiple_of(t * width, width), width)
 
@@ -47,7 +49,12 @@
     def _():
         block[...] = x_ref[0].T
 
-    term = jnp.dot(block[...], w_ref[0], preferred_element_type=jnp.float32)
+    piece = w_refs[0].shape[1]
+    term = None
+    for order, w_ref in enumerate(w_refs):
+        left = block[:, order * piece : (order + 1) * piece]
+        more = jnp.dot(left, w_ref[0], preferred_element_type=jnp.float32)
+        term = more if term is None else term + more
 
     @pl.when(at == 0)
     def _():
@@ -70,7 +77,13 @@
         grid=(steps, kinds),
         in_specs=[
             pl.BlockSpec((1, part, rows), lambda at, t: (at, 0, 0)),
-            pl.BlockSpec((1, part, width), lambda at, t: (t, at, 0)),
+        ]
+        + [
+            pl.BlockSpec(
+                (1, part // STREAMS, width),
+                lambda at, t, order=order: (t, at * STREAMS + order, 0),
+            )
+            for order in range(STREAMS)
         ],
         out_specs=pl.BlockSpec((rows, kinds * width), lambda at, t: (0, 0)),
         out_shape=jax.ShapeDtypeStruct((rows, kinds * width), dtype),
@@ -84,14 +97,18 @@
             bytes_accessed=2 * kinds * depth * width + 2 * rows * depth,
             transcendentals=0,
         ),
-    )(x, w)
-
-
-def expand_kernel(kinds, width, x_ref, w_ref, *refs):
-    total = None
-    for t in range(kinds):
-        term = dot_f32(w_ref[t], x_ref[:, t * width : (t + 1) * width], (1,), (1,))
-        total = term if total is None else total + term
+    )(x, *[w] * STREAMS)
+
+
+def expand_kernel(kinds, width, x_ref, *refs):
+    w_refs, refs = refs[:STREAMS], refs[STREAMS:]
+    pieces = []
+    for w_ref in w_refs:
+        total = None
+        for t in range(kinds):
+            term = dot_f32(w_ref[t], x_ref[:, t * width : (t + 1) * width], (1,), (1,))
+            total = term if total is None else total + term
+        pieces.append(total)
     if len(refs) == 1:
         (out_ref,) = refs
     else:
@@ -101,9 +118,13 @@
         def _():
             sums_ref[...] = jnp.zeros_like(sums_ref)
 
-        sums_ref[0:1, :] += jnp.sum(total * gain_ref[...], 0, keepdims=True)
-        sums_ref[1:2, :] += jnp.sum(total * normed_ref[0].astype(jnp.float32), 0, keepdims=True)
-    out_ref[0] = total.astype(jnp.bfloat16)
+    for order, total in enumerate(pieces):
+        here = slice(order * total.shape[0], (order + 1) * total.shape[0])
+        out_ref[0, here, :] = total.astype(jnp.bfloat16)
+        if len(refs) > 1:
+            by_normed = total * normed_ref[0, here, :].astype(jnp.float32)
+            sums_ref[0:1, :] += jnp.sum(total * gain_ref[here, :], 0, keepdims=True)
+            sums_ref[1:2, :] += jnp.sum(by_normed, 0, keepdims=True)
 
 
 def expand(x, w, parts, cuts, gain=None, normed=None):
@@ -119,7 +140,13 @@
         grid=(parts, cuts),
         in_specs=[
             pl.BlockSpec((rows, kinds * width), lambda at, cut: (0, 0)),
-            pl.BlockSpec((kinds, piece, width), lambda at, cut: (0, at * cuts + cut, 0)),
+        ]
+        + [
+            pl.BlockSpec(
+                (kinds, piece // STREAMS, width),
+                lambda at, cut, order=order: (0, (at * cuts + cut) * STREAMS + order, 0),
+            )
+            for order in range(STREAMS)
         ]
         + ([pl.BlockSpec((piece, 1), lambda at, cut: (at * cuts + cut, 0)), turned] if more else []),
         out_specs=[turned, pl.BlockSpec((2, rows), lambda at, cut: (0, 0))] if more else turned,
@@ -132,7 +159,7 @@
             bytes_accessed=2 * kinds * depth * width + 2 * rows * depth,
             transcendentals=0,
         ),
-    )(x, w, *more)
+    )(x, *[w] * STREAMS, *more)
 
 
 def unit_heads(raw):
@@ -186,8 +213,6 @@
         at = head * DH
         weights_bf = weights.astype(jnp.bfloat16)
         d_out = jnp.concatenate([d_one_ref[:, at : at + DH], d_two_ref[:, at : at + DH]], 0)
-        mixed = dot_f32(weights_bf, values, (1,), (0,))
-        out_ref[:, 3 * width + at : 3 * width + at + DH] = mixed.astype(jnp.bfloat16)
         d_values = dot_f32(weights_bf, d_out, (0,), (0,))
         out_ref[:, 2 * width + at : 2 * width + at + DH] = d_values.astype(jnp.bfloat16)
         d_weights = dot_f32(d_out, values, (1,), (1,)).astype(jnp.bfloat16).astype(jnp.float32)
@@ -218,76 +243,49 @@
     )(projected, segment.reshape(rows, 1), segment.reshape(1, rows), qk_gain, *extra)
 
 
-def weight_kernel(keys, scale, normed_ref, one_ref, two_ref, *refs):
-    b_refs, refs = refs[: len(keys)], refs[len(keys) :]
-    me, t = lax.axis_index("dp"), pl.program_id(0)
-
-    def product(load, total):
-        for order, key in enumerate(keys):
-            term = jnp.dot(load(me ^ key), b_refs[order][...], preferred_element_type=jnp.float32)
-            if scale is None and order == 0:
-                total[...] = term
-            else:
-                total[...] += term
-
-    def normed(at):
-        return normed_ref[at]
-
-    def cot(at):
-        return jnp.concatenate([one_ref[at], two_ref[at]], 1)
-
-    if scale is None:
-        total = refs[0].at[0]
-    else:
-        before_ref, qkv_ref, out_ref, total = refs
-        total[...] = before_ref[0]
-
-    @pl.when(t < 3)
-    def _():
-        product(normed, total)
-        if scale is not None:
-            qkv_ref[0] = (total[...] * scale).astype(jnp.bfloat16)
-
-    @pl.when(t == 3)
-    def _():
-        product(cot, total)
-        if scale is not None:
-            out_ref[...] = (total[...] * scale).astype(jnp.bfloat16)
-
-
-def weight_grads(normed_cols, cot_one, cot_two, gathered, keys, before, scale):
-    count, depth, rows = normed_cols.shape
-    width = gathered[0].shape[1] // 4
-    whole = pl.BlockSpec((count, depth, rows), lambda t: (0, 0, 0))
-    half = pl.BlockSpec((count, depth, rows // 2), lambda t: (0, 0, 0))
-    sums = pl.BlockSpec((1, depth, width), lambda t: (t, 0, 0))
-    sums_shape = jax.ShapeDtypeStruct((4, depth, width), jnp.float32)
+def weight_kernel(keys, cuts, scale, more, *refs):
+    a_refs, b_refs, refs = refs[:cuts], refs[cuts : cuts + len(keys)], refs[cuts + len(keys) :]
+    me = lax.axis_index("dp")
+    before_ref = refs[0] if more else None
+    out_ref = refs[1] if more else refs[0]
+    total = out_ref.at[0] if scale is None else refs[-1]
+    for order, key in enumerate(keys):
+        left = [ref[me ^ key] for ref in a_refs]
+        left = left[0] if cuts == 1 else jnp.concatenate(left, 1)
+        term = jnp.dot(left, b_refs[order][...], preferred_element_type=jnp.float32)
+        if order == 0:
+            total[...] = before_ref[0] + term if more else term
+        else:
+            total[...] += term
+    if scale is not None:
+        out_ref[0] = (total[...] * scale).astype(jnp.bfloat16)
+
+
+def weight_grad(columns, gathered, kinds, before, scale):
+    count, depth, _ = columns[0].shape
+    keys = sorted(gathered)
+    rows, wide = gathered[keys[0]].shape
+    width = wide // kinds
+    block = pl.BlockSpec((1, depth, width), lambda t: (t, 0, 0))
+    more = [] if before is None else [before]
     return pl.pallas_call(
-        functools.partial(weight_kernel, keys, scale),
-        grid=(4,),
-        in_specs=[whole, half, half]
+        functools.partial(weight_kernel, keys, len(columns), scale, bool(more)),
+        grid=(kinds,),
+        in_specs=[pl.BlockSpec(part.shape, lambda t: (0, 0, 0)) for part in columns]
         + [pl.BlockSpec((rows, width), lambda t: (0, t))] * len(keys)
-        + ([] if before is None else [sums]),
-        out_specs=sums
-        if before is None
-        else [
-            pl.BlockSpec((1, depth, width), lambda t: (jnp.minimum(t, 2), 0, 0)),
-            pl.BlockSpec((depth, width), lambda t: (0, 0)),
-        ],
-        out_shape=sums_shape
-        if before is None
-        else [
-            jax.ShapeDtypeStruct((3, depth, width), jnp.bfloat16),
-            jax.ShapeDtypeStruct((depth, width), jnp.bfloat16),
-        ],
-        scratch_shapes=[] if before is None else [pltpu.VMEM((depth, width), jnp.float32)],
+        + [block] * len(more),
+        out_specs=block,
+        out_shape=jax.ShapeDtypeStruct(
+            (kinds, depth, width), jnp.float32 if scale is None else jnp.bfloat16
+        ),
+        scratch_shapes=[] if scale is None else [pltpu.VMEM((depth, width), jnp.float32)],
         compiler_params=params(),
         cost_estimate=pl.CostEstimate(
-            flops=8 * len(keys) * depth * rows * width,
-            bytes_accessed=4 * count * depth * rows + 8 * len(keys) * rows * width,
+            flops=2 * len(keys) * depth * rows * wide,
+            bytes_accessed=2 * count * depth * rows + 2 * len(keys) * rows * wide,
             transcendentals=0,
         ),
-    )(normed_cols, cot_one, cot_two, *gathered, *([] if before is None else [before]))
+    )(*columns, *[gathered[key] for key in keys], *more)
 
 
 def flip(values, axis, bit):
@@ -400,31 +398,31 @@
     normed_cols = columns_to_owner(normed, "dp")
 
     heads_out = attention(forward_kernel, projected, segment, qk_gain, (), 1)
-    attn_part = expand(heads_out, w_out_t, parts, 1)
+    heads_near, heads_far = gather_xor(heads_out, "dp")
+    heads_here, normed_cols = lax.optimization_barrier((heads_out, normed_cols))
+    attn_part = expand(heads_here, w_out_t, parts, 1)
     attn_part, cot_two = lax.optimization_barrier((attn_part, cot_two))
     attn = lax.psum_scatter(attn_part, "mp", scatter_dimension=0, tiled=False)
     output = (packed.astype(jnp.float32) + attn.astype(jnp.float32)).astype(jnp.bfloat16).T
 
     d_heads_two = project(cot_two, w_out_t, jnp.bfloat16)
-    normed_cols, d_heads_two = lax.optimization_barrier((normed_cols, d_heads_two))
-    d_all = attention(backward_kernel, projected, segment, qk_gain, (d_heads_one, d_heads_two), 4)
+    d_heads_two, heads_near = lax.optimization_barrier((d_heads_two, heads_near))
+    d_all = attention(backward_kernel, projected, segment, qk_gain, (d_heads_one, d_heads_two), 3)
     d_part, sums = expand(d_all, w_t, parts, 2, gain_column, normed)
     d_normed = lax.psum_scatter(d_part, "mp", scatter_dimension=0, tiled=False)
     sums = sum(exchange_small(sums, "mp")) / full_width
     scale_grad = 1.0 / math.sqrt(group_rows * groups)
-    columns = (normed_cols, cot_cols_one, columns_to_owner(cot_two, "dp"))
-    sums_near = None
+    cot_cols_two = columns_to_owner(cot_two, "dp")
+    out_grad = weight_grad((cot_cols_one, cot_cols_two), heads_near | heads_far, 1, None, scale_grad)
     near, far = gather_xor(d_all, "dp")
-    for held, scale in ((near, None), (far, scale_grad)):
-        keys = sorted(held)
-        sums_near = weight_grads(*columns, [held[key] for key in keys], keys, sums_near, scale)
-    d_normed, sums_near = lax.optimization_barrier((d_normed, sums_near))
-    qkv_grad, out_grad = sums_near
+    qkv_near = weight_grad((normed_cols,), near, 3, None, None)
+    qkv_grad = weight_grad((normed_cols,), far, 3, qkv_near, scale_grad)
+    d_normed, qkv_grad, out_grad = lax.optimization_barrier((d_normed, qkv_grad, out_grad))
 
     d_unit = d_normed.astype(jnp.float32) * my_gain
     d_input = rstd * (d_unit - sums[0:1] - unit_rows * sums[1:2])
     input_grad = (cotangent.astype(jnp.float32) + d_input.T).astype(jnp.bfloat16)
-    return (output, input_grad, qkv_grad.transpose(1, 0, 2), out_grad)
+    return (output, input_grad, qkv_grad.transpose(1, 0, 2), out_grad[0])
 
 
 def solution(mesh):

time: 347 us -> 350 us (level)
  waiting for transfers between devices: 187 us -> 173 us
  local copies, waits for them, and re-layouts: 9.82 us -> 18.9 us
  starting transfers between devices: 34.8 us -> 41.9 us
    all_to_all x3, waiting for transfers between devices: 44.8 us -> 15.3 us  [columns_to_owner(): return lax.all_to_all(cut, axis, 0, 0, tiled=True)]
    all_gather x1, waiting for transfers between devices: 10.3 us -> 0.01 us  [shards(): cot_two = lax.all_gather(late_cot, 'mp', axis=0, tiled=False)]
    reduce_scatter x1, waiting for transfers between devices: 0.01 us -> 9.97 us  [shards(): attn = lax.psum_scatter(attn_part, 'mp', scatter_dimension=0, tiled=False)]
    ppermute x19 -> x25, waiting for transfers between devices: 55 us -> 64.2 us  [flip(): return lax.ppermute(values, axis, [(at, at ^ bit) for at in range(count)])]
    unnamed x37 -> x87, local copies, waits for them, and re-layouts: 7.07 us -> 16.2 us
    ppermute x1 -> x2, waiting for transfers between devices: 23.3 us -> 28.8 us  [gather_xor(): far = lax.ppermute(onward, axis, pairs)]
    ppermute x19 -> x25, starting transfers between devices: 16.9 us -> 21.9 us  [flip(): return lax.ppermute(values, axis, [(at, at ^ bit) for at in range(count)])]
    pallas_call x2 -> x3, Pallas kernels: 23.4 us -> 23.7 us  [weight_grad(): pl.pallas_call(functools.partial(weight_kernel, keys, len(columns), scale...]
  transfers between devices with their start and end apart: 29 -> 36, of which waited for: 12 -> 14; matrix products, arithmetic and copies ran while one was open for 4% -> 4% of each run, Pallas kernels for 25% -> 18%
where the time goes in v4:
time: 350 us; the launch traced here: 349 us
  waiting for transfers between devices  173 us (49%)
  Pallas kernels  86.9 us (25%)
  starting transfers between devices  41.9 us (12%)
  local copies, waits for them, and re-layouts  18.9 us (5%)
  between operations  14.4 us (4%)
  other arithmetic  9.04 us (3%)
  matrix products  5.06 us (1%)
    ppermute x25, waiting for transfers between devices, flip(): return lax.ppermute(values, axis, [(at, at ^ bit) for at in range(count)])  64.2 us
    all_gather x1, waiting for transfers between devices, shards(): normed = lax.all_gather(normed_part, 'mp', axis=0, tiled=False)  38.5 us
    pallas_call x3, Pallas kernels, project(): pl.pallas_call(functools.partial(project_kernel, steps, width), grid=(ste...  30.2 us
    ppermute x2, waiting for transfers between devices, gather_xor(): far = lax.ppermute(onward, axis, pairs)  28.8 us
    pallas_call x2, Pallas kernels, expand(): pl.pallas_call(functools.partial(expand_kernel, kinds, width), grid=(part...  25.8 us
    pallas_call x3, Pallas kernels, weight_grad(): pl.pallas_call(functools.partial(weight_kernel, keys, len(columns), scale...  23.7 us
    ppermute x25, starting transfers between devices, flip(): return lax.ppermute(values, axis, [(at, at ^ bit) for at in range(count)])  21.9 us
    unnamed x87, local copies, waits for them, and re-layouts  16.2 us
  transfers between devices with their start and end apart: 36, of which 14 were waited for; matrix products, arithmetic and copies ran while one was open for 4% of the time, Pallas kernels for 18%

profile of v4, /device:TPU:0, one launch (start us, length us, event | category | flops | bytes accessed | tf_op | source)
XLA Modules:
  0.0 349.1 jit_solution(2416984525872688200)
XLA Ops:
  8.8 2.9 convolution_convert_fusion
  12.2 3.1 collective-permute-start
  17.9 4.1 %all-to-all-start = ((bf16[8,64,1536]{2,1,0:T(8,128)(2,1)}), bf16[8,64,1536]{2,1,0:T(8,128)(2,1)S(1)}, u32[]{:S(2)}, u32[]{:S(2)}) async-start(bf16[8,64,1536]{2,1,0:T(8,128)(2,1)} %bitcast), calls=%async_computation | async-start | bytes 3145728 | tf_op jit(solution)/shard_map/all_to_all | solution.py:355
  31.2 11.0 %collective-permute-done.4 = f32[3,64]{1,0:T(4,128)S(1)} collective-permute-done((f32[3,64]{1,0:T(4,128)S(1)}, f32[3,64]{1,0:T(4,128)S(1)}, u32[]{:S(2)}, u32[]{:S(2)}) %collective-permute-start.4) | collective-permute-done | bytes 800 | tf_op jit(solution)/shard_map/ppermute | solution.py:293
  43.1 3.0 collective-permute-done.9
  49.0 14.9 %all-gather.7.cloned.1.call-done = bf16[6144,128]{1,0:T(8,128)(2,1)} async-done(((bf16[1536,128]{1,0:T(8,128)(2,1)}), bf16[6144,128]{1,0:T(8,128)(2,1)}) %all-gather.7.cloned.1.call-update) | async-done | bytes 1572880 | tf_op jit(solution)/shard_map/all_gather | solution.py:347
  63.8 3.8 %all-to-all-start.1 = ((bf16[8,768,128]{2,1,0:T(8,128)(2,1)}), bf16[8,768,128]{2,1,0:T(8,128)(2,1)S(1)}, u32[]{:S(2)}, u32[]{:S(2)}) async-start(bf16[8,768,128]{2,1,0:T(8,128)(2,1)} %bitcast.59), calls=%async_computation.1 | async-start | bytes 3145728 | tf_op jit(solution)/shard_map/all_to_all | solution.py:332
  67.6 5.8 %shard_map.121.d_one_ref = bf16[128,768]{1,0:T(8,128)(2,1)S(1)} custom-call(bf16[4,1536,128]{2,1,0:T(8,128)(2,1)S(1)} %bitcast.60, bf16[1,6144,768]{2,1,0:T(8,128)(2,1)} %bitcast.72, bf16[1,6144,768]{2,1,0:T(8,128)(2,1)} %bitcast.73, bf16[1,6144,768]{2,1,0:T(8,128)(2,1)} %bitcast.74, bf16[1,6144,768]{2,1,0:T(8,128)(2,1)} %bitcast.75), custom_call_target="tpu_custom_call" | custom-call | flops 1207959552 | bytes 11010048 | tf_op jit(solution)/shard_map/pallas_call | solution.py:75
  73.4 15.3 %all-to-all-done.1.refs_0_ = bf16[8,768,128]{2,1,0:T(8,128)(2,1)S(1)} async-done(((bf16[8,768,128]{2,1,0:T(8,128)(2,1)}), bf16[8,768,128]{2,1,0:T(8,128)(2,1)S(1)}, u32[]{:S(2)}, u32[]{:S(2)}) %all-to-all-start.1) | async-done | bytes 1572896 | tf_op jit(solution)/shard_map/all_to_all | solution.py:332
  89.8 38.5 %all-gather.9.cloned.1.call-done = bf16[6144,256]{1,0:T(8,128)(2,1)} async-done(((bf16[1536,256]{1,0:T(8,128)(2,1)}), bf16[6144,256]{1,0:T(8,128)(2,1)}) %all-gather.9.cloned.1.call-update) | async-done | bytes 3145744 | tf_op jit(solution)/shard_map/all_gather | solution.py:390
  128.3 4.7 %all-to-all-start.2 = ((bf16[8,768,256]{2,1,0:T(8,128)(2,1)}), bf16[8,768,256]{2,1,0:T(8,128)(2,1)}, u32[]{:S(2)}, u32[]{:S(2)}) async-start(bf16[8,768,256]{2,1,0:T(8,128)(2,1)} %bitcast.56), calls=%async_computation.2 | async-start | bytes 6291456 | tf_op jit(solution)/shard_map/all_to_all | solution.py:332
  134.2 18.4 %shard_map.122.proj_ref = f32[256,2304]{1,0:T(8,128)S(1)} custom-call(bf16[4,1536,256]{2,1,0:T(8,128)(2,1)S(1)} %bitcast.58, bf16[3,6144,768]{2,1,0:T(8,128)(2,1)} %bitcast.64, bf16[3,6144,768]{2,1,0:T(8,128)(2,1)} %bitcast.65, bf16[3,6144,768]{2,1,0:T(8,128)(2,1)} %bitcast.66, bf16[3,6144,768]{2,1,0:T(8,128)(2,1)} %bitcast.67), custom_call_target="tpu_custom_call" | custom-call | flops 7247757312 | bytes 31457280 | tf_op jit(solution)/shard_map/pallas_call | solution.py:75
  159.3 19.1 %collective-permute-done.11.refs_6_ = bf16[256,768]{1,0:T(8,128)(2,1)S(1)} collective-permute-done((bf16[256,768]{1,0:T(8,128)(2,1)S(1)}, bf16[256,768]{1,0:T(8,128)(2,1)S(1)}, u32[]{:S(2)}, u32[]{:S(2)}) %collective-permute-start.11) | collective-permute-done | bytes 393248 | tf_op jit(solution)/shard_map/ppermute | solution.py:293
  181.1 7.2 %shard_map.124 = bf16[4,1536,256]{2,1,0:T(8,128)(2,1)} custom-call(bf16[256,768]{1,0:T(8,128)(2,1)S(1)} %shard_map.123.x_ref.refs_2_, bf16[1,6144,768]{2,1,0:T(8,128)(2,1)} %bitcast.76, bf16[1,6144,768]{2,1,0:T(8,128)(2,1)} %bitcast.77, bf16[1,6144,768]{2,1,0:T(8,128)(2,1)} %bitcast.78, bf16[1,6144,768]{2,1,0:T(8,128)(2,1)} %bitcast.79), custom_call_target="tpu_custom_call" | custom-call | flops 2415919104 | bytes 12582912 | tf_op jit(solution)/shard_map/pallas_call | solution.py:138
  188.3 6.0 %shard_map.125.d_two_ref = bf16[128,768]{1,0:T(8,128)(2,1)S(1)} custom-call(bf16[4,1536,128]{2,1,0:T(8,128)(2,1)} %bitcast.13.x_ref, bf16[1,6144,768]{2,1,0:T(8,128)(2,1)} %bitcast.80, bf16[1,6144,768]{2,1,0:T(8,128)(2,1)} %bitcast.81, bf16[1,6144,768]{2,1,0:T(8,128)(2,1)} %bitcast.82, bf16[1,6144,768]{2,1,0:T(8,128)(2,1)} %bitcast.83), custom_call_target="tpu_custom_call" | custom-call | flops 1207959552 | bytes 11010048 | tf_op jit(solution)/shard_map/pallas_call | solution.py:75
  194.4 4.7 %shard_map.126.x_ref.refs_1_ = bf16[256,2304]{1,0:T(8,128)(2,1)S(1)} custom-call(f32[256,2304]{1,0:T(8,128)S(1)} %copy-done.2, s32[256,1]{1,0:T(8,128)S(1)} %copy.22.row_ref, s32[1,256]{1,0:T(1,128)S(1)} %bitcast.63, f32[2,128]{1,0:T(2,128)S(1)} %copy-done.21, bf16[128,768]{1,0:T(8,128)(2,1)S(1)} %shard_map.121.d_one_ref, ...), custom_call_target="tpu_custom_call" | custom-call | flops 805306368 | bytes 4718592 | tf_op jit(solution)/shard_map/pallas_call | solution.py:234
  199.1 18.6 %shard_map.127 = (bf16[4,1536,256]{2,1,0:T(8,128)(2,1)S(1)}, f32[2,256]{1,0:T(2,128)S(1)}) custom-call(bf16[256,2304]{1,0:T(8,128)(2,1)S(1)} %shard_map.126.x_ref.refs_1_, bf16[3,6144,768]{2,1,0:T(8,128)(2,1)} %bitcast.68, bf16[3,6144,768]{2,1,0:T(8,128)(2,1)} %bitcast.69, bf16[3,6144,768]{2,1,0:T(8,128)(2,1)} %bitcast.70, bf16[3,6144,768]{2,1,0:T(8,128)(2,1)} %bitcast.71, ...), custom_call_target="tpu_custom_call" | custom-call | flops 7247757312 | bytes 31457280 | tf_op jit(solution)/shard_map/pallas_call | solution.py:138
  223.1 25.4 %collective-permute-done.16.refs_5_ = bf16[256,2304]{1,0:T(8,128)(2,1)S(1)} collective-permute-done((bf16[256,2304]{1,0:T(8,128)(2,1)S(1)}, bf16[256,2304]{1,0:T(8,128)(2,1)S(1)}, u32[]{:S(2)}, u32[]{:S(2)}) %collective-permute-start.16) | collective-permute-done | bytes 1179680 | tf_op jit(solution)/shard_map/ppermute | solution.py:293
  251.7 4.7 %all-to-all-start.3 = ((bf16[8,768,128]{2,1,0:T(8,128)(2,1)}), bf16[8,768,128]{2,1,0:T(8,128)(2,1)}, u32[]{:S(2)}, u32[]{:S(2)}) async-start(bf16[8,768,128]{2,1,0:T(8,128)(2,1)} %bitcast.18), calls=%async_computation.5 | async-start | bytes 3145728 | tf_op jit(solution)/shard_map/all_to_all | solution.py:332
  259.7 28.8 %collective-permute-done.22.refs_8_ = bf16[256,768]{1,0:T(8,128)(2,1)S(1)} collective-permute-done((bf16[256,768]{1,0:T(8,128)(2,1)S(1)}, bf16[256,768]{1,0:T(8,128)(2,1)S(1)}, u32[]{:S(2)}, u32[]{:S(2)}) %collective-permute-start.22) | collective-permute-done | bytes 393248 | tf_op jit(solution)/shard_map/ppermute | solution.py:321
  303.5 5.2 %shard_map.130 = bf16[1,768,768]{2,1,0:T(8,128)(2,1)} custom-call(bf16[8,768,128]{2,1,0:T(8,128)(2,1)S(1)} %copy-done.8, bf16[8,768,128]{2,1,0:T(8,128)(2,1)} %all-to-all-done.3.refs_1_, bf16[256,768]{1,0:T(8,128)(2,1)S(1)} %copy-done.14, bf16[256,768]{1,0:T(8,128)(2,1)S(1)} %copy-done.23, bf16[256,768]{1,0:T(8,128)(2,1)S(1)} %copy-done.19, ...), custom_call_target="tpu_custom_call" | custom-call | flops 2415919104 | bytes 6291456 | tf_op jit(solution)/shard_map/pallas_call | solution.py:271
  308.8 9.9 %shard_map.128.refs_3_ = f32[3,768,768]{2,1,0:T(8,128)} custom-call(bf16[8,768,256]{2,1,0:T(8,128)(2,1)} %all-to-all-done.2.refs_0_, bf16[256,2304]{1,0:T(8,128)(2,1)S(1)} %shard_map.126.x_ref.refs_1_, bf16[256,2304]{1,0:T(8,128)(2,1)} %collective-permute-done.15.refs_2_, bf16[256,2304]{1,0:T(8,128)(2,1)S(1)} %copy-done.12, ...), custom_call_target="tpu_custom_call" | custom-call | flops 5435817984 | bytes 10223616 | tf_op jit(solution)/shard_map/pallas_call | solution.py:271
  318.7 8.6 %shard_map.129 = bf16[3,768,768]{2,1,0:T(8,128)(2,1)} custom-call(bf16[8,768,256]{2,1,0:T(8,128)(2,1)} %all-to-all-done.2.refs_0_, bf16[256,2304]{1,0:T(8,128)(2,1)} %collective-permute-done.18.refs_1_, bf16[256,2304]{1,0:T(8,128)(2,1)} %collective-permute-done.19.refs_2_, f32[3,768,768]{2,1,0:T(8,128)} %shard_map.128.refs_3_), custom_call_target="tpu_custom_call" | custom-call | flops 1811939328 | bytes 5505024 | tf_op jit(solution)/shard_map/pallas_call | solution.py:271
  330.1 10.0 %reduce-scatter.3.cloned.1.call-done = bf16[1,1536,256]{2,1,0:T(8,128)(2,1)} async-done(((bf16[4,1536,256]{2,1,0:T(8,128)(2,1)}), bf16[1,1536,256]{2,1,0:T(8,128)(2,1)}) %reduce-scatter.3.cloned.1.call-update) | async-done | bytes 786448 | tf_op jit(solution)/shard_map/reduce_scatter | solution.py:405
  (186 shorter events, 61.2 us)
Async XLA Ops:
  17.9 28.8 %all-to-all-start = ((bf16[8,64,1536]{2,1,0:T(8,128)(2,1)}), bf16[8,64,1536]{2,1,0:T(8,128)(2,1)S(1)}, u32[]{:S(2)}, u32[]{:S(2)}) async-start(bf16[8,64,1536]{2,1,0:T(8,128)(2,1)} %bitcast), calls=%async_computation | async-start | bytes 3145728 | tf_op jit(solution)/shard_map/all_to_all | solution.py:355
  22.0 41.8 %all-gather.7.cloned.1.call-start = ((), (), s32[]{:S(2)}) async-start(), calls=%async_computation.8 | async-start | bytes 1966080 | tf_op jit(solution)/shard_map/all_gather | solution.py:347
  23.7 104.6 %all-gather.9.cloned.1.call-start = ((), (), s32[]{:S(2)}) async-start(), calls=%async_computation.9 | async-start | bytes 3932160 | tf_op jit(solution)/shard_map/all_gather | solution.py:390
  25.1 17.1 %collective-permute-start.4 = (f32[3,64]{1,0:T(4,128)S(1)}, f32[3,64]{1,0:T(4,128)S(1)}, u32[]{:S(2)}, u32[]{:S(2)}) collective-permute-start(f32[3,64]{1,0:T(4,128)S(1)} %bitcast.101), channel_id=1, source_target_pairs={{0,8},{4,12},{8,0},{12,4},{16,24},{20,28},{24,16},{28,20},{1,9},{5... | collective-permute-start | bytes 2312 | tf_op jit(solution)/shard_map/ppermute | solution.py:293
  26.8 16.3 %collective-permute-start.5 = (f32[3,64]{1,0:T(4,128)S(1)}, f32[3,64]{1,0:T(4,128)S(1)}, u32[]{:S(2)}, u32[]{:S(2)}) collective-permute-start(f32[3,64]{1,0:T(4,128)S(1)} %bitcast.96), channel_id=1, source_target_pairs={{0,12},{4,8},{8,4},{12,0},{16,28},{20,24},{24,20},{28,16},{1,13},{... | collective-permute-start | bytes 2312 | tf_op jit(solution)/shard_map/ppermute | solution.py:293
  26.8 16.3 %collective-permute-start.6 = (f32[3,64]{1,0:T(4,128)S(1)}, f32[3,64]{1,0:T(4,128)S(1)}, u32[]{:S(2)}, u32[]{:S(2)}) collective-permute-start(f32[3,64]{1,0:T(4,128)S(1)} %bitcast.97), channel_id=1, source_target_pairs={{0,16},{4,20},{8,24},{12,28},{16,0},{20,4},{24,8},{28,12},{1,17},{... | collective-permute-start | bytes 2312 | tf_op jit(solution)/shard_map/ppermute | solution.py:293
  63.8 24.8 %all-to-all-start.1 = ((bf16[8,768,128]{2,1,0:T(8,128)(2,1)}), bf16[8,768,128]{2,1,0:T(8,128)(2,1)S(1)}, u32[]{:S(2)}, u32[]{:S(2)}) async-start(bf16[8,768,128]{2,1,0:T(8,128)(2,1)} %bitcast.59), calls=%async_computation.1 | async-start | bytes 3145728 | tf_op jit(solution)/shard_map/all_to_all | solution.py:332
  128.3 52.8 %all-to-all-start.2 = ((bf16[8,768,256]{2,1,0:T(8,128)(2,1)}), bf16[8,768,256]{2,1,0:T(8,128)(2,1)}, u32[]{:S(2)}, u32[]{:S(2)}) async-start(bf16[8,768,256]{2,1,0:T(8,128)(2,1)} %bitcast.56), calls=%async_computation.2 | async-start | bytes 6291456 | tf_op jit(solution)/shard_map/all_to_all | solution.py:332
  133.1 55.3 %all-gather.11.cloned.1.call-start = ((), (), s32[]{:S(2)}) async-start(), calls=%async_computation.10 | async-start | bytes 1966080 | tf_op jit(solution)/shard_map/all_gather | solution.py:396
  133.8 193.4 %reduce-scatter.5.cloned.1.call-start = ((), (), s32[]{:S(2)}) async-start(), calls=%async_computation.7 | async-start | bytes 3932160 | tf_op jit(solution)/shard_map/reduce_scatter | solution.py:412
  156.1 22.2 %collective-permute-start.11 = (bf16[256,768]{1,0:T(8,128)(2,1)S(1)}, bf16[256,768]{1,0:T(8,128)(2,1)S(1)}, u32[]{:S(2)}, u32[]{:S(2)}) collective-permute-start(bf16[256,768]{1,0:T(8,128)(2,1)S(1)} %shard_map.123.x_ref.refs_2_), channel_id=1, source_target_pairs={{0,16},{4,20},{8,24},{12,28},{16,0},{20,4},{24,8},{28,12},{1,17},{... | collective-permute-start | bytes 1179656 | tf_op jit(solution)/shard_map/ppermute | solution.py:293
  157.8 20.6 %collective-permute-start.12 = (bf16[256,768]{1,0:T(8,128)(2,1)S(1)}, bf16[256,768]{1,0:T(8,128)(2,1)S(1)}, u32[]{:S(2)}, u32[]{:S(2)}) collective-permute-start(bf16[256,768]{1,0:T(8,128)(2,1)S(1)} %shard_map.123.x_ref.refs_2_), channel_id=1, source_target_pairs={{0,8},{4,12},{8,0},{12,4},{16,24},{20,28},{24,16},{28,20},{1,9},{5... | collective-permute-start | bytes 1179656 | tf_op jit(solution)/shard_map/ppermute | solution.py:293
  178.4 16.0 %collective-permute-start.13 = (bf16[256,768]{1,0:T(8,128)(2,1)S(1)}, bf16[256,768]{1,0:T(8,128)(2,1)S(1)}, u32[]{:S(2)}, u32[]{:S(2)}) collective-permute-start(bf16[256,768]{1,0:T(8,128)(2,1)S(1)} %collective-permute-done.12.refs_4_), channel_id=1, source_target_pairs={{0,4},{4,0},{8,12},{12,8},{16,20},{20,16},{24,28},{28,24},{1,5},{5... | collective-permute-start | bytes 1179656 | tf_op jit(solution)/shard_map/ppermute | solution.py:293
  178.4 16.0 %collective-permute-start.14 = (bf16[256,768]{1,0:T(8,128)(2,1)S(1)}, bf16[256,768]{1,0:T(8,128)(2,1)S(1)}, u32[]{:S(2)}, u32[]{:S(2)}) collective-permute-start(bf16[256,768]{1,0:T(8,128)(2,1)S(1)} %collective-permute-done.11.refs_6_), channel_id=1, source_target_pairs={{0,4},{4,0},{8,12},{12,8},{16,20},{20,16},{24,28},{28,24},{1,5},{5... | collective-permute-start | bytes 1179656 | tf_op jit(solution)/shard_map/ppermute | solution.py:293
  219.4 120.7 %reduce-scatter.3.cloned.1.call-start = ((), (), s32[]{:S(2)}) async-start(), calls=%async_computation.6 | async-start | bytes 3932160 | tf_op jit(solution)/shard_map/reduce_scatter | solution.py:405
  220.2 28.3 %collective-permute-start.16 = (bf16[256,2304]{1,0:T(8,128)(2,1)S(1)}, bf16[256,2304]{1,0:T(8,128)(2,1)S(1)}, u32[]{:S(2)}, u32[]{:S(2)}) collective-permute-start(bf16[256,2304]{1,0:T(8,128)(2,1)S(1)} %shard_map.126.x_ref.refs_1_), channel_id=1, source_target_pairs={{0,16},{4,20},{8,24},{12,28},{16,0},{20,4},{24,8},{28,12},{1,17},{... | collective-permute-start | bytes 3538952 | tf_op jit(solution)/shard_map/ppermute | solution.py:293
  221.6 28.0 %collective-permute-start.17 = (bf16[256,2304]{1,0:T(8,128)(2,1)S(1)}, bf16[256,2304]{1,0:T(8,128)(2,1)S(1)}, u32[]{:S(2)}, u32[]{:S(2)}) collective-permute-start(bf16[256,2304]{1,0:T(8,128)(2,1)S(1)} %shard_map.126.x_ref.refs_1_), channel_id=1, source_target_pairs={{0,8},{4,12},{8,0},{12,4},{16,24},{20,28},{24,16},{28,20},{1,9},{5... | collective-permute-start | bytes 3538952 | tf_op jit(solution)/shard_map/ppermute | solution.py:293
  251.1 42.2 %collective-permute-start.18 = (bf16[256,2304]{1,0:T(8,128)(2,1)}, bf16[256,2304]{1,0:T(8,128)(2,1)}, u32[]{:S(2)}, u32[]{:S(2)}) collective-permute-start(bf16[256,2304]{1,0:T(8,128)(2,1)} %broadcast_select_fusion), channel_id=1, source_target_pairs={{0,16},{4,12},{8,24},{12,4},{16,0},{20,28},{24,8},{28,20},{1,17},{... | collective-permute-start | bytes 3538952 | tf_op jit(solution)/shard_map/ppermute | solution.py:321
  251.7 44.8 %all-to-all-start.3 = ((bf16[8,768,128]{2,1,0:T(8,128)(2,1)}), bf16[8,768,128]{2,1,0:T(8,128)(2,1)}, u32[]{:S(2)}, u32[]{:S(2)}) async-start(bf16[8,768,128]{2,1,0:T(8,128)(2,1)} %bitcast.18), calls=%async_computation.5 | async-start | bytes 3145728 | tf_op jit(solution)/shard_map/all_to_all | solution.py:332
  256.4 52.3 %collective-permute-start.20 = (bf16[256,2304]{1,0:T(8,128)(2,1)}, bf16[256,2304]{1,0:T(8,128)(2,1)}, u32[]{:S(2)}, u32[]{:S(2)}) collective-permute-start(bf16[256,2304]{1,0:T(8,128)(2,1)} %copy-done.11), channel_id=1, source_target_pairs={{0,4},{4,0},{8,12},{12,8},{16,20},{20,16},{24,28},{28,24},{1,5},{5... | collective-permute-start | bytes 3538952 | tf_op jit(solution)/shard_map/ppermute | solution.py:293
  256.6 52.2 %collective-permute-start.21 = (bf16[256,2304]{1,0:T(8,128)(2,1)}, bf16[256,2304]{1,0:T(8,128)(2,1)}, u32[]{:S(2)}, u32[]{:S(2)}) collective-permute-start(bf16[256,2304]{1,0:T(8,128)(2,1)} %copy-done.9), channel_id=1, source_target_pairs={{0,4},{4,0},{8,12},{12,8},{16,20},{20,16},{24,28},{28,24},{1,5},{5... | collective-permute-start | bytes 3538952 | tf_op jit(solution)/shard_map/ppermute | solution.py:293
  258.0 30.5 %collective-permute-start.22 = (bf16[256,768]{1,0:T(8,128)(2,1)S(1)}, bf16[256,768]{1,0:T(8,128)(2,1)S(1)}, u32[]{:S(2)}, u32[]{:S(2)}) collective-permute-start(bf16[256,768]{1,0:T(8,128)(2,1)S(1)} %broadcast_select_fusion.1), channel_id=1, source_target_pairs={{0,16},{4,12},{8,24},{12,4},{16,0},{20,28},{24,8},{28,20},{1,17},{... | collective-permute-start | bytes 1179656 | tf_op jit(solution)/shard_map/ppermute | solution.py:321
  259.7 29.9 %collective-permute-start.24 = (f32[2,256]{1,0:T(2,128)S(1)}, f32[2,256]{1,0:T(2,128)S(1)}, u32[]{:S(2)}, u32[]{:S(2)}) collective-permute-start(f32[2,256]{1,0:T(2,128)S(1)} %get-tuple-element.67), channel_id=1, source_target_pairs={{0,1},{1,0},{2,3},{3,2},{4,5},{5,4},{6,7},{7,6},{8,9},{9,8},{10,11... | collective-permute-start | bytes 6152 | tf_op jit(solution)/shard_map/ppermute | solution.py:293
  293.2 25.4 %collective-permute-start.19 = (bf16[256,2304]{1,0:T(8,128)(2,1)}, bf16[256,2304]{1,0:T(8,128)(2,1)}, u32[]{:S(2)}, u32[]{:S(2)}) collective-permute-start(bf16[256,2304]{1,0:T(8,128)(2,1)} %collective-permute-done.18.refs_1_), channel_id=1, source_target_pairs={{0,4},{4,0},{8,12},{12,8},{16,20},{20,16},{24,28},{28,24},{1,5},{5... | collective-permute-start | bytes 3538952 | tf_op jit(solution)/shard_map/ppermute | solution.py:293
  (50 other events, 356.5 us)
Sparse Core Ops, SparseCore 0:
  25.0 38.7 all-gather.6
  65.9 62.3 all-gather.8
  136.0 36.1 all-gather.10
  219.5 58.0 reduce-scatter.4
  279.8 60.2 reduce-scatter.2

commit v5 on v4

--- a/solution.py
+++ b/solution.py
@@ -10,7 +10,7 @@
 
 DH = 128
 VMEM_BYTES = 48 * 1024 * 1024
-STREAMS = 4
+STREAMS = 1
 
 
 def dot_f32(left, right, left_dims, right_dims):
@@ -398,9 +398,9 @@
     normed_cols = columns_to_owner(normed, "dp")
 
     heads_out = attention(forward_kernel, projected, segment, qk_gain, (), 1)
-    heads_near, heads_far = gather_xor(heads_out, "dp")
-    heads_here, normed_cols = lax.optimization_barrier((heads_out, normed_cols))
-    attn_part = expand(heads_here, w_out_t, parts, 1)
+    late_heads, normed_cols = lax.optimization_barrier((heads_out, normed_cols))
+    heads_near, heads_far = gather_xor(late_heads, "dp")
+    attn_part = expand(heads_out, w_out_t, parts, 1)
     attn_part, cot_two = lax.optimization_barrier((attn_part, cot_two))
     attn = lax.psum_scatter(attn_part, "mp", scatter_dimension=0, tiled=False)
     output = (packed.astype(jnp.float32) + attn.astype(jnp.float32)).astype(jnp.bfloat16).T

time: 350 us -> 372 us (1.063)
  blocking collectives: 0 us -> 41.5 us
  waiting for transfers between devices: 173 us -> 159 us
  Pallas kernels: 86.9 us -> 80.7 us
  starting transfers between devices: 41.9 us -> 36.4 us
  local copies, waits for them, and re-layouts: 18.9 us -> 24.2 us
    all_to_all x0 -> x1, blocking collectives: none -> 41.5 us  [columns_to_owner(): return lax.all_to_all(cut, axis, 0, 0, tiled=True)]
    reduce_scatter x1, waiting for transfers between devices: 9.97 us -> 0.01 us  [shards(): attn = lax.psum_scatter(attn_part, 'mp', scatter_dimension=0, tiled=False)]
    ppermute x25, waiting for transfers between devices: 64.2 us -> 54.5 us  [flip(): return lax.ppermute(values, axis, [(at, at ^ bit) for at in range(count)])]
    all_gather x1, waiting for transfers between devices: 0.01 us -> 6.56 us  [shards(): cot_two = lax.all_gather(late_cot, 'mp', axis=0, tiled=False)]
    unnamed x87 -> x95, local copies, waits for them, and re-layouts: 16.2 us -> 21.4 us
    all_to_all x3 -> x2, starting transfers between devices: 13.2 us -> 8.46 us  [columns_to_owner(): return lax.all_to_all(cut, axis, 0, 0, tiled=True)]
    pallas_call x2, Pallas kernels: 25.8 us -> 21.8 us  [expand(): pl.pallas_call(functools.partial(expand_kernel, kinds, width), grid=(part...]
    all_to_all x3 -> x2, waiting for transfers between devices: 15.3 us -> 15.3 us  [columns_to_owner(): return lax.all_to_all(cut, axis, 0, 0, tiled=True)]
  transfers between devices with their start and end apart: 36 -> 35, of which waited for: 14 -> 14; matrix products, arithmetic and copies ran while one was open for 4% -> 3% of each run, Pallas kernels for 18% -> 22%
where the time goes in v5:
time: 372 us; the launch traced here: 371 us
  waiting for transfers between devices  159 us (43%)
  Pallas kernels  80.7 us (22%)
  blocking collectives  41.5 us (11%)
  starting transfers between devices  36.4 us (10%)
  local copies, waits for them, and re-layouts  24.2 us (7%)
  between operations  14.4 us (4%)
  other arithmetic  9.05 us (2%)
  matrix products  5.06 us (1%)
    ppermute x25, waiting for transfers between devices, flip(): return lax.ppermute(values, axis, [(at, at ^ bit) for at in range(count)])  54.5 us
    all_to_all x1, blocking collectives, columns_to_owner(): return lax.all_to_all(cut, axis, 0, 0, tiled=True)  41.5 us
    all_gather x1, waiting for transfers between devices, shards(): normed = lax.all_gather(normed_part, 'mp', axis=0, tiled=False)  39.7 us
    pallas_call x3, Pallas kernels, project(): pl.pallas_call(functools.partial(project_kernel, steps, width), grid=(ste...  29.2 us
    ppermute x2, waiting for transfers between devices, gather_xor(): far = lax.ppermute(onward, axis, pairs)  28.3 us
    pallas_call x3, Pallas kernels, weight_grad(): pl.pallas_call(functools.partial(weight_kernel, keys, len(columns), scale...  22.5 us
    pallas_call x2, Pallas kernels, expand(): pl.pallas_call(functools.partial(expand_kernel, kinds, width), grid=(part...  21.8 us
    unnamed x95, local copies, waits for them, and re-layouts  21.4 us
  transfers between devices with their start and end apart: 35, of which 14 were waited for; matrix products, arithmetic and copies ran while one was open for 3% of the time, Pallas kernels for 22%

profile of v5, /device:TPU:0, one launch (start us, length us, event | category | flops | bytes accessed | tf_op | source)
XLA Modules:
  0.0 370.7 jit_solution(18026610690514056499)
XLA Ops:
  8.8 2.9 convolution_convert_fusion
  12.2 3.1 collective-permute-start
  17.9 4.1 %all-to-all-start = ((bf16[8,64,1536]{2,1,0:T(8,128)(2,1)}), bf16[8,64,1536]{2,1,0:T(8,128)(2,1)S(1)}, u32[]{:S(2)}, u32[]{:S(2)}) async-start(bf16[8,64,1536]{2,1,0:T(8,128)(2,1)} %bitcast), calls=%async_computation | async-start | bytes 3145728 | tf_op jit(solution)/shard_map/all_to_all | solution.py:355
  31.2 11.0 %collective-permute-done.4 = f32[3,64]{1,0:T(4,128)S(1)} collective-permute-done((f32[3,64]{1,0:T(4,128)S(1)}, f32[3,64]{1,0:T(4,128)S(1)}, u32[]{:S(2)}, u32[]{:S(2)}) %collective-permute-start.4) | collective-permute-done | bytes 800 | tf_op jit(solution)/shard_map/ppermute | solution.py:293
  43.1 3.0 collective-permute-done.9
  49.0 14.9 %all-gather.7.cloned.1.call-done = bf16[6144,128]{1,0:T(8,128)(2,1)} async-done(((bf16[1536,128]{1,0:T(8,128)(2,1)}), bf16[6144,128]{1,0:T(8,128)(2,1)}) %all-gather.7.cloned.1.call-update) | async-done | bytes 1572880 | tf_op jit(solution)/shard_map/all_gather | solution.py:347
  63.8 3.8 %all-to-all-start.1 = ((bf16[8,768,128]{2,1,0:T(8,128)(2,1)}), bf16[8,768,128]{2,1,0:T(8,128)(2,1)S(1)}, u32[]{:S(2)}, u32[]{:S(2)}) async-start(bf16[8,768,128]{2,1,0:T(8,128)(2,1)} %bitcast.59), calls=%async_computation.1 | async-start | bytes 3145728 | tf_op jit(solution)/shard_map/all_to_all | solution.py:332
  67.7 5.6 %shard_map.121.d_one_ref = bf16[128,768]{1,0:T(8,128)(2,1)S(1)} custom-call(bf16[4,1536,128]{2,1,0:T(8,128)(2,1)S(1)} %bitcast.60, bf16[1,6144,768]{2,1,0:T(8,128)(2,1)} %bitcast.66), custom_call_target="tpu_custom_call" | custom-call | flops 1207959552 | bytes 11010048 | tf_op jit(solution)/shard_map/pallas_call | solution.py:75
  73.3 15.3 %all-to-all-done.1.refs_0_ = bf16[8,768,128]{2,1,0:T(8,128)(2,1)S(1)} async-done(((bf16[8,768,128]{2,1,0:T(8,128)(2,1)}), bf16[8,768,128]{2,1,0:T(8,128)(2,1)S(1)}, u32[]{:S(2)}, u32[]{:S(2)}) %all-to-all-start.1) | async-done | bytes 1572896 | tf_op jit(solution)/shard_map/all_to_all | solution.py:332
  88.7 39.7 %all-gather.9.cloned.1.call-done = bf16[6144,256]{1,0:T(8,128)(2,1)} async-done(((bf16[1536,256]{1,0:T(8,128)(2,1)}), bf16[6144,256]{1,0:T(8,128)(2,1)}) %all-gather.9.cloned.1.call-update) | async-done | bytes 3145744 | tf_op jit(solution)/shard_map/all_gather | solution.py:390
  130.5 17.6 %shard_map.122.proj_ref = f32[256,2304]{1,0:T(8,128)S(1)} custom-call(bf16[4,1536,256]{2,1,0:T(8,128)(2,1)S(1)} %bitcast.57, bf16[3,6144,768]{2,1,0:T(8,128)(2,1)} %bitcast.64), custom_call_target="tpu_custom_call" | custom-call | flops 7247757312 | bytes 31457280 | tf_op jit(solution)/shard_map/pallas_call | solution.py:75
  151.2 6.0 %shard_map.124 = bf16[4,1536,256]{2,1,0:T(8,128)(2,1)S(1)} custom-call(bf16[256,768]{1,0:T(8,128)(2,1)S(1)} %shard_map.123.x_ref.refs_2_, bf16[1,6144,768]{2,1,0:T(8,128)(2,1)} %bitcast.67), custom_call_target="tpu_custom_call" | custom-call | flops 2415919104 | bytes 12582912 | tf_op jit(solution)/shard_map/pallas_call | solution.py:138
  159.7 6.6 %all-gather.11.cloned.1.call-done = bf16[6144,128]{1,0:T(8,128)(2,1)} async-done(((bf16[1536,128]{1,0:T(8,128)(2,1)}), bf16[6144,128]{1,0:T(8,128)(2,1)}) %all-gather.11.cloned.1.call-update) | async-done | bytes 1572880 | tf_op jit(solution)/shard_map/all_gather | solution.py:396
  168.2 41.5 %all_to_all.20.refs_0_ = bf16[8,768,256]{2,1,0:T(8,128)(2,1)} all-to-all(bf16[8,768,256]{2,1,0:T(8,128)(2,1)S(1)} %bitcast.58), channel_id=1, replica_groups=mesh['dp'=8,'mp'=4] {'dp'}, dimensions={0} | all-to-all | bytes 6291456 | tf_op jit(solution)/shard_map/all_to_all | solution.py:332
  211.4 9.8 %collective-permute-done.11.refs_6_ = bf16[256,768]{1,0:T(8,128)(2,1)S(1)} collective-permute-done((bf16[256,768]{1,0:T(8,128)(2,1)S(1)}, bf16[256,768]{1,0:T(8,128)(2,1)S(1)}, u32[]{:S(2)}, u32[]{:S(2)}) %collective-permute-start.11) | collective-permute-done | bytes 393248 | tf_op jit(solution)/shard_map/ppermute | solution.py:293
  224.2 5.9 %shard_map.125.d_two_ref = bf16[128,768]{1,0:T(8,128)(2,1)S(1)} custom-call(bf16[4,1536,128]{2,1,0:T(8,128)(2,1)} %bitcast.12.x_ref, bf16[1,6144,768]{2,1,0:T(8,128)(2,1)} %bitcast.68), custom_call_target="tpu_custom_call" | custom-call | flops 1207959552 | bytes 11010048 | tf_op jit(solution)/shard_map/pallas_call | solution.py:75
  230.2 4.7 %shard_map.126.x_ref.refs_1_ = bf16[256,2304]{1,0:T(8,128)(2,1)S(1)} custom-call(f32[256,2304]{1,0:T(8,128)S(1)} %copy-done.5, s32[256,1]{1,0:T(8,128)S(1)} %copy.22.row_ref, s32[1,256]{1,0:T(1,128)S(1)} %bitcast.63, f32[2,128]{1,0:T(2,128)S(1)} %copy-done.25, bf16[128,768]{1,0:T(8,128)(2,1)S(1)} %shard_map.121.d_one_ref, ...), custom_call_target="tpu_custom_call" | custom-call | flops 805306368 | bytes 4718592 | tf_op jit(solution)/shard_map/pallas_call | solution.py:234
  234.9 15.8 %shard_map.127 = (bf16[4,1536,256]{2,1,0:T(8,128)(2,1)S(1)}, f32[2,256]{1,0:T(2,128)S(1)}) custom-call(bf16[256,2304]{1,0:T(8,128)(2,1)S(1)} %shard_map.126.x_ref.refs_1_, bf16[3,6144,768]{2,1,0:T(8,128)(2,1)} %bitcast.65, f32[6144,1]{1,0:T(8,128)} %copy.25.refs_1_, bf16[4,1536,256]{2,1,0:T(8,128)(2,1)} %bitcast.56), custom_call_target="tpu_custom_call" | custom-call | flops 7247757312 | bytes 31457280 | tf_op jit(solution)/shard_map/pallas_call | solution.py:138
  255.4 25.4 %collective-permute-done.16.refs_5_ = bf16[256,2304]{1,0:T(8,128)(2,1)S(1)} collective-permute-done((bf16[256,2304]{1,0:T(8,128)(2,1)S(1)}, bf16[256,2304]{1,0:T(8,128)(2,1)S(1)}, u32[]{:S(2)}, u32[]{:S(2)}) %collective-permute-start.16) | collective-permute-done | bytes 1179680 | tf_op jit(solution)/shard_map/ppermute | solution.py:293
  284.1 4.7 %all-to-all-start.3 = ((bf16[8,768,128]{2,1,0:T(8,128)(2,1)}), bf16[8,768,128]{2,1,0:T(8,128)(2,1)}, u32[]{:S(2)}, u32[]{:S(2)}) async-start(bf16[8,768,128]{2,1,0:T(8,128)(2,1)} %bitcast.18), calls=%async_computation.5 | async-start | bytes 3145728 | tf_op jit(solution)/shard_map/all_to_all | solution.py:332
  292.6 28.3 %collective-permute-done.22.refs_8_ = bf16[256,768]{1,0:T(8,128)(2,1)S(1)} collective-permute-done((bf16[256,768]{1,0:T(8,128)(2,1)S(1)}, bf16[256,768]{1,0:T(8,128)(2,1)S(1)}, u32[]{:S(2)}, u32[]{:S(2)}) %collective-permute-start.22) | collective-permute-done | bytes 393248 | tf_op jit(solution)/shard_map/ppermute | solution.py:321
  336.2 5.0 %shard_map.130 = bf16[1,768,768]{2,1,0:T(8,128)(2,1)} custom-call(bf16[8,768,128]{2,1,0:T(8,128)(2,1)S(1)} %copy-done.11, bf16[8,768,128]{2,1,0:T(8,128)(2,1)} %all-to-all-done.3.refs_1_, bf16[256,768]{1,0:T(8,128)(2,1)S(1)} %copy-done.18, bf16[256,768]{1,0:T(8,128)(2,1)S(1)} %copy-done.27, bf16[256,768]{1,0:T(8,128)(2,1)S(1)} %copy-done.23, ...), custom_call_target="tpu_custom_call" | custom-call | flops 2415919104 | bytes 6291456 | tf_op jit(solution)/shard_map/pallas_call | solution.py:271
  341.3 10.0 %shard_map.128.refs_3_ = f32[3,768,768]{2,1,0:T(8,128)} custom-call(bf16[8,768,256]{2,1,0:T(8,128)(2,1)} %all_to_all.20.refs_0_, bf16[256,2304]{1,0:T(8,128)(2,1)S(1)} %shard_map.126.x_ref.refs_1_, bf16[256,2304]{1,0:T(8,128)(2,1)} %collective-permute-done.15.refs_2_, bf16[256,2304]{1,0:T(8,128)(2,1)S(1)} %copy-done.15, ...), custom_call_target="tpu_custom_call" | custom-call | flops 5435817984 | bytes 10223616 | tf_op jit(solution)/shard_map/pallas_call | solution.py:271
  351.4 7.4 %shard_map.129 = bf16[3,768,768]{2,1,0:T(8,128)(2,1)} custom-call(bf16[8,768,256]{2,1,0:T(8,128)(2,1)S(1)} %copy-done.3, bf16[256,2304]{1,0:T(8,128)(2,1)} %collective-permute-done.18.refs_1_, bf16[256,2304]{1,0:T(8,128)(2,1)} %collective-permute-done.19.refs_2_, f32[3,768,768]{2,1,0:T(8,128)} %shard_map.128.refs_3_), custom_call_target="tpu_custom_call" | custom-call | flops 1811939328 | bytes 5505024 | tf_op jit(solution)/shard_map/pallas_call | solution.py:271
  (193 shorter events, 64.1 us)
Async XLA Ops:
  12.2 11.8 %collective-permute-start = (f32[2,256]{1,0:T(2,128)S(1)}, f32[2,256]{1,0:T(2,128)S(1)}, u32[]{:S(2)}, u32[]{:S(2)}) collective-permute-start(f32[2,256]{1,0:T(2,128)S(1)} %pad_maximum_fusion.1), channel_id=1, source_target_pairs={{0,1},{1,0},{2,3},{3,2},{4,5},{5,4},{6,7},{7,6},{8,9},{9,8},{10,11... | collective-permute-start | bytes 6152 | tf_op jit(solution)/shard_map/ppermute | solution.py:293
  17.9 28.8 %all-to-all-start = ((bf16[8,64,1536]{2,1,0:T(8,128)(2,1)}), bf16[8,64,1536]{2,1,0:T(8,128)(2,1)S(1)}, u32[]{:S(2)}, u32[]{:S(2)}) async-start(bf16[8,64,1536]{2,1,0:T(8,128)(2,1)} %bitcast), calls=%async_computation | async-start | bytes 3145728 | tf_op jit(solution)/shard_map/all_to_all | solution.py:355
  22.0 41.8 %all-gather.7.cloned.1.call-start = ((), (), s32[]{:S(2)}) async-start(), calls=%async_computation.8 | async-start | bytes 1966080 | tf_op jit(solution)/shard_map/all_gather | solution.py:347
  23.7 104.6 %all-gather.9.cloned.1.call-start = ((), (), s32[]{:S(2)}) async-start(), calls=%async_computation.9 | async-start | bytes 3932160 | tf_op jit(solution)/shard_map/all_gather | solution.py:390
  25.1 17.1 %collective-permute-start.4 = (f32[3,64]{1,0:T(4,128)S(1)}, f32[3,64]{1,0:T(4,128)S(1)}, u32[]{:S(2)}, u32[]{:S(2)}) collective-permute-start(f32[3,64]{1,0:T(4,128)S(1)} %bitcast.86), channel_id=1, source_target_pairs={{0,8},{4,12},{8,0},{12,4},{16,24},{20,28},{24,16},{28,20},{1,9},{5... | collective-permute-start | bytes 2312 | tf_op jit(solution)/shard_map/ppermute | solution.py:293
  26.8 16.3 %collective-permute-start.5 = (f32[3,64]{1,0:T(4,128)S(1)}, f32[3,64]{1,0:T(4,128)S(1)}, u32[]{:S(2)}, u32[]{:S(2)}) collective-permute-start(f32[3,64]{1,0:T(4,128)S(1)} %bitcast.81), channel_id=1, source_target_pairs={{0,12},{4,8},{8,4},{12,0},{16,28},{20,24},{24,20},{28,16},{1,13},{... | collective-permute-start | bytes 2312 | tf_op jit(solution)/shard_map/ppermute | solution.py:293
  26.8 16.3 %collective-permute-start.6 = (f32[3,64]{1,0:T(4,128)S(1)}, f32[3,64]{1,0:T(4,128)S(1)}, u32[]{:S(2)}, u32[]{:S(2)}) collective-permute-start(f32[3,64]{1,0:T(4,128)S(1)} %bitcast.82), channel_id=1, source_target_pairs={{0,16},{4,20},{8,24},{12,28},{16,0},{20,4},{24,8},{28,12},{1,17},{... | collective-permute-start | bytes 2312 | tf_op jit(solution)/shard_map/ppermute | solution.py:293
  28.5 14.6 %collective-permute-start.7 = (f32[3,64]{1,0:T(4,128)S(1)}, f32[3,64]{1,0:T(4,128)S(1)}, u32[]{:S(2)}, u32[]{:S(2)}) collective-permute-start(f32[3,64]{1,0:T(4,128)S(1)} %bitcast.83), channel_id=1, source_target_pairs={{0,20},{4,16},{8,28},{12,24},{16,4},{20,0},{24,12},{28,8},{1,21},{... | collective-permute-start | bytes 2312 | tf_op jit(solution)/shard_map/ppermute | solution.py:293
  28.6 14.6 %collective-permute-start.8 = (f32[3,64]{1,0:T(4,128)S(1)}, f32[3,64]{1,0:T(4,128)S(1)}, u32[]{:S(2)}, u32[]{:S(2)}) collective-permute-start(f32[3,64]{1,0:T(4,128)S(1)} %bitcast.85), channel_id=1, source_target_pairs={{0,24},{4,28},{8,16},{12,20},{16,8},{20,12},{24,0},{28,4},{1,25},{... | collective-permute-start | bytes 2312 | tf_op jit(solution)/shard_map/ppermute | solution.py:293
  63.8 24.8 %all-to-all-start.1 = ((bf16[8,768,128]{2,1,0:T(8,128)(2,1)}), bf16[8,768,128]{2,1,0:T(8,128)(2,1)S(1)}, u32[]{:S(2)}, u32[]{:S(2)}) async-start(bf16[8,768,128]{2,1,0:T(8,128)(2,1)} %bitcast.59), calls=%async_computation.1 | async-start | bytes 3145728 | tf_op jit(solution)/shard_map/all_to_all | solution.py:332
  67.6 98.6 %all-gather.11.cloned.1.call-start = ((), (), s32[]{:S(2)}) async-start(), calls=%async_computation.10 | async-start | bytes 1966080 | tf_op jit(solution)/shard_map/all_gather | solution.py:396
  128.4 230.4 %reduce-scatter.3.cloned.1.call-start = ((), (), s32[]{:S(2)}) async-start(), calls=%async_computation.6 | async-start | bytes 3932160 | tf_op jit(solution)/shard_map/reduce_scatter | solution.py:405
  166.3 195.0 %reduce-scatter.5.cloned.1.call-start = ((), (), s32[]{:S(2)}) async-start(), calls=%async_computation.7 | async-start | bytes 3932160 | tf_op jit(solution)/shard_map/reduce_scatter | solution.py:412
  209.7 11.5 %collective-permute-start.11 = (bf16[256,768]{1,0:T(8,128)(2,1)S(1)}, bf16[256,768]{1,0:T(8,128)(2,1)S(1)}, u32[]{:S(2)}, u32[]{:S(2)}) collective-permute-start(bf16[256,768]{1,0:T(8,128)(2,1)S(1)} %copy-done.17), channel_id=1, source_target_pairs={{0,16},{4,20},{8,24},{12,28},{16,0},{20,4},{24,8},{28,12},{1,17},{... | collective-permute-start | bytes 1179656 | tf_op jit(solution)/shard_map/ppermute | solution.py:293
  210.2 11.2 %collective-permute-start.12 = (bf16[256,768]{1,0:T(8,128)(2,1)S(1)}, bf16[256,768]{1,0:T(8,128)(2,1)S(1)}, u32[]{:S(2)}, u32[]{:S(2)}) collective-permute-start(bf16[256,768]{1,0:T(8,128)(2,1)S(1)} %copy-done.17), channel_id=1, source_target_pairs={{0,8},{4,12},{8,0},{12,4},{16,24},{20,28},{24,16},{28,20},{1,9},{5... | collective-permute-start | bytes 1179656 | tf_op jit(solution)/shard_map/ppermute | solution.py:293
  252.5 28.4 %collective-permute-start.16 = (bf16[256,2304]{1,0:T(8,128)(2,1)S(1)}, bf16[256,2304]{1,0:T(8,128)(2,1)S(1)}, u32[]{:S(2)}, u32[]{:S(2)}) collective-permute-start(bf16[256,2304]{1,0:T(8,128)(2,1)S(1)} %shard_map.126.x_ref.refs_1_), channel_id=1, source_target_pairs={{0,16},{4,20},{8,24},{12,28},{16,0},{20,4},{24,8},{28,12},{1,17},{... | collective-permute-start | bytes 3538952 | tf_op jit(solution)/shard_map/ppermute | solution.py:293
  254.0 28.0 %collective-permute-start.17 = (bf16[256,2304]{1,0:T(8,128)(2,1)S(1)}, bf16[256,2304]{1,0:T(8,128)(2,1)S(1)}, u32[]{:S(2)}, u32[]{:S(2)}) collective-permute-start(bf16[256,2304]{1,0:T(8,128)(2,1)S(1)} %shard_map.126.x_ref.refs_1_), channel_id=1, source_target_pairs={{0,8},{4,12},{8,0},{12,4},{16,24},{20,28},{24,16},{28,20},{1,9},{5... | collective-permute-start | bytes 3538952 | tf_op jit(solution)/shard_map/ppermute | solution.py:293
  283.4 42.1 %collective-permute-start.18 = (bf16[256,2304]{1,0:T(8,128)(2,1)}, bf16[256,2304]{1,0:T(8,128)(2,1)}, u32[]{:S(2)}, u32[]{:S(2)}) collective-permute-start(bf16[256,2304]{1,0:T(8,128)(2,1)} %broadcast_select_fusion), channel_id=1, source_target_pairs={{0,16},{4,12},{8,24},{12,4},{16,0},{20,28},{24,8},{28,20},{1,17},{... | collective-permute-start | bytes 3538952 | tf_op jit(solution)/shard_map/ppermute | solution.py:321
  284.1 44.9 %all-to-all-start.3 = ((bf16[8,768,128]{2,1,0:T(8,128)(2,1)}), bf16[8,768,128]{2,1,0:T(8,128)(2,1)}, u32[]{:S(2)}, u32[]{:S(2)}) async-start(bf16[8,768,128]{2,1,0:T(8,128)(2,1)} %bitcast.18), calls=%async_computation.5 | async-start | bytes 3145728 | tf_op jit(solution)/shard_map/all_to_all | solution.py:332
  288.8 52.5 %collective-permute-start.20 = (bf16[256,2304]{1,0:T(8,128)(2,1)}, bf16[256,2304]{1,0:T(8,128)(2,1)}, u32[]{:S(2)}, u32[]{:S(2)}) collective-permute-start(bf16[256,2304]{1,0:T(8,128)(2,1)} %copy-done.14), channel_id=1, source_target_pairs={{0,4},{4,0},{8,12},{12,8},{16,20},{20,16},{24,28},{28,24},{1,5},{5... | collective-permute-start | bytes 3538952 | tf_op jit(solution)/shard_map/ppermute | solution.py:293
  288.9 52.3 %collective-permute-start.21 = (bf16[256,2304]{1,0:T(8,128)(2,1)}, bf16[256,2304]{1,0:T(8,128)(2,1)}, u32[]{:S(2)}, u32[]{:S(2)}) collective-permute-start(bf16[256,2304]{1,0:T(8,128)(2,1)} %copy-done.12), channel_id=1, source_target_pairs={{0,4},{4,0},{8,12},{12,8},{16,20},{20,16},{24,28},{28,24},{1,5},{5... | collective-permute-start | bytes 3538952 | tf_op jit(solution)/shard_map/ppermute | solution.py:293
  290.4 30.5 %collective-permute-start.22 = (bf16[256,768]{1,0:T(8,128)(2,1)S(1)}, bf16[256,768]{1,0:T(8,128)(2,1)S(1)}, u32[]{:S(2)}, u32[]{:S(2)}) collective-permute-start(bf16[256,768]{1,0:T(8,128)(2,1)S(1)} %broadcast_select_fusion.1), channel_id=1, source_target_pairs={{0,16},{4,12},{8,24},{12,4},{16,0},{20,28},{24,8},{28,20},{1,17},{... | collective-permute-start | bytes 1179656 | tf_op jit(solution)/shard_map/ppermute | solution.py:321
  292.1 30.2 %collective-permute-start.24 = (f32[2,256]{1,0:T(2,128)S(1)}, f32[2,256]{1,0:T(2,128)S(1)}, u32[]{:S(2)}, u32[]{:S(2)}) collective-permute-start(f32[2,256]{1,0:T(2,128)S(1)} %get-tuple-element.67), channel_id=1, source_target_pairs={{0,1},{1,0},{2,3},{3,2},{4,5},{5,4},{6,7},{7,6},{8,9},{9,8},{10,11... | collective-permute-start | bytes 6152 | tf_op jit(solution)/shard_map/ppermute | solution.py:293
  325.5 25.8 %collective-permute-start.19 = (bf16[256,2304]{1,0:T(8,128)(2,1)}, bf16[256,2304]{1,0:T(8,128)(2,1)}, u32[]{:S(2)}, u32[]{:S(2)}) collective-permute-start(bf16[256,2304]{1,0:T(8,128)(2,1)} %collective-permute-done.18.refs_1_), channel_id=1, source_target_pairs={{0,4},{4,0},{8,12},{12,8},{16,20},{20,16},{24,28},{28,24},{1,5},{5... | collective-permute-start | bytes 3538952 | tf_op jit(solution)/shard_map/ppermute | solution.py:293
  (53 other events, 461.4 us)
Sparse Core Ops, SparseCore 0:
  25.0 38.7 all-gather.6
  65.9 62.3 all-gather.8
  130.5 35.7 all-gather.10
  168.4 59.1 reduce-scatter.2
  252.5 58.2 reduce-scatter.4

commit v6 on v3

--- a/solution.py
+++ b/solution.py
@@ -324,7 +324,7 @@
     near = dict(zip(keys, spread_own))
     near.update(spread({high: over_high}))
     near.update(spread({low: over_low}))
-    return near, spread({high | low: far})
+    return near, high | low, far, spread
 
 
 def columns_to_owner(turned, axis):
@@ -400,24 +400,26 @@
     normed_cols = columns_to_owner(normed, "dp")
 
     heads_out = attention(forward_kernel, projected, segment, qk_gain, (), 1)
+    heads_out, normed_cols = lax.optimization_barrier((heads_out, normed_cols))
     attn_part = expand(heads_out, w_out_t, parts, 1)
     attn_part, cot_two = lax.optimization_barrier((attn_part, cot_two))
     attn = lax.psum_scatter(attn_part, "mp", scatter_dimension=0, tiled=False)
     output = (packed.astype(jnp.float32) + attn.astype(jnp.float32)).astype(jnp.bfloat16).T
 
     d_heads_two = project(cot_two, w_out_t, jnp.bfloat16)
-    normed_cols, d_heads_two = lax.optimization_barrier((normed_cols, d_heads_two))
     d_all = attention(backward_kernel, projected, segment, qk_gain, (d_heads_one, d_heads_two), 4)
     d_part, sums = expand(d_all, w_t, parts, 2, gain_column, normed)
     d_normed = lax.psum_scatter(d_part, "mp", scatter_dimension=0, tiled=False)
     sums = sum(exchange_small(sums, "mp")) / full_width
     scale_grad = 1.0 / math.sqrt(group_rows * groups)
     columns = (normed_cols, cot_cols_one, columns_to_owner(cot_two, "dp"))
-    sums_near = None
-    near, far = gather_xor(d_all, "dp")
-    for held, scale in ((near, None), (far, scale_grad)):
-        keys = sorted(held)
-        sums_near = weight_grads(*columns, [held[key] for key in keys], keys, sums_near, scale)
+    near, far_key, far, spread = gather_xor(d_all, "dp")
+    keys = sorted(near)
+    sums_near = weight_grads(*columns, [near[key] for key in keys], keys, None, None)
+    far, sums_near = lax.optimization_barrier((far, sums_near))
+    far = spread({far_key: far})
+    keys = sorted(far)
+    sums_near = weight_grads(*columns, [far[key] for key in keys], keys, sums_near, scale_grad)
     d_normed, sums_near = lax.optimization_barrier((d_normed, sums_near))
     qkv_grad, out_grad = sums_near
 

time: 347 us -> 309 us (0.89)
  waiting for transfers between devices: 187 us -> 146 us
  starting transfers between devices: 34.8 us -> 38.6 us
    ppermute x19, waiting for transfers between devices: 55 us -> 29.1 us  [flip(): return lax.ppermute(values, axis, [(at, at ^ bit) for at in range(count)])]
    ppermute x1, waiting for transfers between devices: 23.3 us -> 1.77 us  [gather_xor(): far = lax.ppermute(onward, axis, pairs)]
    reduce_scatter x1, waiting for transfers between devices: 0.01 us -> 15.8 us  [shards(): d_normed = lax.psum_scatter(d_part, 'mp', scatter_dimension=0, tiled=False)]
    all_gather x1, waiting for transfers between devices: 10.3 us -> 0.01 us  [shards(): cot_two = lax.all_gather(late_cot, 'mp', axis=0, tiled=False)]
    unnamed x37 -> x43, local copies, waits for them, and re-layouts: 7.07 us -> 9.6 us
  transfers between devices with their start and end apart: 29 -> 29, of which waited for: 12 -> 11; matrix products, arithmetic and copies ran while one was open for 4% -> 4% of each run, Pallas kernels for 25% -> 27%
where the time goes in v6:
time: 309 us; the launch traced here: 308 us
  waiting for transfers between devices  146 us (47%)
  Pallas kernels  82.9 us (27%)
  starting transfers between devices  38.6 us (12%)
  between operations  14.3 us (5%)
  local copies, waits for them, and re-layouts  12.3 us (4%)
  other arithmetic  8.78 us (3%)
  matrix products  5.06 us (2%)
    all_to_all x3, waiting for transfers between devices, columns_to_owner(): return lax.all_to_all(cut, axis, 0, 0, tiled=True)  44.8 us
    all_gather x1, waiting for transfers between devices, shards(): normed = lax.all_gather(normed_part, 'mp', axis=0, tiled=False)  38.5 us
    pallas_call x3, Pallas kernels, project(): pl.pallas_call(functools.partial(project_kernel, steps, width), grid=(ste...  29.4 us
    ppermute x19, waiting for transfers between devices, flip(): return lax.ppermute(values, axis, [(at, at ^ bit) for at in range(count)])  29.1 us
    pallas_call x2, Pallas kernels, weight_grads(): pl.pallas_call(functools.partial(weight_kernel, keys, scale), grid=(4,),...  23.7 us
    pallas_call x2, Pallas kernels, expand(): pl.pallas_call(functools.partial(expand_kernel, kinds, width), grid=(part...  23.2 us
    ppermute x19, starting transfers between devices, flip(): return lax.ppermute(values, axis, [(at, at ^ bit) for at in range(count)])  19.9 us
    reduce_scatter x1, waiting for transfers between devices, shards(): d_normed = lax.psum_scatter(d_part, 'mp', scatter_dimension=0, tiled=False)  15.8 us
  transfers between devices with their start and end apart: 29, of which 11 were waited for; matrix products, arithmetic and copies ran while one was open for 4% of the time, Pallas kernels for 27%

profile of v6, /device:TPU:0, one launch (start us, length us, event | category | flops | bytes accessed | tf_op | source)
XLA Modules:
  0.0 307.5 jit_solution(11978823912010275214)
XLA Ops:
  8.8 2.9 convolution_convert_fusion
  12.2 5.1 %collective-permute-start.2 = (f32[2,256]{1,0:T(2,128)S(1)}, f32[2,256]{1,0:T(2,128)S(1)}, u32[]{:S(2)}, u32[]{:S(2)}) collective-permute-start(f32[2,256]{1,0:T(2,128)S(1)} %pad_maximum_fusion.1), channel_id=1, source_target_pairs={{0,3},{1,2},{2,1},{3,0},{4,7},{5,6},{6,5},{7,4},{8,11},{9,10},{10,... | collective-permute-start | bytes 6152 | tf_op jit(solution)/shard_map/ppermute | solution.py:295
  18.0 4.0 %all-to-all-start = ((bf16[8,64,1536]{2,1,0:T(8,128)(2,1)}), bf16[8,64,1536]{2,1,0:T(8,128)(2,1)S(1)}, u32[]{:S(2)}, u32[]{:S(2)}) async-start(bf16[8,64,1536]{2,1,0:T(8,128)(2,1)} %bitcast), calls=%async_computation | async-start | bytes 3145728 | tf_op jit(solution)/shard_map/all_to_all | solution.py:357
  30.8 11.8 %collective-permute-done.9 = f32[3,64]{1,0:T(4,128)S(1)} collective-permute-done((f32[3,64]{1,0:T(4,128)S(1)}, f32[3,64]{1,0:T(4,128)S(1)}, u32[]{:S(2)}, u32[]{:S(2)}) %collective-permute-start.9) | collective-permute-done | bytes 800 | tf_op jit(solution)/shard_map/ppermute | solution.py:295
  49.0 14.8 %all-gather.7.cloned.1.call-done = bf16[6144,128]{1,0:T(8,128)(2,1)} async-done(((bf16[1536,128]{1,0:T(8,128)(2,1)}), bf16[6144,128]{1,0:T(8,128)(2,1)}) %all-gather.7.cloned.1.call-update) | async-done | bytes 1572880 | tf_op jit(solution)/shard_map/all_gather | solution.py:349
  63.8 3.8 %all-to-all-start.1 = ((bf16[8,768,128]{2,1,0:T(8,128)(2,1)}), bf16[8,768,128]{2,1,0:T(8,128)(2,1)S(1)}, u32[]{:S(2)}, u32[]{:S(2)}) async-start(bf16[8,768,128]{2,1,0:T(8,128)(2,1)} %bitcast.58), calls=%async_computation.1 | async-start | bytes 3145728 | tf_op jit(solution)/shard_map/all_to_all | solution.py:334
  67.6 5.6 %shard_map.121.d_one_ref = bf16[128,768]{1,0:T(8,128)(2,1)S(1)} custom-call(bf16[4,1536,128]{2,1,0:T(8,128)(2,1)S(1)} %bitcast.59, bf16[1,6144,768]{2,1,0:T(8,128)(2,1)} %bitcast.65), custom_call_target="tpu_custom_call" | custom-call | flops 1207959552 | bytes 11010048 | tf_op jit(solution)/shard_map/pallas_call | solution.py:68
  73.3 15.4 %all-to-all-done.1.one_ref = bf16[8,768,128]{2,1,0:T(8,128)(2,1)S(1)} async-done(((bf16[8,768,128]{2,1,0:T(8,128)(2,1)}), bf16[8,768,128]{2,1,0:T(8,128)(2,1)S(1)}, u32[]{:S(2)}, u32[]{:S(2)}) %all-to-all-start.1) | async-done | bytes 1572896 | tf_op jit(solution)/shard_map/all_to_all | solution.py:334
  89.8 38.5 %all-gather.9.cloned.1.call-done = bf16[6144,256]{1,0:T(8,128)(2,1)} async-done(((bf16[1536,256]{1,0:T(8,128)(2,1)}), bf16[6144,256]{1,0:T(8,128)(2,1)}) %all-gather.9.cloned.1.call-update) | async-done | bytes 3145744 | tf_op jit(solution)/shard_map/all_gather | solution.py:392
  128.3 4.7 %all-to-all-start.2 = ((bf16[8,768,256]{2,1,0:T(8,128)(2,1)}), bf16[8,768,256]{2,1,0:T(8,128)(2,1)}, u32[]{:S(2)}, u32[]{:S(2)}) async-start(bf16[8,768,256]{2,1,0:T(8,128)(2,1)} %bitcast.55), calls=%async_computation.2 | async-start | bytes 6291456 | tf_op jit(solution)/shard_map/all_to_all | solution.py:334
  134.0 17.6 %shard_map.122.proj_ref = f32[256,2304]{1,0:T(8,128)S(1)} custom-call(bf16[4,1536,256]{2,1,0:T(8,128)(2,1)S(1)} %bitcast.57, bf16[3,6144,768]{2,1,0:T(8,128)(2,1)} %bitcast.63), custom_call_target="tpu_custom_call" | custom-call | flops 7247757312 | bytes 31457280 | tf_op jit(solution)/shard_map/pallas_call | solution.py:68
  154.7 16.3 %all-to-all-done.2.normed_ref = bf16[8,768,256]{2,1,0:T(8,128)(2,1)} async-done(((bf16[8,768,256]{2,1,0:T(8,128)(2,1)}), bf16[8,768,256]{2,1,0:T(8,128)(2,1)}, u32[]{:S(2)}, u32[]{:S(2)}) %all-to-all-start.2) | async-done | bytes 3145760 | tf_op jit(solution)/shard_map/all_to_all | solution.py:334
  171.0 7.3 %shard_map.124 = bf16[4,1536,256]{2,1,0:T(8,128)(2,1)} custom-call(bf16[256,768]{1,0:T(8,128)(2,1)S(1)} %shard_map.123.x_ref, bf16[1,6144,768]{2,1,0:T(8,128)(2,1)} %bitcast.66), custom_call_target="tpu_custom_call" | custom-call | flops 2415919104 | bytes 12582912 | tf_op jit(solution)/shard_map/pallas_call | solution.py:117
  180.7 6.2 %shard_map.125.d_two_ref = bf16[128,768]{1,0:T(8,128)(2,1)S(1)} custom-call(bf16[4,1536,128]{2,1,0:T(8,128)(2,1)} %bitcast.13.x_ref, bf16[1,6144,768]{2,1,0:T(8,128)(2,1)} %bitcast.67), custom_call_target="tpu_custom_call" | custom-call | flops 1207959552 | bytes 11010048 | tf_op jit(solution)/shard_map/pallas_call | solution.py:68
  187.0 4.1 %shard_map.126.x_ref.refs_0_ = bf16[256,3072]{1,0:T(8,128)(2,1)S(1)} custom-call(f32[256,2304]{1,0:T(8,128)S(1)} %copy-done.2, s32[256,1]{1,0:T(8,128)S(1)} %copy.22.row_ref, s32[1,256]{1,0:T(1,128)S(1)} %bitcast.62, f32[2,128]{1,0:T(2,128)S(1)} %copy-done.10, bf16[128,768]{1,0:T(8,128)(2,1)S(1)} %shard_map.121.d_one_ref, ...), custom_call_target="tpu_custom_call" | custom-call | flops 805306368 | bytes 4718592 | tf_op jit(solution)/shard_map/pallas_call | solution.py:209
  192.4 15.9 %shard_map.127 = (bf16[4,1536,256]{2,1,0:T(8,128)(2,1)S(1)}, f32[2,256]{1,0:T(2,128)S(1)}) custom-call(bf16[256,3072]{1,0:T(8,128)(2,1)S(1)} %shard_map.126.x_ref.refs_0_, bf16[3,6144,768]{2,1,0:T(8,128)(2,1)} %bitcast.64, f32[6144,1]{1,0:T(8,128)} %copy.25.refs_0_, bf16[4,1536,256]{2,1,0:T(8,128)(2,1)} %bitcast.56), custom_call_target="tpu_custom_call" | custom-call | flops 7247757312 | bytes 31457280 | tf_op jit(solution)/shard_map/pallas_call | solution.py:117
  210.0 4.5 %all-to-all-start.3 = ((bf16[8,768,128]{2,1,0:T(8,128)(2,1)}), bf16[8,768,128]{2,1,0:T(8,128)(2,1)}, u32[]{:S(2)}, u32[]{:S(2)}) async-start(bf16[8,768,128]{2,1,0:T(8,128)(2,1)} %bitcast.18), calls=%async_computation.5 | async-start | bytes 3145728 | tf_op jit(solution)/shard_map/all_to_all | solution.py:334
  214.5 14.0 %collective-permute-done.11.refs_4_ = bf16[256,3072]{1,0:T(8,128)(2,1)} collective-permute-done((bf16[256,3072]{1,0:T(8,128)(2,1)S(1)}, bf16[256,3072]{1,0:T(8,128)(2,1)}, u32[]{:S(2)}, u32[]{:S(2)}) %collective-permute-start.11) | collective-permute-done | bytes 1572896 | tf_op jit(solution)/shard_map/ppermute | solution.py:295
  229.8 2.7 broadcast_select_fusion
  233.8 13.2 %all-to-all-done.3.two_ref = bf16[8,768,128]{2,1,0:T(8,128)(2,1)} async-done(((bf16[8,768,128]{2,1,0:T(8,128)(2,1)}), bf16[8,768,128]{2,1,0:T(8,128)(2,1)}, u32[]{:S(2)}, u32[]{:S(2)}) %all-to-all-start.3) | async-done | bytes 1572896 | tf_op jit(solution)/shard_map/all_to_all | solution.py:334
  247.0 13.0 %shard_map.128.refs_2_ = f32[4,768,768]{2,1,0:T(8,128)} custom-call(bf16[8,768,256]{2,1,0:T(8,128)(2,1)} %all-to-all-done.2.normed_ref, bf16[8,768,128]{2,1,0:T(8,128)(2,1)S(1)} %copy-done.4, bf16[8,768,128]{2,1,0:T(8,128)(2,1)} %all-to-all-done.3.two_ref, bf16[256,3072]{1,0:T(8,128)(2,1)S(1)} %shard_map.126.x_ref.refs_0_, ...), custom_call_target="tpu_custom_call" | custom-call | flops 7247757312 | bytes 15728640 | tf_op jit(solution)/shard_map/pallas_call | solution.py:265
  263.3 3.5 %collective-permute-start.17 = (f32[2,256]{1,0:T(2,128)S(1)}, f32[2,256]{1,0:T(2,128)S(1)}, u32[]{:S(2)}, u32[]{:S(2)}) collective-permute-start(f32[2,256]{1,0:T(2,128)S(1)} %get-tuple-element.53), channel_id=1, source_target_pairs={{0,1},{1,0},{2,3},{3,2},{4,5},{5,4},{6,7},{7,6},{8,9},{9,8},{10,11... | collective-permute-start | bytes 6152 | tf_op jit(solution)/shard_map/ppermute | solution.py:295
  269.2 10.7 %shard_map.129 = (bf16[3,768,768]{2,1,0:T(8,128)(2,1)}, bf16[768,768]{1,0:T(8,128)(2,1)}) custom-call(bf16[8,768,256]{2,1,0:T(8,128)(2,1)} %all-to-all-done.2.normed_ref, bf16[8,768,128]{2,1,0:T(8,128)(2,1)S(1)} %copy-done.4, bf16[8,768,128]{2,1,0:T(8,128)(2,1)} %all-to-all-done.3.two_ref, bf16[256,3072]{1,0:T(8,128)(2,1)} %collective-permute-done.13.refs_0_, ...), custom_call_target="tpu_custom_call" | custom-call | flops 2415919104 | bytes 9437184 | tf_op jit(solution)/shard_map/pallas_call | solution.py:265
  282.3 15.8 %reduce-scatter.5.cloned.1.call-done = bf16[1,1536,256]{2,1,0:T(8,128)(2,1)} async-done(((bf16[4,1536,256]{2,1,0:T(8,128)(2,1)}), bf16[1,1536,256]{2,1,0:T(8,128)(2,1)}) %reduce-scatter.5.cloned.1.call-update) | async-done | bytes 786448 | tf_op jit(solution)/shard_map/reduce_scatter | solution.py:412
  (126 shorter events, 41.8 us)
Async XLA Ops:
  12.2 11.8 %collective-permute-start.2 = (f32[2,256]{1,0:T(2,128)S(1)}, f32[2,256]{1,0:T(2,128)S(1)}, u32[]{:S(2)}, u32[]{:S(2)}) collective-permute-start(f32[2,256]{1,0:T(2,128)S(1)} %pad_maximum_fusion.1), channel_id=1, source_target_pairs={{0,3},{1,2},{2,1},{3,0},{4,7},{5,6},{6,5},{7,4},{8,11},{9,10},{10,... | collective-permute-start | bytes 6152 | tf_op jit(solution)/shard_map/ppermute | solution.py:295
  17.3 6.7 %collective-permute-start.1 = (f32[2,256]{1,0:T(2,128)S(1)}, f32[2,256]{1,0:T(2,128)S(1)}, u32[]{:S(2)}, u32[]{:S(2)}) collective-permute-start(f32[2,256]{1,0:T(2,128)S(1)} %pad_maximum_fusion.1), channel_id=1, source_target_pairs={{0,2},{1,3},{2,0},{3,1},{4,6},{5,7},{6,4},{7,5},{8,10},{9,11},{10,... | collective-permute-start | bytes 6152 | tf_op jit(solution)/shard_map/ppermute | solution.py:295
  17.3 6.7 %collective-permute-start = (f32[2,256]{1,0:T(2,128)S(1)}, f32[2,256]{1,0:T(2,128)S(1)}, u32[]{:S(2)}, u32[]{:S(2)}) collective-permute-start(f32[2,256]{1,0:T(2,128)S(1)} %pad_maximum_fusion.1), channel_id=1, source_target_pairs={{0,1},{1,0},{2,3},{3,2},{4,5},{5,4},{6,7},{7,6},{8,9},{9,8},{10,11... | collective-permute-start | bytes 6152 | tf_op jit(solution)/shard_map/ppermute | solution.py:295
  18.0 28.8 %all-to-all-start = ((bf16[8,64,1536]{2,1,0:T(8,128)(2,1)}), bf16[8,64,1536]{2,1,0:T(8,128)(2,1)S(1)}, u32[]{:S(2)}, u32[]{:S(2)}) async-start(bf16[8,64,1536]{2,1,0:T(8,128)(2,1)} %bitcast), calls=%async_computation | async-start | bytes 3145728 | tf_op jit(solution)/shard_map/all_to_all | solution.py:357
  22.0 41.8 %all-gather.7.cloned.1.call-start = ((), (), s32[]{:S(2)}) async-start(), calls=%async_computation.8 | async-start | bytes 1966080 | tf_op jit(solution)/shard_map/all_gather | solution.py:349
  23.7 104.6 %all-gather.9.cloned.1.call-start = ((), (), s32[]{:S(2)}) async-start(), calls=%async_computation.9 | async-start | bytes 3932160 | tf_op jit(solution)/shard_map/all_gather | solution.py:392
  24.6 18.0 %collective-permute-start.9 = (f32[3,64]{1,0:T(4,128)S(1)}, f32[3,64]{1,0:T(4,128)S(1)}, u32[]{:S(2)}, u32[]{:S(2)}) collective-permute-start(f32[3,64]{1,0:T(4,128)S(1)} %bitcast.85), channel_id=1, source_target_pairs={{0,28},{4,24},{8,20},{12,16},{16,12},{20,8},{24,4},{28,0},{1,29},{... | collective-permute-start | bytes 2312 | tf_op jit(solution)/shard_map/ppermute | solution.py:295
  27.2 15.9 %collective-permute-start.8 = (f32[3,64]{1,0:T(4,128)S(1)}, f32[3,64]{1,0:T(4,128)S(1)}, u32[]{:S(2)}, u32[]{:S(2)}) collective-permute-start(f32[3,64]{1,0:T(4,128)S(1)} %bitcast.84), channel_id=1, source_target_pairs={{0,24},{4,28},{8,16},{12,20},{16,8},{20,12},{24,0},{28,4},{1,25},{... | collective-permute-start | bytes 2312 | tf_op jit(solution)/shard_map/ppermute | solution.py:295
  27.6 16.1 %collective-permute-start.7 = (f32[3,64]{1,0:T(4,128)S(1)}, f32[3,64]{1,0:T(4,128)S(1)}, u32[]{:S(2)}, u32[]{:S(2)}) collective-permute-start(f32[3,64]{1,0:T(4,128)S(1)} %bitcast.79), channel_id=1, source_target_pairs={{0,20},{4,16},{8,28},{12,24},{16,4},{20,0},{24,12},{28,8},{1,21},{... | collective-permute-start | bytes 2312 | tf_op jit(solution)/shard_map/ppermute | solution.py:295
  29.0 14.8 %collective-permute-start.6 = (f32[3,64]{1,0:T(4,128)S(1)}, f32[3,64]{1,0:T(4,128)S(1)}, u32[]{:S(2)}, u32[]{:S(2)}) collective-permute-start(f32[3,64]{1,0:T(4,128)S(1)} %bitcast.80), channel_id=1, source_target_pairs={{0,16},{4,20},{8,24},{12,28},{16,0},{20,4},{24,8},{28,12},{1,17},{... | collective-permute-start | bytes 2312 | tf_op jit(solution)/shard_map/ppermute | solution.py:295
  29.3 14.4 %collective-permute-start.5 = (f32[3,64]{1,0:T(4,128)S(1)}, f32[3,64]{1,0:T(4,128)S(1)}, u32[]{:S(2)}, u32[]{:S(2)}) collective-permute-start(f32[3,64]{1,0:T(4,128)S(1)} %bitcast.81), channel_id=1, source_target_pairs={{0,12},{4,8},{8,4},{12,0},{16,28},{20,24},{24,20},{28,16},{1,13},{... | collective-permute-start | bytes 2312 | tf_op jit(solution)/shard_map/ppermute | solution.py:295
  63.8 24.8 %all-to-all-start.1 = ((bf16[8,768,128]{2,1,0:T(8,128)(2,1)}), bf16[8,768,128]{2,1,0:T(8,128)(2,1)S(1)}, u32[]{:S(2)}, u32[]{:S(2)}) async-start(bf16[8,768,128]{2,1,0:T(8,128)(2,1)} %bitcast.58), calls=%async_computation.1 | async-start | bytes 3145728 | tf_op jit(solution)/shard_map/all_to_all | solution.py:334
  128.3 42.6 %all-to-all-start.2 = ((bf16[8,768,256]{2,1,0:T(8,128)(2,1)}), bf16[8,768,256]{2,1,0:T(8,128)(2,1)}, u32[]{:S(2)}, u32[]{:S(2)}) async-start(bf16[8,768,256]{2,1,0:T(8,128)(2,1)} %bitcast.55), calls=%async_computation.2 | async-start | bytes 6291456 | tf_op jit(solution)/shard_map/all_to_all | solution.py:334
  133.1 45.2 %all-gather.11.cloned.1.call-start = ((), (), s32[]{:S(2)}) async-start(), calls=%async_computation.10 | async-start | bytes 1966080 | tf_op jit(solution)/shard_map/all_gather | solution.py:398
  133.8 146.0 %reduce-scatter.3.cloned.1.call-start = ((), (), s32[]{:S(2)}) async-start(), calls=%async_computation.6 | async-start | bytes 3932160 | tf_op jit(solution)/shard_map/reduce_scatter | solution.py:406
  178.3 119.8 %reduce-scatter.5.cloned.1.call-start = ((), (), s32[]{:S(2)}) async-start(), calls=%async_computation.7 | async-start | bytes 3932160 | tf_op jit(solution)/shard_map/reduce_scatter | solution.py:412
  191.1 23.4 %collective-permute-start.10 = (bf16[256,3072]{1,0:T(8,128)(2,1)S(1)}, bf16[256,3072]{1,0:T(8,128)(2,1)}, u32[]{:S(2)}, u32[]{:S(2)}) collective-permute-start(bf16[256,3072]{1,0:T(8,128)(2,1)S(1)} %shard_map.126.x_ref.refs_0_), channel_id=1, source_target_pairs={{0,4},{4,0},{8,12},{12,8},{16,20},{20,16},{24,28},{28,24},{1,5},{5... | collective-permute-start | bytes 4718600 | tf_op jit(solution)/shard_map/ppermute | solution.py:295
  191.2 37.4 %collective-permute-start.11 = (bf16[256,3072]{1,0:T(8,128)(2,1)S(1)}, bf16[256,3072]{1,0:T(8,128)(2,1)}, u32[]{:S(2)}, u32[]{:S(2)}) collective-permute-start(bf16[256,3072]{1,0:T(8,128)(2,1)S(1)} %shard_map.126.x_ref.refs_0_), channel_id=1, source_target_pairs={{0,16},{4,20},{8,24},{12,28},{16,0},{20,4},{24,8},{28,12},{1,17},{... | collective-permute-start | bytes 4718600 | tf_op jit(solution)/shard_map/ppermute | solution.py:295
  192.0 37.3 %collective-permute-start.12 = (bf16[256,3072]{1,0:T(8,128)(2,1)S(1)}, bf16[256,3072]{1,0:T(8,128)(2,1)}, u32[]{:S(2)}, u32[]{:S(2)}) collective-permute-start(bf16[256,3072]{1,0:T(8,128)(2,1)S(1)} %shard_map.126.x_ref.refs_0_), channel_id=1, source_target_pairs={{0,8},{4,12},{8,0},{12,4},{16,24},{20,28},{24,16},{28,20},{1,9},{5... | collective-permute-start | bytes 4718600 | tf_op jit(solution)/shard_map/ppermute | solution.py:295
  210.0 37.0 %all-to-all-start.3 = ((bf16[8,768,128]{2,1,0:T(8,128)(2,1)}), bf16[8,768,128]{2,1,0:T(8,128)(2,1)}, u32[]{:S(2)}, u32[]{:S(2)}) async-start(bf16[8,768,128]{2,1,0:T(8,128)(2,1)} %bitcast.18), calls=%async_computation.5 | async-start | bytes 3145728 | tf_op jit(solution)/shard_map/all_to_all | solution.py:334
  229.3 17.7 %collective-permute-start.14 = (bf16[256,3072]{1,0:T(8,128)(2,1)}, bf16[256,3072]{1,0:T(8,128)(2,1)}, u32[]{:S(2)}, u32[]{:S(2)}) collective-permute-start(bf16[256,3072]{1,0:T(8,128)(2,1)} %collective-permute-done.12.refs_2_), channel_id=1, source_target_pairs={{0,4},{4,0},{8,12},{12,8},{16,20},{20,16},{24,28},{28,24},{1,5},{5... | collective-permute-start | bytes 4718600 | tf_op jit(solution)/shard_map/ppermute | solution.py:295
  229.3 17.7 %collective-permute-start.15 = (bf16[256,3072]{1,0:T(8,128)(2,1)}, bf16[256,3072]{1,0:T(8,128)(2,1)}, u32[]{:S(2)}, u32[]{:S(2)}) collective-permute-start(bf16[256,3072]{1,0:T(8,128)(2,1)} %collective-permute-done.11.refs_4_), channel_id=1, source_target_pairs={{0,4},{4,0},{8,12},{12,8},{16,20},{20,16},{24,28},{28,24},{1,5},{5... | collective-permute-start | bytes 4718600 | tf_op jit(solution)/shard_map/ppermute | solution.py:295
  232.5 29.2 %collective-permute-start.13 = (bf16[256,3072]{1,0:T(8,128)(2,1)}, bf16[256,3072]{1,0:T(8,128)(2,1)}, u32[]{:S(2)}, u32[]{:S(2)}) collective-permute-start(bf16[256,3072]{1,0:T(8,128)(2,1)} %broadcast_select_fusion), channel_id=1, source_target_pairs={{0,16},{4,12},{8,24},{12,4},{16,0},{20,28},{24,8},{28,20},{1,17},{... | collective-permute-start | bytes 4718600 | tf_op jit(solution)/shard_map/ppermute | solution.py:323
  261.8 7.4 %collective-permute-start.16 = (bf16[256,3072]{1,0:T(8,128)(2,1)}, bf16[256,3072]{1,0:T(8,128)(2,1)}, u32[]{:S(2)}, u32[]{:S(2)}) collective-permute-start(bf16[256,3072]{1,0:T(8,128)(2,1)} %collective-permute-done.13.refs_0_), channel_id=1, source_target_pairs={{0,4},{4,0},{8,12},{12,8},{16,20},{20,16},{24,28},{28,24},{1,5},{5... | collective-permute-start | bytes 4718600 | tf_op jit(solution)/shard_map/ppermute | solution.py:295
  (21 other events, 165.1 us)
Sparse Core Ops, SparseCore 0:
  25.0 38.7 all-gather.6
  65.9 62.3 all-gather.8
  136.1 36.1 all-gather.10
  178.4 57.1 reduce-scatter.2
  237.7 60.3 reduce-scatter.4

commit v7 on v6

--- a/solution.py
+++ b/solution.py
@@ -22,21 +22,58 @@
     return pltpu.CompilerParams(vmem_limit_bytes=VMEM_BYTES)
 
 
-def turn_kernel(x_ref, one_ref, two_ref):
-    half = one_ref.shape[1]
-    one_ref[...] = x_ref[:half, :].T
-    two_ref[...] = x_ref[half:, :].T
-
-
-def turn_halves(x):
+def turn_kernel(x_ref, out_ref):
+    out_ref[...] = x_ref[...].T
+
+
+def turn(x):
     rows, part = x.shape
-    shape = jax.ShapeDtypeStruct((part, rows // 2), x.dtype)
     return pl.pallas_call(
         turn_kernel,
-        out_shape=[shape, shape],
+        out_shape=jax.ShapeDtypeStruct((part, rows), x.dtype),
         compiler_params=params(),
         cost_estimate=pl.CostEstimate(flops=0, bytes_accessed=4 * rows * part, transcendentals=0),
     )(x)
+
+
+def add_block_kernel(first, at_ref, x_ref, w_ref, *refs):
+    out_ref, block = refs[-2:]
+
+    @pl.when(pl.program_id(0) == 0)
+    def _():
+        block[...] = x_ref[...].T
+
+    term = jnp.dot(block[...], w_ref[0], preferred_element_type=jnp.float32)
+    out_ref[...] = term if first else refs[0][...] + term
+
+
+def add_block(total, x, w, at):
+    part, rows = x.shape
+    kinds, _, width = w.shape
+    sums = pl.BlockSpec((rows, width), lambda t, at_ref: (0, t))
+    before = [] if total is None else [total]
+    return pl.pallas_call(
+        functools.partial(add_block_kernel, total is None),
+        grid_spec=pltpu.PrefetchScalarGridSpec(
+            num_scalar_prefetch=1,
+            grid=(kinds,),
+            in_specs=[
+                pl.BlockSpec((part, rows), lambda t, at_ref: (0, 0)),
+                pl.BlockSpec((1, part, width), lambda t, at_ref: (t, at_ref[0], 0)),
+            ]
+            + [sums] * len(before),
+            out_specs=sums,
+            scratch_shapes=[pltpu.VMEM((rows, part), jnp.bfloat16)],
+        ),
+        out_shape=jax.ShapeDtypeStruct((rows, kinds * width), jnp.float32),
+        input_output_aliases={} if total is None else {3: 0},
+        compiler_params=params(),
+        cost_estimate=pl.CostEstimate(
+            flops=2 * rows * part * kinds * width,
+            bytes_accessed=2 * kinds * part * width + 8 * rows * kinds * width,
+            transcendentals=0,
+        ),
+    )(at.reshape(1).astype(jnp.int32), x, w, *before)
 
 
 def project_kernel(steps, width, x_ref, w_ref, out_ref, total, block):
@@ -176,7 +213,7 @@
     )
 
 
-def backward_kernel(heads, proj_ref, row_ref, col_ref, gain_ref, d_one_ref, d_two_ref, out_ref):
+def backward_kernel(heads, proj_ref, row_ref, col_ref, gain_ref, d_ref, out_ref):
     same = row_ref[...] == col_ref[...]
     width = heads * DH
     for head in range(heads):
@@ -185,7 +222,7 @@
         )
         at = head * DH
         weights_bf = weights.astype(jnp.bfloat16)
-        d_out = jnp.concatenate([d_one_ref[:, at : at + DH], d_two_ref[:, at : at + DH]], 0)
+        d_out = d_ref[:, at : at + DH]
         mixed = dot_f32(weights_bf, values, (1,), (0,))
         out_ref[:, 3 * width + at : 3 * width + at + DH] = mixed.astype(jnp.bfloat16)
         d_values = dot_f32(weights_bf, d_out, (0,), (0,))
@@ -218,7 +255,7 @@
     )(projected, segment.reshape(rows, 1), segment.reshape(1, rows), qk_gain, *extra)
 
 
-def weight_kernel(keys, scale, normed_ref, one_ref, two_ref, *refs):
+def weight_kernel(keys, scale, normed_ref, cot_ref, *refs):
     b_refs, refs = refs[: len(keys)], refs[len(keys) :]
     me, t = lax.axis_index("dp"), pl.program_id(0)
 
@@ -234,7 +271,7 @@
         return normed_ref[at]
 
     def cot(at):
-        return jnp.concatenate([one_ref[at], two_ref[at]], 1)
+        return cot_ref[at]
 
     if scale is None:
         total = refs[0].at[0]
@@ -255,17 +292,16 @@
             out_ref[...] = (total[...] * scale).astype(jnp.bfloat16)
 
 
-def weight_grads(normed_cols, cot_one, cot_two, gathered, keys, before, scale):
+def weight_grads(normed_cols, cot_cols, gathered, keys, before, scale):
     count, depth, rows = normed_cols.shape
     width = gathered[0].shape[1] // 4
     whole = pl.BlockSpec((count, depth, rows), lambda t: (0, 0, 0))
-    half = pl.BlockSpec((count, depth, rows // 2), lambda t: (0, 0, 0))
     sums = pl.BlockSpec((1, depth, width), lambda t: (t, 0, 0))
     sums_shape = jax.ShapeDtypeStruct((4, depth, width), jnp.float32)
     return pl.pallas_call(
         functools.partial(weight_kernel, keys, scale),
         grid=(4,),
-        in_specs=[whole, half, half]
+        in_specs=[whole, whole]
         + [pl.BlockSpec((rows, width), lambda t: (0, t))] * len(keys)
         + ([] if before is None else [sums]),
         out_specs=sums
@@ -287,7 +323,7 @@
             bytes_accessed=4 * count * depth * rows + 8 * len(keys) * rows * width,
             transcendentals=0,
         ),
-    )(normed_cols, cot_one, cot_two, *gathered, *([] if before is None else [before]))
+    )(normed_cols, cot_cols, *gathered, *([] if before is None else [before]))
 
 
 def flip(values, axis, bit):
@@ -327,6 +363,25 @@
     return near, high | low, far, spread
 
 
+def line_blocks(values, axis, beside):
+    count, me = lax.axis_size(axis), lax.axis_index(axis)
+    blocks = [(me, None, values)]
+    right = left = values
+    for step in range(1, count):
+        right = lax.ppermute(right, axis, [(at, at + 1) for at in range(step - 1, count - 1)])
+        left = lax.ppermute(left, axis, [(at, at - 1) for at in range(1, count - step + 1)])
+        if step == 1:
+            right, left, beside = lax.optimization_barrier((right, left, beside))
+        over, under = me >= step, me + step < count
+        if 2 * step >= count:
+            at = jnp.where(over, me - step, jnp.minimum(me + step, count - 1))
+            blocks.append((at, over | under, right + left))
+        else:
+            blocks.append((jnp.maximum(me - step, 0), over, right))
+            blocks.append((jnp.minimum(me + step, count - 1), under, left))
+    return blocks, beside
+
+
 def columns_to_owner(turned, axis):
     count = lax.axis_size(axis)
     parts, part, rows = turned.shape
@@ -345,8 +400,7 @@
     w_t = jnp.transpose(w_qkv, (1, 0, 2))
     w_out_t = w_out[None]
 
-    first_cot, second_cot = turn_halves(cotangent)
-    cot_one = lax.all_gather(first_cot, "mp", axis=0, tiled=False)
+    whole_cot = lax.all_gather(turn(cotangent), "mp", axis=0, tiled=False)
 
     position = jnp.arange(group_rows, dtype=jnp.int32)
     earlier = (dest_group[:, None] == dest_group[None, :]) & (position[None, :] < position[:, None])
@@ -388,31 +442,35 @@
     unit_rows = (packed.astype(jnp.float32) - mean) * rstd
     normed_part = (unit_rows * my_gain).astype(jnp.bfloat16)
 
-    normed_part, cot_one = lax.optimization_barrier((normed_part, cot_one))
-    normed = lax.all_gather(normed_part, "mp", axis=0, tiled=False)
-    d_heads_one = project(cot_one, w_out_t, jnp.bfloat16)
-    cot_cols_one = columns_to_owner(cot_one, "dp")
-    normed, d_heads_one, cot_cols_one, late_cot = lax.optimization_barrier(
-        (normed, d_heads_one, cot_cols_one, second_cot)
-    )
-    cot_two = lax.all_gather(late_cot, "mp", axis=0, tiled=False)
-    projected = project(normed, w_t, jnp.float32)
+    blocks, whole_cot = line_blocks(normed_part, "mp", whole_cot)
+    d_heads = project(whole_cot, w_out_t, jnp.bfloat16)
+    cot_cols = columns_to_owner(whole_cot, "dp")
+    projected = None
+    normed = jnp.zeros((parts, part_width, group_rows), jnp.bfloat16)
+    for order, (at, there, block) in enumerate(blocks):
+        if order == len(blocks) - 1:
+            block, cot_cols, d_heads, projected = lax.optimization_barrier(
+                (block, cot_cols, d_heads, projected)
+            )
+        projected = add_block(projected, block, w_t, at)
+        if there is not None:
+            at, block = jnp.where(there, at, my_index), jnp.where(there, block, normed_part)
+        normed = lax.dynamic_update_slice(normed, block[None], (at, 0, 0))
     normed_cols = columns_to_owner(normed, "dp")
 
     heads_out = attention(forward_kernel, projected, segment, qk_gain, (), 1)
-    heads_out, normed_cols = lax.optimization_barrier((heads_out, normed_cols))
     attn_part = expand(heads_out, w_out_t, parts, 1)
-    attn_part, cot_two = lax.optimization_barrier((attn_part, cot_two))
+    attn_part, d_heads = lax.optimization_barrier((attn_part, d_heads))
     attn = lax.psum_scatter(attn_part, "mp", scatter_dimension=0, tiled=False)
     output = (packed.astype(jnp.float32) + attn.astype(jnp.float32)).astype(jnp.bfloat16).T
 
-    d_heads_two = project(cot_two, w_out_t, jnp.bfloat16)
-    d_all = attention(backward_kernel, projected, segment, qk_gain, (d_heads_one, d_heads_two), 4)
-    d_part, sums = expand(d_all, w_t, parts, 2, gain_column, normed)
+    d_all = attention(backward_kernel, projected, segment, qk_gain, (d_heads,), 4)
+    late_all, normed_cols = lax.optimization_barrier((d_all, normed_cols))
+    d_part, sums = expand(late_all, w_t, parts, 2, gain_column, normed)
     d_normed = lax.psum_scatter(d_part, "mp", scatter_dimension=0, tiled=False)
     sums = sum(exchange_small(sums, "mp")) / full_width
     scale_grad = 1.0 / math.sqrt(group_rows * groups)
-    columns = (normed_cols, cot_cols_one, columns_to_owner(cot_two, "dp"))
+    columns = (normed_cols, cot_cols)
     near, far_key, far, spread = gather_xor(d_all, "dp")
     keys = sorted(near)
     sums_near = weight_grads(*columns, [near[key] for key in keys], keys, None, None)

time: 309 us -> 297 us (0.961)
  waiting for transfers between devices: 146 us -> 117 us
  Pallas kernels: 82.9 us -> 90.2 us
  starting transfers between devices: 38.6 us -> 45.6 us
    all_gather x3 -> x1, waiting for transfers between devices: 53.3 us -> 0.01 us  [shards(): whole_cot = lax.all_gather(turn(cotangent), 'mp', axis=0, tiled=False)]
    ppermute x0 -> x6, waiting for transfers between devices: none -> 53 us  [the longest x3 32.9 us: line_blocks(): lax.ppermute(right, axis, [(at, at + 1) for at in range(step - 1, count -...]
    pallas_call x1 -> x6, Pallas kernels: 0.9 us -> 29.2 us  [the longest x5 28 us: add_block(): pl.pallas_call(functools.partial(add_block_kernel, total is None), grid_s...]
    pallas_call x3 -> x1, Pallas kernels: 29.4 us -> 6.25 us  [project(): pl.pallas_call(functools.partial(project_kernel, steps, width), grid=(ste...]
    all_to_all x3 -> x2, waiting for transfers between devices: 44.8 us -> 27.2 us  [columns_to_owner(): return lax.all_to_all(cut, axis, 0, 0, tiled=True)]
    reduce_scatter x1, waiting for transfers between devices: 15.8 us -> 0.67 us  [shards(): d_normed = lax.psum_scatter(d_part, 'mp', scatter_dimension=0, tiled=False)]
    ppermute x0 -> x6, starting transfers between devices: none -> 8.65 us  [the longest x3 4.61 us: line_blocks(): lax.ppermute(right, axis, [(at, at + 1) for at in range(step - 1, count -...]
    ppermute x19, waiting for transfers between devices: 29.1 us -> 36 us  [flip(): return lax.ppermute(values, axis, [(at, at ^ bit) for at in range(count)])]
  transfers between devices with their start and end apart: 29 -> 32, of which waited for: 11 -> 13; matrix products, arithmetic and copies ran while one was open for 4% -> 6% of each run, Pallas kernels for 27% -> 26%
where the time goes in v7:
time: 297 us; the launch traced here: 296 us
  waiting for transfers between devices  117 us (39%)
  Pallas kernels  90.2 us (30%)
  starting transfers between devices  45.6 us (15%)
  local copies, waits for them, and re-layouts  15 us (5%)
  between operations  14.4 us (5%)
  other arithmetic  10.1 us (3%)
  matrix products  3.7 us (1%)
    ppermute x19, waiting for transfers between devices, flip(): return lax.ppermute(values, axis, [(at, at ^ bit) for at in range(count)])  36 us
    ppermute x3, waiting for transfers between devices, line_blocks(): lax.ppermute(right, axis, [(at, at + 1) for at in range(step - 1, count -...  32.9 us
    pallas_call x5, Pallas kernels, add_block(): pl.pallas_call(functools.partial(add_block_kernel, total is None), grid_s...  28 us
    all_to_all x2, waiting for transfers between devices, columns_to_owner(): return lax.all_to_all(cut, axis, 0, 0, tiled=True)  27.2 us
    pallas_call x2, Pallas kernels, weight_grads(): pl.pallas_call(functools.partial(weight_kernel, keys, scale), grid=(4,),...  24.2 us
    pallas_call x2, Pallas kernels, expand(): pl.pallas_call(functools.partial(expand_kernel, kinds, width), grid=(part...  23.5 us
    ppermute x19, starting transfers between devices, flip(): return lax.ppermute(values, axis, [(at, at ^ bit) for at in range(count)])  21.7 us
    ppermute x3, waiting for transfers between devices, line_blocks(): lax.ppermute(left, axis, [(at, at - 1) for at in range(1, count - step +...  20.1 us
  transfers between devices with their start and end apart: 32, of which 13 were waited for; matrix products, arithmetic and copies ran while one was open for 6% of the time, Pallas kernels for 26%

profile of v7, /device:TPU:0, one launch (start us, length us, event | category | flops | bytes accessed | tf_op | source)
XLA Modules:
  0.0 296.0 jit_solution(13519081665394455242)
XLA Ops:
  12.0 5.1 %collective-permute-start.2 = (f32[2,256]{1,0:T(2,128)S(1)}, f32[2,256]{1,0:T(2,128)S(1)}, u32[]{:S(2)}, u32[]{:S(2)}) collective-permute-start(f32[2,256]{1,0:T(2,128)S(1)} %pad_maximum_fusion.1), channel_id=1, source_target_pairs={{0,3},{1,2},{2,1},{3,0},{4,7},{5,6},{6,5},{7,4},{8,11},{9,10},{10,... | collective-permute-start | bytes 6152 | tf_op jit(solution)/shard_map/ppermute | solution.py:331
  17.8 4.0 %all-to-all-start = ((bf16[8,64,1536]{2,1,0:T(8,128)(2,1)}), bf16[8,64,1536]{2,1,0:T(8,128)(2,1)S(1)}, u32[]{:S(2)}, u32[]{:S(2)}) async-start(bf16[8,64,1536]{2,1,0:T(8,128)(2,1)} %bitcast), calls=%async_computation | async-start | bytes 3145728 | tf_op jit(solution)/shard_map/all_to_all | solution.py:411
  28.8 13.6 %collective-permute-done.9 = f32[3,64]{1,0:T(4,128)S(1)} collective-permute-done((f32[3,64]{1,0:T(4,128)S(1)}, f32[3,64]{1,0:T(4,128)S(1)}, u32[]{:S(2)}, u32[]{:S(2)}) %collective-permute-start.9) | collective-permute-done | bytes 800 | tf_op jit(solution)/shard_map/ppermute | solution.py:331
  53.6 32.9 %collective-permute-done.10.x_ref = bf16[1536,256]{1,0:T(8,128)(2,1)S(1)} collective-permute-done((bf16[1536,256]{1,0:T(8,128)(2,1)S(1)}, bf16[1536,256]{1,0:T(8,128)(2,1)S(1)}, u32[]{:S(2)}, u32[]{:S(2)}) %collective-permute-start.10) | collective-permute-done | bytes 786464 | tf_op jit(solution)/shard_map/ppermute | solution.py:371
  87.4 3.7 %collective-permute-done.11.x_ref = bf16[1536,256]{1,0:T(8,128)(2,1)} collective-permute-done((bf16[1536,256]{1,0:T(8,128)(2,1)S(1)}, bf16[1536,256]{1,0:T(8,128)(2,1)}, u32[]{:S(2)}, u32[]{:S(2)}) %collective-permute-start.11) | collective-permute-done | bytes 786464 | tf_op jit(solution)/shard_map/ppermute | solution.py:372
  91.1 4.6 %all-to-all-start.1 = ((bf16[8,768,256]{2,1,0:T(8,128)(2,1)}), bf16[8,768,256]{2,1,0:T(8,128)(2,1)}, u32[]{:S(2)}, u32[]{:S(2)}) async-start(bf16[8,768,256]{2,1,0:T(8,128)(2,1)} %bitcast.67), calls=%async_computation.1 | async-start | bytes 6291456 | tf_op jit(solution)/shard_map/all_to_all | solution.py:389
  96.6 5.4 %shard_map.122.refs_0_ = f32[256,2304]{1,0:T(8,128)S(1)} custom-call(s32[1]{0:T(128)} %bitcast.13.at_ref, bf16[1536,256]{1,0:T(8,128)(2,1)S(1)} %get-tuple-element.71.x_ref, bf16[3,6144,768]{2,1,0:T(8,128)(2,1)} %bitcast.72), custom_call_target="tpu_custom_call" | custom-call | flops 1811939328 | bytes 11796480 | tf_op jit(solution)/shard_map/pallas_call | solution.py:55
  104.3 5.4 %shard_map.123.refs_0_ = f32[256,2304]{1,0:T(8,128)S(1)} custom-call(s32[1]{0:T(128)} %bitcast.12.at_ref, bf16[1536,256]{1,0:T(8,128)(2,1)S(1)} %copy-done.6, bf16[3,6144,768]{2,1,0:T(8,128)(2,1)} %bitcast.73, f32[256,2304]{1,0:T(8,128)S(1)} %shard_map.122.refs_0_), custom_call_target="tpu_custom_call", output_to_operand_aliasing={{}: (3, {})} | custom-call | flops 1811939328 | bytes 11796480 | tf_op jit(solution)/shard_map/pallas_call | solution.py:55
  109.7 6.3 %shard_map.121.d_ref = bf16[256,768]{1,0:T(8,128)(2,1)S(1)} custom-call(bf16[4,1536,256]{2,1,0:T(8,128)(2,1)S(1)} %bitcast.68, bf16[1,6144,768]{2,1,0:T(8,128)(2,1)} %bitcast.78), custom_call_target="tpu_custom_call" | custom-call | flops 2415919104 | bytes 12582912 | tf_op jit(solution)/shard_map/pallas_call | solution.py:105
  118.0 9.4 %collective-permute-done.14 = bf16[1536,256]{1,0:T(8,128)(2,1)S(1)} collective-permute-done((bf16[1536,256]{1,0:T(8,128)(2,1)}, bf16[1536,256]{1,0:T(8,128)(2,1)S(1)}, u32[]{:S(2)}, u32[]{:S(2)}) %collective-permute-start.14) | collective-permute-done | bytes 786464 | tf_op jit(solution)/shard_map/ppermute | solution.py:372
  128.9 5.5 %shard_map.124.refs_0_ = f32[256,2304]{1,0:T(8,128)S(1)} custom-call(s32[1]{0:T(128)} %bitcast.11.at_ref, bf16[1536,256]{1,0:T(8,128)(2,1)} %collective-permute-done.11.x_ref, bf16[3,6144,768]{2,1,0:T(8,128)(2,1)} %bitcast.74, f32[256,2304]{1,0:T(8,128)S(1)} %shard_map.123.refs_0_), custom_call_target="tpu_custom_call", output_to_operand_aliasing={{}: (3, {})} | custom-call | flops 1811939328 | bytes 11796480 | tf_op jit(solution)/shard_map/pallas_call | solution.py:55
  134.8 6.4 %shard_map.125.refs_0_ = f32[256,2304]{1,0:T(8,128)S(1)} custom-call(s32[1]{0:T(128)} %bitcast.9.at_ref, bf16[1536,256]{1,0:T(8,128)(2,1)S(1)} %get-tuple-element.69.x_ref, bf16[3,6144,768]{2,1,0:T(8,128)(2,1)} %bitcast.75, f32[256,2304]{1,0:T(8,128)S(1)} %shard_map.124.refs_0_), custom_call_target="tpu_custom_call", output_to_operand_aliasing={{}: (3, {})} | custom-call | flops 1811939328 | bytes 11796480 | tf_op jit(solution)/shard_map/pallas_call | solution.py:55
  141.3 7.0 %collective-permute-done.15 = bf16[1536,256]{1,0:T(8,128)(2,1)S(1)} collective-permute-done((bf16[1536,256]{1,0:T(8,128)(2,1)S(1)}, bf16[1536,256]{1,0:T(8,128)(2,1)S(1)}, u32[]{:S(2)}, u32[]{:S(2)}) %collective-permute-start.15) | collective-permute-done | bytes 786464 | tf_op jit(solution)/shard_map/ppermute | solution.py:372
  150.6 5.3 %shard_map.126.proj_ref = f32[256,2304]{1,0:T(8,128)S(1)} custom-call(s32[1]{0:T(128)} %bitcast.5.at_ref, bf16[1536,256]{1,0:T(8,128)(2,1)S(1)} %copy-done.2, bf16[3,6144,768]{2,1,0:T(8,128)(2,1)} %bitcast.76, f32[256,2304]{1,0:T(8,128)S(1)} %shard_map.125.refs_0_), custom_call_target="tpu_custom_call", output_to_operand_aliasing={{}: (3, {})} | custom-call | flops 1811939328 | bytes 11796480 | tf_op jit(solution)/shard_map/pallas_call | solution.py:55
  157.5 6.0 %shard_map.128 = bf16[4,1536,256]{2,1,0:T(8,128)(2,1)S(1)} custom-call(bf16[256,768]{1,0:T(8,128)(2,1)S(1)} %shard_map.127.x_ref, bf16[1,6144,768]{2,1,0:T(8,128)(2,1)} %bitcast.79), custom_call_target="tpu_custom_call" | custom-call | flops 2415919104 | bytes 12582912 | tf_op jit(solution)/shard_map/pallas_call | solution.py:154
  167.4 4.7 %all-to-all-start.2 = ((bf16[8,768,256]{2,1,0:T(8,128)(2,1)}), bf16[8,768,256]{2,1,0:T(8,128)(2,1)}, u32[]{:S(2)}, u32[]{:S(2)}) async-start(bf16[8,768,256]{2,1,0:T(8,128)(2,1)} %bitcast.80), calls=%async_computation.3 | async-start | bytes 6291456 | tf_op jit(solution)/shard_map/all_to_all | solution.py:389
  174.6 5.4 %shard_map.129.x_ref.refs_0_ = bf16[256,3072]{1,0:T(8,128)(2,1)} custom-call(f32[256,2304]{1,0:T(8,128)S(1)} %shard_map.126.proj_ref, s32[256,1]{1,0:T(8,128)S(1)} %copy-done.8, s32[1,256]{1,0:T(1,128)S(1)} %bitcast.71, f32[2,128]{1,0:T(2,128)S(1)} %copy-done.10, bf16[256,768]{1,0:T(8,128)(2,1)S(1)} %shard_map.121.d_ref), custom_call_target="tpu_custom_call" | custom-call | flops 805306368 | bytes 4718592 | tf_op jit(solution)/shard_map/pallas_call | solution.py:246
  183.3 27.2 %all-to-all-done.2.normed_ref = bf16[8,768,256]{2,1,0:T(8,128)(2,1)} async-done(((bf16[8,768,256]{2,1,0:T(8,128)(2,1)}), bf16[8,768,256]{2,1,0:T(8,128)(2,1)}, u32[]{:S(2)}, u32[]{:S(2)}) %all-to-all-start.2) | async-done | bytes 3145760 | tf_op jit(solution)/shard_map/all_to_all | solution.py:389
  210.5 17.5 %shard_map.130 = (bf16[4,1536,256]{2,1,0:T(8,128)(2,1)}, f32[2,256]{1,0:T(2,128)S(1)}) custom-call(bf16[256,3072]{1,0:T(8,128)(2,1)} %shard_map.129.x_ref.refs_0_, bf16[3,6144,768]{2,1,0:T(8,128)(2,1)} %bitcast.77, f32[6144,1]{1,0:T(8,128)} %copy.29.refs_0_, bf16[4,1536,256]{2,1,0:T(8,128)(2,1)} %bitcast_dynamic-update-slice_fusion.refs_1_), custom_call_target="tpu_custom_call" | custom-call | flops 7247757312 | bytes 31457280 | tf_op jit(solution)/shard_map/pallas_call | solution.py:154
  228.1 14.7 %collective-permute-done.17.refs_4_ = bf16[256,3072]{1,0:T(8,128)(2,1)} collective-permute-done((bf16[256,3072]{1,0:T(8,128)(2,1)}, bf16[256,3072]{1,0:T(8,128)(2,1)}, u32[]{:S(2)}, u32[]{:S(2)}) %collective-permute-start.17) | collective-permute-done | bytes 1572896 | tf_op jit(solution)/shard_map/ppermute | solution.py:331
  245.0 3.4 %collective-permute-done.20.refs_3_ = bf16[256,3072]{1,0:T(8,128)(2,1)S(1)} collective-permute-done((bf16[256,3072]{1,0:T(8,128)(2,1)S(1)}, bf16[256,3072]{1,0:T(8,128)(2,1)S(1)}, u32[]{:S(2)}, u32[]{:S(2)}) %collective-permute-start.20) | collective-permute-done | bytes 1572896 | tf_op jit(solution)/shard_map/ppermute | solution.py:331
  250.7 13.4 %shard_map.131.refs_2_ = f32[4,768,768]{2,1,0:T(8,128)} custom-call(bf16[8,768,256]{2,1,0:T(8,128)(2,1)} %all-to-all-done.2.normed_ref, bf16[8,768,256]{2,1,0:T(8,128)(2,1)} %all-to-all-done.1.cot_ref, bf16[256,3072]{1,0:T(8,128)(2,1)} %shard_map.129.x_ref.refs_0_, bf16[256,3072]{1,0:T(8,128)(2,1)} %collective-permute-done.16.refs_1_, ...), custom_call_target="tpu_custom_call" | custom-call | flops 7247757312 | bytes 15728640 | tf_op jit(solution)/shard_map/pallas_call | solution.py:301
  264.6 4.4 %collective-permute-start.23 = (f32[2,256]{1,0:T(2,128)S(1)}, f32[2,256]{1,0:T(2,128)S(1)}, u32[]{:S(2)}, u32[]{:S(2)}) collective-permute-start(f32[2,256]{1,0:T(2,128)S(1)} %get-tuple-element.51), channel_id=1, source_target_pairs={{0,1},{1,0},{2,3},{3,2},{4,5},{5,4},{6,7},{7,6},{8,9},{9,8},{10,11... | collective-permute-start | bytes 6152 | tf_op jit(solution)/shard_map/ppermute | solution.py:331
  272.6 10.8 %shard_map.132 = (bf16[3,768,768]{2,1,0:T(8,128)(2,1)}, bf16[768,768]{1,0:T(8,128)(2,1)}) custom-call(bf16[8,768,256]{2,1,0:T(8,128)(2,1)} %all-to-all-done.2.normed_ref, bf16[8,768,256]{2,1,0:T(8,128)(2,1)} %all-to-all-done.1.cot_ref, bf16[256,3072]{1,0:T(8,128)(2,1)} %collective-permute-done.19.refs_0_, ...), custom_call_target="tpu_custom_call" | custom-call | flops 2415919104 | bytes 9437184 | tf_op jit(solution)/shard_map/pallas_call | solution.py:301
  (159 shorter events, 59.5 us)
Async XLA Ops:
  7.2 83.9 %all-gather.3.cloned.1.call-start = ((), (), s32[]{:S(2)}) async-start(), calls=%async_computation.7 | async-start | bytes 3932160 | tf_op jit(solution)/shard_map/all_gather | solution.py:403
  12.0 10.0 %collective-permute-start.2 = (f32[2,256]{1,0:T(2,128)S(1)}, f32[2,256]{1,0:T(2,128)S(1)}, u32[]{:S(2)}, u32[]{:S(2)}) collective-permute-start(f32[2,256]{1,0:T(2,128)S(1)} %pad_maximum_fusion.1), channel_id=1, source_target_pairs={{0,3},{1,2},{2,1},{3,0},{4,7},{5,6},{6,5},{7,4},{8,11},{9,10},{10,... | collective-permute-start | bytes 6152 | tf_op jit(solution)/shard_map/ppermute | solution.py:331
  17.8 28.8 %all-to-all-start = ((bf16[8,64,1536]{2,1,0:T(8,128)(2,1)}), bf16[8,64,1536]{2,1,0:T(8,128)(2,1)S(1)}, u32[]{:S(2)}, u32[]{:S(2)}) async-start(bf16[8,64,1536]{2,1,0:T(8,128)(2,1)} %bitcast), calls=%async_computation | async-start | bytes 3145728 | tf_op jit(solution)/shard_map/all_to_all | solution.py:411
  22.5 19.8 %collective-permute-start.9 = (f32[3,64]{1,0:T(4,128)S(1)}, f32[3,64]{1,0:T(4,128)S(1)}, u32[]{:S(2)}, u32[]{:S(2)}) collective-permute-start(f32[3,64]{1,0:T(4,128)S(1)} %bitcast.98), channel_id=1, source_target_pairs={{0,28},{4,24},{8,20},{12,16},{16,12},{20,8},{24,4},{28,0},{1,29},{... | collective-permute-start | bytes 2312 | tf_op jit(solution)/shard_map/ppermute | solution.py:331
  25.3 17.7 %collective-permute-start.8 = (f32[3,64]{1,0:T(4,128)S(1)}, f32[3,64]{1,0:T(4,128)S(1)}, u32[]{:S(2)}, u32[]{:S(2)}) collective-permute-start(f32[3,64]{1,0:T(4,128)S(1)} %bitcast.97), channel_id=1, source_target_pairs={{0,24},{4,28},{8,16},{12,20},{16,8},{20,12},{24,0},{28,4},{1,25},{... | collective-permute-start | bytes 2312 | tf_op jit(solution)/shard_map/ppermute | solution.py:331
  25.6 18.6 %collective-permute-start.7 = (f32[3,64]{1,0:T(4,128)S(1)}, f32[3,64]{1,0:T(4,128)S(1)}, u32[]{:S(2)}, u32[]{:S(2)}) collective-permute-start(f32[3,64]{1,0:T(4,128)S(1)} %bitcast.92), channel_id=1, source_target_pairs={{0,20},{4,16},{8,28},{12,24},{16,4},{20,0},{24,12},{28,8},{1,21},{... | collective-permute-start | bytes 2312 | tf_op jit(solution)/shard_map/ppermute | solution.py:331
  27.0 17.2 %collective-permute-start.6 = (f32[3,64]{1,0:T(4,128)S(1)}, f32[3,64]{1,0:T(4,128)S(1)}, u32[]{:S(2)}, u32[]{:S(2)}) collective-permute-start(f32[3,64]{1,0:T(4,128)S(1)} %bitcast.93), channel_id=1, source_target_pairs={{0,16},{4,20},{8,24},{12,28},{16,0},{20,4},{24,8},{28,12},{1,17},{... | collective-permute-start | bytes 2312 | tf_op jit(solution)/shard_map/ppermute | solution.py:331
  27.3 16.9 %collective-permute-start.5 = (f32[3,64]{1,0:T(4,128)S(1)}, f32[3,64]{1,0:T(4,128)S(1)}, u32[]{:S(2)}, u32[]{:S(2)}) collective-permute-start(f32[3,64]{1,0:T(4,128)S(1)} %bitcast.94), channel_id=1, source_target_pairs={{0,12},{4,8},{8,4},{12,0},{16,28},{20,24},{24,20},{28,16},{1,13},{... | collective-permute-start | bytes 2312 | tf_op jit(solution)/shard_map/ppermute | solution.py:331
  49.1 37.4 %collective-permute-start.10 = (bf16[1536,256]{1,0:T(8,128)(2,1)S(1)}, bf16[1536,256]{1,0:T(8,128)(2,1)S(1)}, u32[]{:S(2)}, u32[]{:S(2)}) collective-permute-start(bf16[1536,256]{1,0:T(8,128)(2,1)S(1)} %get-tuple-element.71.x_ref), channel_id=1, source_target_pairs={{0,1},{1,2},{2,3},{4,5},{5,6},{6,7},{8,9},{9,10},{10,11},{12,13},{... | collective-permute-start | bytes 2359304 | tf_op jit(solution)/shard_map/ppermute | solution.py:371
  52.3 38.8 %collective-permute-start.11 = (bf16[1536,256]{1,0:T(8,128)(2,1)S(1)}, bf16[1536,256]{1,0:T(8,128)(2,1)}, u32[]{:S(2)}, u32[]{:S(2)}) collective-permute-start(bf16[1536,256]{1,0:T(8,128)(2,1)S(1)} %get-tuple-element.71.x_ref), channel_id=1, source_target_pairs={{1,0},{2,1},{3,2},{5,4},{6,5},{7,6},{9,8},{10,9},{11,10},{13,12},{... | collective-permute-start | bytes 2359304 | tf_op jit(solution)/shard_map/ppermute | solution.py:372
  91.1 58.3 %all-to-all-start.1 = ((bf16[8,768,256]{2,1,0:T(8,128)(2,1)}), bf16[8,768,256]{2,1,0:T(8,128)(2,1)}, u32[]{:S(2)}, u32[]{:S(2)}) async-start(bf16[8,768,256]{2,1,0:T(8,128)(2,1)} %bitcast.67), calls=%async_computation.1 | async-start | bytes 6291456 | tf_op jit(solution)/shard_map/all_to_all | solution.py:389
  95.7 187.6 %reduce-scatter.3.cloned.1.call-start = ((), (), s32[]{:S(2)}) async-start(), calls=%async_computation.5 | async-start | bytes 3932160 | tf_op jit(solution)/shard_map/reduce_scatter | solution.py:464
  102.0 15.3 %collective-permute-start.12 = (bf16[1536,256]{1,0:T(8,128)(2,1)S(1)}, bf16[1536,256]{1,0:T(8,128)(2,1)S(1)}, u32[]{:S(2)}, u32[]{:S(2)}) collective-permute-start(bf16[1536,256]{1,0:T(8,128)(2,1)S(1)} %copy-done.6), channel_id=1, source_target_pairs={{1,2},{2,3},{5,6},{6,7},{9,10},{10,11},{13,14},{14,15},{17,18},{18... | collective-permute-start | bytes 2359304 | tf_op jit(solution)/shard_map/ppermute | solution.py:371
  102.7 24.7 %collective-permute-start.14 = (bf16[1536,256]{1,0:T(8,128)(2,1)}, bf16[1536,256]{1,0:T(8,128)(2,1)S(1)}, u32[]{:S(2)}, u32[]{:S(2)}) collective-permute-start(bf16[1536,256]{1,0:T(8,128)(2,1)} %collective-permute-done.11.x_ref), channel_id=1, source_target_pairs={{1,0},{2,1},{5,4},{6,5},{9,8},{10,9},{13,12},{14,13},{17,16},{18,1... | collective-permute-start | bytes 2359304 | tf_op jit(solution)/shard_map/ppermute | solution.py:372
  117.3 24.0 %collective-permute-start.13 = (bf16[1536,256]{1,0:T(8,128)(2,1)S(1)}, bf16[1536,256]{1,0:T(8,128)(2,1)S(1)}, u32[]{:S(2)}, u32[]{:S(2)}) collective-permute-start(bf16[1536,256]{1,0:T(8,128)(2,1)S(1)} %collective-permute-done.12), channel_id=1, source_target_pairs={{2,3},{6,7},{10,11},{14,15},{18,19},{22,23},{26,27},{30,31}} | collective-permute-start | bytes 2359304 | tf_op jit(solution)/shard_map/ppermute | solution.py:371
  127.4 20.9 %collective-permute-start.15 = (bf16[1536,256]{1,0:T(8,128)(2,1)S(1)}, bf16[1536,256]{1,0:T(8,128)(2,1)S(1)}, u32[]{:S(2)}, u32[]{:S(2)}) collective-permute-start(bf16[1536,256]{1,0:T(8,128)(2,1)S(1)} %collective-permute-done.14), channel_id=1, source_target_pairs={{1,0},{5,4},{9,8},{13,12},{17,16},{21,20},{25,24},{29,28}} | collective-permute-start | bytes 2359304 | tf_op jit(solution)/shard_map/ppermute | solution.py:372
  167.4 43.1 %all-to-all-start.2 = ((bf16[8,768,256]{2,1,0:T(8,128)(2,1)}), bf16[8,768,256]{2,1,0:T(8,128)(2,1)}, u32[]{:S(2)}, u32[]{:S(2)}) async-start(bf16[8,768,256]{2,1,0:T(8,128)(2,1)} %bitcast.80), calls=%async_computation.3 | async-start | bytes 6291456 | tf_op jit(solution)/shard_map/all_to_all | solution.py:389
  172.1 114.4 %reduce-scatter.5.cloned.1.call-start = ((), (), s32[]{:S(2)}) async-start(), calls=%async_computation.6 | async-start | bytes 3932160 | tf_op jit(solution)/shard_map/reduce_scatter | solution.py:470
  180.0 48.0 %collective-permute-start.16 = (bf16[256,3072]{1,0:T(8,128)(2,1)}, bf16[256,3072]{1,0:T(8,128)(2,1)}, u32[]{:S(2)}, u32[]{:S(2)}) collective-permute-start(bf16[256,3072]{1,0:T(8,128)(2,1)} %shard_map.129.x_ref.refs_0_), channel_id=1, source_target_pairs={{0,4},{4,0},{8,12},{12,8},{16,20},{20,16},{24,28},{28,24},{1,5},{5... | collective-permute-start | bytes 4718600 | tf_op jit(solution)/shard_map/ppermute | solution.py:331
  180.1 62.6 %collective-permute-start.17 = (bf16[256,3072]{1,0:T(8,128)(2,1)}, bf16[256,3072]{1,0:T(8,128)(2,1)}, u32[]{:S(2)}, u32[]{:S(2)}) collective-permute-start(bf16[256,3072]{1,0:T(8,128)(2,1)} %shard_map.129.x_ref.refs_0_), channel_id=1, source_target_pairs={{0,16},{4,20},{8,24},{12,28},{16,0},{20,4},{24,8},{28,12},{1,17},{... | collective-permute-start | bytes 4718600 | tf_op jit(solution)/shard_map/ppermute | solution.py:331
  181.8 60.9 %collective-permute-start.18 = (bf16[256,3072]{1,0:T(8,128)(2,1)}, bf16[256,3072]{1,0:T(8,128)(2,1)S(1)}, u32[]{:S(2)}, u32[]{:S(2)}) collective-permute-start(bf16[256,3072]{1,0:T(8,128)(2,1)} %shard_map.129.x_ref.refs_0_), channel_id=1, source_target_pairs={{0,8},{4,12},{8,0},{12,4},{16,24},{20,28},{24,16},{28,20},{1,9},{5... | collective-permute-start | bytes 4718600 | tf_op jit(solution)/shard_map/ppermute | solution.py:331
  243.5 20.7 %collective-permute-start.19 = (bf16[256,3072]{1,0:T(8,128)(2,1)S(1)}, bf16[256,3072]{1,0:T(8,128)(2,1)}, u32[]{:S(2)}, u32[]{:S(2)}) collective-permute-start(bf16[256,3072]{1,0:T(8,128)(2,1)S(1)} %broadcast_select_fusion), channel_id=1, source_target_pairs={{0,16},{4,12},{8,24},{12,4},{16,0},{20,28},{24,8},{28,20},{1,17},{... | collective-permute-start | bytes 4718600 | tf_op jit(solution)/shard_map/ppermute | solution.py:359
  264.1 8.4 %collective-permute-start.22 = (bf16[256,3072]{1,0:T(8,128)(2,1)}, bf16[256,3072]{1,0:T(8,128)(2,1)S(1)}, u32[]{:S(2)}, u32[]{:S(2)}) collective-permute-start(bf16[256,3072]{1,0:T(8,128)(2,1)} %collective-permute-done.19.refs_0_), channel_id=1, source_target_pairs={{0,4},{4,0},{8,12},{12,8},{16,20},{20,16},{24,28},{28,24},{1,5},{5... | collective-permute-start | bytes 4718600 | tf_op jit(solution)/shard_map/ppermute | solution.py:331
  264.6 7.9 %collective-permute-start.23 = (f32[2,256]{1,0:T(2,128)S(1)}, f32[2,256]{1,0:T(2,128)S(1)}, u32[]{:S(2)}, u32[]{:S(2)}) collective-permute-start(f32[2,256]{1,0:T(2,128)S(1)} %get-tuple-element.51), channel_id=1, source_target_pairs={{0,1},{1,0},{2,3},{3,2},{4,5},{5,4},{6,7},{7,6},{8,9},{9,8},{10,11... | collective-permute-start | bytes 6152 | tf_op jit(solution)/shard_map/ppermute | solution.py:331
  (34 other events, 180.5 us)
Sparse Core Ops, SparseCore 0:
  10.1 79.0 all-gather.2
  165.3 58.4 reduce-scatter.2
  228.2 58.3 reduce-scatter.4

commit v8 on v7

--- a/solution.py
+++ b/solution.py
@@ -442,17 +442,20 @@
     unit_rows = (packed.astype(jnp.float32) - mean) * rstd
     normed_part = (unit_rows * my_gain).astype(jnp.bfloat16)
 
-    blocks, whole_cot = line_blocks(normed_part, "mp", whole_cot)
+    projected = add_block(None, normed_part, w_t, my_index)
+    blocks, (whole_cot, projected) = line_blocks(normed_part, "mp", (whole_cot, projected))
     d_heads = project(whole_cot, w_out_t, jnp.bfloat16)
-    cot_cols = columns_to_owner(whole_cot, "dp")
-    projected = None
     normed = jnp.zeros((parts, part_width, group_rows), jnp.bfloat16)
     for order, (at, there, block) in enumerate(blocks):
         if order == len(blocks) - 1:
             block, cot_cols, d_heads, projected = lax.optimization_barrier(
                 (block, cot_cols, d_heads, projected)
             )
-        projected = add_block(projected, block, w_t, at)
+        if order > 0:
+            projected = add_block(projected, block, w_t, at)
+        if order == 1:
+            projected, late_cot = lax.optimization_barrier((projected, whole_cot))
+            cot_cols = columns_to_owner(late_cot, "dp")
         if there is not None:
             at, block = jnp.where(there, at, my_index), jnp.where(there, block, normed_part)
         normed = lax.dynamic_update_slice(normed, block[None], (at, 0, 0))

time: 297 us -> 297 us (level)
  waiting for transfers between devices: 117 us -> 112 us
    ppermute x3, waiting for transfers between devices: 32.9 us -> 26.8 us  [line_blocks(): lax.ppermute(right, axis, [(at, at + 1) for at in range(step - 1, count -...]
    unnamed x63 -> x55, local copies, waits for them, and re-layouts: 10.7 us -> 13.3 us
  transfers between devices with their start and end apart: 32 -> 32, of which waited for: 13 -> 13; matrix products, arithmetic and copies ran while one was open for 6% -> 7% of each run, Pallas kernels for 26% -> 23%
where the time goes in v8:
time: 297 us; the launch traced here: 296 us
  waiting for transfers between devices  112 us (38%)
  Pallas kernels  88.9 us (30%)
  starting transfers between devices  46.2 us (16%)
  local copies, waits for them, and re-layouts  17.6 us (6%)
  between operations  14.4 us (5%)
  other arithmetic  12.6 us (4%)
  matrix products  3.72 us (1%)
    ppermute x19, waiting for transfers between devices, flip(): return lax.ppermute(values, axis, [(at, at ^ bit) for at in range(count)])  36 us
    all_to_all x2, waiting for transfers between devices, columns_to_owner(): return lax.all_to_all(cut, axis, 0, 0, tiled=True)  27.2 us
    pallas_call x5, Pallas kernels, add_block(): pl.pallas_call(functools.partial(add_block_kernel, total is None), grid_s...  26.8 us
    ppermute x3, waiting for transfers between devices, line_blocks(): lax.ppermute(right, axis, [(at, at + 1) for at in range(step - 1, count -...  26.8 us
    pallas_call x2, Pallas kernels, weight_grads(): pl.pallas_call(functools.partial(weight_kernel, keys, scale), grid=(4,),...  24.2 us
    pallas_call x2, Pallas kernels, expand(): pl.pallas_call(functools.partial(expand_kernel, kinds, width), grid=(part...  23.5 us
    ppermute x19, starting transfers between devices, flip(): return lax.ppermute(values, axis, [(at, at ^ bit) for at in range(count)])  21.7 us
    ppermute x3, waiting for transfers between devices, line_blocks(): lax.ppermute(left, axis, [(at, at - 1) for at in range(1, count - step +...  21.3 us
  transfers between devices with their start and end apart: 32, of which 13 were waited for; matrix products, arithmetic and copies ran while one was open for 7% of the time, Pallas kernels for 23%

profile of v8, /device:TPU:0, one launch (start us, length us, event | category | flops | bytes accessed | tf_op | source)
XLA Modules:
  0.0 295.5 jit_solution(14930899088677265513)
XLA Ops:
  12.0 5.1 %collective-permute-start.2 = (f32[2,256]{1,0:T(2,128)S(1)}, f32[2,256]{1,0:T(2,128)S(1)}, u32[]{:S(2)}, u32[]{:S(2)}) collective-permute-start(f32[2,256]{1,0:T(2,128)S(1)} %pad_maximum_fusion.1), channel_id=1, source_target_pairs={{0,3},{1,2},{2,1},{3,0},{4,7},{5,6},{6,5},{7,4},{8,11},{9,10},{10,... | collective-permute-start | bytes 6152 | tf_op jit(solution)/shard_map/ppermute | solution.py:331
  17.8 4.0 %all-to-all-start = ((bf16[8,64,1536]{2,1,0:T(8,128)(2,1)}), bf16[8,64,1536]{2,1,0:T(8,128)(2,1)S(1)}, u32[]{:S(2)}, u32[]{:S(2)}) async-start(bf16[8,64,1536]{2,1,0:T(8,128)(2,1)} %bitcast), calls=%async_computation | async-start | bytes 3145728 | tf_op jit(solution)/shard_map/all_to_all | solution.py:411
  28.8 13.6 %collective-permute-done.9 = f32[3,64]{1,0:T(4,128)S(1)} collective-permute-done((f32[3,64]{1,0:T(4,128)S(1)}, f32[3,64]{1,0:T(4,128)S(1)}, u32[]{:S(2)}, u32[]{:S(2)}) %collective-permute-start.9) | collective-permute-done | bytes 800 | tf_op jit(solution)/shard_map/ppermute | solution.py:331
  50.8 4.0 %collective-permute-start.10 = (bf16[1536,256]{1,0:T(8,128)(2,1)S(1)}, bf16[1536,256]{1,0:T(8,128)(2,1)}, u32[]{:S(2)}, u32[]{:S(2)}) collective-permute-start(bf16[1536,256]{1,0:T(8,128)(2,1)S(1)} %get-tuple-element.77.x_ref), channel_id=1, source_target_pairs={{0,1},{1,2},{2,3},{4,5},{5,6},{6,7},{8,9},{9,10},{10,11},{12,13},{... | collective-permute-start | bytes 2359304 | tf_op jit(solution)/shard_map/ppermute | solution.py:371
  56.1 5.3 %shard_map.121.refs_0_ = f32[256,2304]{1,0:T(8,128)S(1)} custom-call(s32[1]{0:T(128)} %bitcast.7.at_ref, bf16[1536,256]{1,0:T(8,128)(2,1)S(1)} %get-tuple-element.77.x_ref, bf16[3,6144,768]{2,1,0:T(8,128)(2,1)} %bitcast.72), custom_call_target="tpu_custom_call" | custom-call | flops 1811939328 | bytes 11796480 | tf_op jit(solution)/shard_map/pallas_call | solution.py:55
  61.4 26.8 %collective-permute-done.10.x_ref = bf16[1536,256]{1,0:T(8,128)(2,1)} collective-permute-done((bf16[1536,256]{1,0:T(8,128)(2,1)S(1)}, bf16[1536,256]{1,0:T(8,128)(2,1)}, u32[]{:S(2)}, u32[]{:S(2)}) %collective-permute-start.10) | collective-permute-done | bytes 786464 | tf_op jit(solution)/shard_map/ppermute | solution.py:371
  91.1 5.5 %shard_map.122.refs_0_ = f32[256,2304]{1,0:T(8,128)S(1)} custom-call(s32[1]{0:T(128)} %bitcast.9.at_ref, bf16[1536,256]{1,0:T(8,128)(2,1)} %collective-permute-done.10.x_ref, bf16[3,6144,768]{2,1,0:T(8,128)(2,1)} %bitcast.73, f32[256,2304]{1,0:T(8,128)S(1)} %shard_map.121.refs_0_), custom_call_target="tpu_custom_call", output_to_operand_aliasing={{}: (3, {})} | custom-call | flops 1811939328 | bytes 11796480 | tf_op jit(solution)/shard_map/pallas_call | solution.py:55
  96.6 4.5 %all-to-all-start.1 = ((bf16[8,768,256]{2,1,0:T(8,128)(2,1)}), bf16[8,768,256]{2,1,0:T(8,128)(2,1)}, u32[]{:S(2)}, u32[]{:S(2)}) async-start(bf16[8,768,256]{2,1,0:T(8,128)(2,1)} %bitcast.67), calls=%async_computation.1 | async-start | bytes 6291456 | tf_op jit(solution)/shard_map/all_to_all | solution.py:389
  106.9 6.2 %shard_map.123.d_ref = bf16[256,768]{1,0:T(8,128)(2,1)S(1)} custom-call(bf16[4,1536,256]{2,1,0:T(8,128)(2,1)S(1)} %bitcast.68, bf16[1,6144,768]{2,1,0:T(8,128)(2,1)} %bitcast.78), custom_call_target="tpu_custom_call" | custom-call | flops 2415919104 | bytes 12582912 | tf_op jit(solution)/shard_map/pallas_call | solution.py:105
  116.1 11.0 %collective-permute-done.14 = bf16[1536,256]{1,0:T(8,128)(2,1)S(1)} collective-permute-done((bf16[1536,256]{1,0:T(8,128)(2,1)}, bf16[1536,256]{1,0:T(8,128)(2,1)S(1)}, u32[]{:S(2)}, u32[]{:S(2)}) %collective-permute-start.14) | collective-permute-done | bytes 786464 | tf_op jit(solution)/shard_map/ppermute | solution.py:372
  128.5 5.5 %shard_map.124.refs_0_ = f32[256,2304]{1,0:T(8,128)S(1)} custom-call(s32[1]{0:T(128)} %bitcast.13.at_ref, bf16[1536,256]{1,0:T(8,128)(2,1)} %collective-permute-done.11.x_ref, bf16[3,6144,768]{2,1,0:T(8,128)(2,1)} %bitcast.74, f32[256,2304]{1,0:T(8,128)S(1)} %shard_map.122.refs_0_), custom_call_target="tpu_custom_call", output_to_operand_aliasing={{}: (3, {})} | custom-call | flops 1811939328 | bytes 11796480 | tf_op jit(solution)/shard_map/pallas_call | solution.py:55
  135.2 5.3 %shard_map.125.refs_0_ = f32[256,2304]{1,0:T(8,128)S(1)} custom-call(s32[1]{0:T(128)} %bitcast.12.at_ref, bf16[1536,256]{1,0:T(8,128)(2,1)S(1)} %get-tuple-element.75.x_ref, bf16[3,6144,768]{2,1,0:T(8,128)(2,1)} %bitcast.75, f32[256,2304]{1,0:T(8,128)S(1)} %shard_map.124.refs_0_), custom_call_target="tpu_custom_call", output_to_operand_aliasing={{}: (3, {})} | custom-call | flops 1811939328 | bytes 11796480 | tf_op jit(solution)/shard_map/pallas_call | solution.py:55
  140.5 7.5 %collective-permute-done.15 = bf16[1536,256]{1,0:T(8,128)(2,1)S(1)} collective-permute-done((bf16[1536,256]{1,0:T(8,128)(2,1)S(1)}, bf16[1536,256]{1,0:T(8,128)(2,1)S(1)}, u32[]{:S(2)}, u32[]{:S(2)}) %collective-permute-start.15) | collective-permute-done | bytes 786464 | tf_op jit(solution)/shard_map/ppermute | solution.py:372
  150.2 5.3 %shard_map.126.proj_ref = f32[256,2304]{1,0:T(8,128)S(1)} custom-call(s32[1]{0:T(128)} %bitcast.5.at_ref, bf16[1536,256]{1,0:T(8,128)(2,1)S(1)} %copy-done.2, bf16[3,6144,768]{2,1,0:T(8,128)(2,1)} %bitcast.76, f32[256,2304]{1,0:T(8,128)S(1)} %shard_map.125.refs_0_), custom_call_target="tpu_custom_call", output_to_operand_aliasing={{}: (3, {})} | custom-call | flops 1811939328 | bytes 11796480 | tf_op jit(solution)/shard_map/pallas_call | solution.py:55
  157.2 6.0 %shard_map.128 = bf16[4,1536,256]{2,1,0:T(8,128)(2,1)S(1)} custom-call(bf16[256,768]{1,0:T(8,128)(2,1)S(1)} %shard_map.127.x_ref, bf16[1,6144,768]{2,1,0:T(8,128)(2,1)} %bitcast.79), custom_call_target="tpu_custom_call" | custom-call | flops 2415919104 | bytes 12582912 | tf_op jit(solution)/shard_map/pallas_call | solution.py:154
  167.0 4.7 %all-to-all-start.2 = ((bf16[8,768,256]{2,1,0:T(8,128)(2,1)}), bf16[8,768,256]{2,1,0:T(8,128)(2,1)}, u32[]{:S(2)}, u32[]{:S(2)}) async-start(bf16[8,768,256]{2,1,0:T(8,128)(2,1)} %bitcast.80), calls=%async_computation.3 | async-start | bytes 6291456 | tf_op jit(solution)/shard_map/all_to_all | solution.py:389
  174.2 5.4 %shard_map.129.x_ref.refs_0_ = bf16[256,3072]{1,0:T(8,128)(2,1)} custom-call(f32[256,2304]{1,0:T(8,128)S(1)} %shard_map.126.proj_ref, s32[256,1]{1,0:T(8,128)S(1)} %copy-done.6, s32[1,256]{1,0:T(1,128)S(1)} %bitcast.71, f32[2,128]{1,0:T(2,128)S(1)} %copy-done.8, bf16[256,768]{1,0:T(8,128)(2,1)S(1)} %shard_map.123.d_ref), custom_call_target="tpu_custom_call" | custom-call | flops 805306368 | bytes 4718592 | tf_op jit(solution)/shard_map/pallas_call | solution.py:246
  182.9 27.2 %all-to-all-done.2.normed_ref = bf16[8,768,256]{2,1,0:T(8,128)(2,1)} async-done(((bf16[8,768,256]{2,1,0:T(8,128)(2,1)}), bf16[8,768,256]{2,1,0:T(8,128)(2,1)}, u32[]{:S(2)}, u32[]{:S(2)}) %all-to-all-start.2) | async-done | bytes 3145760 | tf_op jit(solution)/shard_map/all_to_all | solution.py:389
  210.1 17.5 %shard_map.130 = (bf16[4,1536,256]{2,1,0:T(8,128)(2,1)}, f32[2,256]{1,0:T(2,128)S(1)}) custom-call(bf16[256,3072]{1,0:T(8,128)(2,1)} %shard_map.129.x_ref.refs_0_, bf16[3,6144,768]{2,1,0:T(8,128)(2,1)} %bitcast.77, f32[6144,1]{1,0:T(8,128)} %copy.29.refs_0_, bf16[4,1536,256]{2,1,0:T(8,128)(2,1)} %bitcast_dynamic-update-slice_fusion.refs_1_), custom_call_target="tpu_custom_call" | custom-call | flops 7247757312 | bytes 31457280 | tf_op jit(solution)/shard_map/pallas_call | solution.py:154
  227.7 14.7 %collective-permute-done.17.refs_4_ = bf16[256,3072]{1,0:T(8,128)(2,1)} collective-permute-done((bf16[256,3072]{1,0:T(8,128)(2,1)}, bf16[256,3072]{1,0:T(8,128)(2,1)}, u32[]{:S(2)}, u32[]{:S(2)}) %collective-permute-start.17) | collective-permute-done | bytes 1572896 | tf_op jit(solution)/shard_map/ppermute | solution.py:331
  244.6 3.4 %collective-permute-done.20.refs_3_ = bf16[256,3072]{1,0:T(8,128)(2,1)S(1)} collective-permute-done((bf16[256,3072]{1,0:T(8,128)(2,1)S(1)}, bf16[256,3072]{1,0:T(8,128)(2,1)S(1)}, u32[]{:S(2)}, u32[]{:S(2)}) %collective-permute-start.20) | collective-permute-done | bytes 1572896 | tf_op jit(solution)/shard_map/ppermute | solution.py:331
  250.3 13.5 %shard_map.131.refs_2_ = f32[4,768,768]{2,1,0:T(8,128)} custom-call(bf16[8,768,256]{2,1,0:T(8,128)(2,1)} %all-to-all-done.2.normed_ref, bf16[8,768,256]{2,1,0:T(8,128)(2,1)} %all-to-all-done.1.cot_ref, bf16[256,3072]{1,0:T(8,128)(2,1)} %shard_map.129.x_ref.refs_0_, bf16[256,3072]{1,0:T(8,128)(2,1)} %collective-permute-done.16.refs_1_, ...), custom_call_target="tpu_custom_call" | custom-call | flops 7247757312 | bytes 15728640 | tf_op jit(solution)/shard_map/pallas_call | solution.py:301
  264.2 4.4 %collective-permute-start.23 = (f32[2,256]{1,0:T(2,128)S(1)}, f32[2,256]{1,0:T(2,128)S(1)}, u32[]{:S(2)}, u32[]{:S(2)}) collective-permute-start(f32[2,256]{1,0:T(2,128)S(1)} %get-tuple-element.57), channel_id=1, source_target_pairs={{0,1},{1,0},{2,3},{3,2},{4,5},{5,4},{6,7},{7,6},{8,9},{9,8},{10,11... | collective-permute-start | bytes 6152 | tf_op jit(solution)/shard_map/ppermute | solution.py:331
  272.2 10.8 %shard_map.132 = (bf16[3,768,768]{2,1,0:T(8,128)(2,1)}, bf16[768,768]{1,0:T(8,128)(2,1)}) custom-call(bf16[8,768,256]{2,1,0:T(8,128)(2,1)} %all-to-all-done.2.normed_ref, bf16[8,768,256]{2,1,0:T(8,128)(2,1)} %all-to-all-done.1.cot_ref, bf16[256,3072]{1,0:T(8,128)(2,1)} %collective-permute-done.19.refs_0_, ...), custom_call_target="tpu_custom_call" | custom-call | flops 2415919104 | bytes 9437184 | tf_op jit(solution)/shard_map/pallas_call | solution.py:301
  (151 shorter events, 64.2 us)
Async XLA Ops:
  7.2 83.9 %all-gather.3.cloned.1.call-start = ((), (), s32[]{:S(2)}) async-start(), calls=%async_computation.7 | async-start | bytes 3932160 | tf_op jit(solution)/shard_map/all_gather | solution.py:403
  12.0 10.0 %collective-permute-start.2 = (f32[2,256]{1,0:T(2,128)S(1)}, f32[2,256]{1,0:T(2,128)S(1)}, u32[]{:S(2)}, u32[]{:S(2)}) collective-permute-start(f32[2,256]{1,0:T(2,128)S(1)} %pad_maximum_fusion.1), channel_id=1, source_target_pairs={{0,3},{1,2},{2,1},{3,0},{4,7},{5,6},{6,5},{7,4},{8,11},{9,10},{10,... | collective-permute-start | bytes 6152 | tf_op jit(solution)/shard_map/ppermute | solution.py:331
  17.8 28.8 %all-to-all-start = ((bf16[8,64,1536]{2,1,0:T(8,128)(2,1)}), bf16[8,64,1536]{2,1,0:T(8,128)(2,1)S(1)}, u32[]{:S(2)}, u32[]{:S(2)}) async-start(bf16[8,64,1536]{2,1,0:T(8,128)(2,1)} %bitcast), calls=%async_computation | async-start | bytes 3145728 | tf_op jit(solution)/shard_map/all_to_all | solution.py:411
  22.5 19.8 %collective-permute-start.9 = (f32[3,64]{1,0:T(4,128)S(1)}, f32[3,64]{1,0:T(4,128)S(1)}, u32[]{:S(2)}, u32[]{:S(2)}) collective-permute-start(f32[3,64]{1,0:T(4,128)S(1)} %bitcast.98), channel_id=1, source_target_pairs={{0,28},{4,24},{8,20},{12,16},{16,12},{20,8},{24,4},{28,0},{1,29},{... | collective-permute-start | bytes 2312 | tf_op jit(solution)/shard_map/ppermute | solution.py:331
  25.3 17.7 %collective-permute-start.8 = (f32[3,64]{1,0:T(4,128)S(1)}, f32[3,64]{1,0:T(4,128)S(1)}, u32[]{:S(2)}, u32[]{:S(2)}) collective-permute-start(f32[3,64]{1,0:T(4,128)S(1)} %bitcast.97), channel_id=1, source_target_pairs={{0,24},{4,28},{8,16},{12,20},{16,8},{20,12},{24,0},{28,4},{1,25},{... | collective-permute-start | bytes 2312 | tf_op jit(solution)/shard_map/ppermute | solution.py:331
  25.6 18.6 %collective-permute-start.7 = (f32[3,64]{1,0:T(4,128)S(1)}, f32[3,64]{1,0:T(4,128)S(1)}, u32[]{:S(2)}, u32[]{:S(2)}) collective-permute-start(f32[3,64]{1,0:T(4,128)S(1)} %bitcast.92), channel_id=1, source_target_pairs={{0,20},{4,16},{8,28},{12,24},{16,4},{20,0},{24,12},{28,8},{1,21},{... | collective-permute-start | bytes 2312 | tf_op jit(solution)/shard_map/ppermute | solution.py:331
  27.0 17.2 %collective-permute-start.6 = (f32[3,64]{1,0:T(4,128)S(1)}, f32[3,64]{1,0:T(4,128)S(1)}, u32[]{:S(2)}, u32[]{:S(2)}) collective-permute-start(f32[3,64]{1,0:T(4,128)S(1)} %bitcast.93), channel_id=1, source_target_pairs={{0,16},{4,20},{8,24},{12,28},{16,0},{20,4},{24,8},{28,12},{1,17},{... | collective-permute-start | bytes 2312 | tf_op jit(solution)/shard_map/ppermute | solution.py:331
  27.3 16.9 %collective-permute-start.5 = (f32[3,64]{1,0:T(4,128)S(1)}, f32[3,64]{1,0:T(4,128)S(1)}, u32[]{:S(2)}, u32[]{:S(2)}) collective-permute-start(f32[3,64]{1,0:T(4,128)S(1)} %bitcast.94), channel_id=1, source_target_pairs={{0,12},{4,8},{8,4},{12,0},{16,28},{20,24},{24,20},{28,16},{1,13},{... | collective-permute-start | bytes 2312 | tf_op jit(solution)/shard_map/ppermute | solution.py:331
  50.8 37.4 %collective-permute-start.10 = (bf16[1536,256]{1,0:T(8,128)(2,1)S(1)}, bf16[1536,256]{1,0:T(8,128)(2,1)}, u32[]{:S(2)}, u32[]{:S(2)}) collective-permute-start(bf16[1536,256]{1,0:T(8,128)(2,1)S(1)} %get-tuple-element.77.x_ref), channel_id=1, source_target_pairs={{0,1},{1,2},{2,3},{4,5},{5,6},{6,7},{8,9},{9,10},{10,11},{12,13},{... | collective-permute-start | bytes 2359304 | tf_op jit(solution)/shard_map/ppermute | solution.py:371
  54.8 36.3 %collective-permute-start.11 = (bf16[1536,256]{1,0:T(8,128)(2,1)S(1)}, bf16[1536,256]{1,0:T(8,128)(2,1)}, u32[]{:S(2)}, u32[]{:S(2)}) collective-permute-start(bf16[1536,256]{1,0:T(8,128)(2,1)S(1)} %get-tuple-element.77.x_ref), channel_id=1, source_target_pairs={{1,0},{2,1},{3,2},{5,4},{6,5},{7,6},{9,8},{10,9},{11,10},{13,12},{... | collective-permute-start | bytes 2359304 | tf_op jit(solution)/shard_map/ppermute | solution.py:372
  96.6 52.5 %all-to-all-start.1 = ((bf16[8,768,256]{2,1,0:T(8,128)(2,1)}), bf16[8,768,256]{2,1,0:T(8,128)(2,1)}, u32[]{:S(2)}, u32[]{:S(2)}) async-start(bf16[8,768,256]{2,1,0:T(8,128)(2,1)} %bitcast.67), calls=%async_computation.1 | async-start | bytes 6291456 | tf_op jit(solution)/shard_map/all_to_all | solution.py:389
  101.1 181.9 %reduce-scatter.3.cloned.1.call-start = ((), (), s32[]{:S(2)}) async-start(), calls=%async_computation.5 | async-start | bytes 3932160 | tf_op jit(solution)/shard_map/reduce_scatter | solution.py:467
  102.0 13.4 %collective-permute-start.12 = (bf16[1536,256]{1,0:T(8,128)(2,1)}, bf16[1536,256]{1,0:T(8,128)(2,1)S(1)}, u32[]{:S(2)}, u32[]{:S(2)}) collective-permute-start(bf16[1536,256]{1,0:T(8,128)(2,1)} %collective-permute-done.10.x_ref), channel_id=1, source_target_pairs={{1,2},{2,3},{5,6},{6,7},{9,10},{10,11},{13,14},{14,15},{17,18},{18... | collective-permute-start | bytes 2359304 | tf_op jit(solution)/shard_map/ppermute | solution.py:371
  102.7 24.4 %collective-permute-start.14 = (bf16[1536,256]{1,0:T(8,128)(2,1)}, bf16[1536,256]{1,0:T(8,128)(2,1)S(1)}, u32[]{:S(2)}, u32[]{:S(2)}) collective-permute-start(bf16[1536,256]{1,0:T(8,128)(2,1)} %collective-permute-done.11.x_ref), channel_id=1, source_target_pairs={{1,0},{2,1},{5,4},{6,5},{9,8},{10,9},{13,12},{14,13},{17,16},{18,1... | collective-permute-start | bytes 2359304 | tf_op jit(solution)/shard_map/ppermute | solution.py:372
  115.4 25.1 %collective-permute-start.13 = (bf16[1536,256]{1,0:T(8,128)(2,1)S(1)}, bf16[1536,256]{1,0:T(8,128)(2,1)S(1)}, u32[]{:S(2)}, u32[]{:S(2)}) collective-permute-start(bf16[1536,256]{1,0:T(8,128)(2,1)S(1)} %collective-permute-done.12), channel_id=1, source_target_pairs={{2,3},{6,7},{10,11},{14,15},{18,19},{22,23},{26,27},{30,31}} | collective-permute-start | bytes 2359304 | tf_op jit(solution)/shard_map/ppermute | solution.py:371
  127.1 20.9 %collective-permute-start.15 = (bf16[1536,256]{1,0:T(8,128)(2,1)S(1)}, bf16[1536,256]{1,0:T(8,128)(2,1)S(1)}, u32[]{:S(2)}, u32[]{:S(2)}) collective-permute-start(bf16[1536,256]{1,0:T(8,128)(2,1)S(1)} %collective-permute-done.14), channel_id=1, source_target_pairs={{1,0},{5,4},{9,8},{13,12},{17,16},{21,20},{25,24},{29,28}} | collective-permute-start | bytes 2359304 | tf_op jit(solution)/shard_map/ppermute | solution.py:372
  167.0 43.1 %all-to-all-start.2 = ((bf16[8,768,256]{2,1,0:T(8,128)(2,1)}), bf16[8,768,256]{2,1,0:T(8,128)(2,1)}, u32[]{:S(2)}, u32[]{:S(2)}) async-start(bf16[8,768,256]{2,1,0:T(8,128)(2,1)} %bitcast.80), calls=%async_computation.3 | async-start | bytes 6291456 | tf_op jit(solution)/shard_map/all_to_all | solution.py:389
  171.7 114.4 %reduce-scatter.5.cloned.1.call-start = ((), (), s32[]{:S(2)}) async-start(), calls=%async_computation.6 | async-start | bytes 3932160 | tf_op jit(solution)/shard_map/reduce_scatter | solution.py:473
  179.6 48.0 %collective-permute-start.16 = (bf16[256,3072]{1,0:T(8,128)(2,1)}, bf16[256,3072]{1,0:T(8,128)(2,1)}, u32[]{:S(2)}, u32[]{:S(2)}) collective-permute-start(bf16[256,3072]{1,0:T(8,128)(2,1)} %shard_map.129.x_ref.refs_0_), channel_id=1, source_target_pairs={{0,4},{4,0},{8,12},{12,8},{16,20},{20,16},{24,28},{28,24},{1,5},{5... | collective-permute-start | bytes 4718600 | tf_op jit(solution)/shard_map/ppermute | solution.py:331
  179.7 62.6 %collective-permute-start.17 = (bf16[256,3072]{1,0:T(8,128)(2,1)}, bf16[256,3072]{1,0:T(8,128)(2,1)}, u32[]{:S(2)}, u32[]{:S(2)}) collective-permute-start(bf16[256,3072]{1,0:T(8,128)(2,1)} %shard_map.129.x_ref.refs_0_), channel_id=1, source_target_pairs={{0,16},{4,20},{8,24},{12,28},{16,0},{20,4},{24,8},{28,12},{1,17},{... | collective-permute-start | bytes 4718600 | tf_op jit(solution)/shard_map/ppermute | solution.py:331
  181.4 60.9 %collective-permute-start.18 = (bf16[256,3072]{1,0:T(8,128)(2,1)}, bf16[256,3072]{1,0:T(8,128)(2,1)S(1)}, u32[]{:S(2)}, u32[]{:S(2)}) collective-permute-start(bf16[256,3072]{1,0:T(8,128)(2,1)} %shard_map.129.x_ref.refs_0_), channel_id=1, source_target_pairs={{0,8},{4,12},{8,0},{12,4},{16,24},{20,28},{24,16},{28,20},{1,9},{5... | collective-permute-start | bytes 4718600 | tf_op jit(solution)/shard_map/ppermute | solution.py:331
  243.1 20.7 %collective-permute-start.19 = (bf16[256,3072]{1,0:T(8,128)(2,1)S(1)}, bf16[256,3072]{1,0:T(8,128)(2,1)}, u32[]{:S(2)}, u32[]{:S(2)}) collective-permute-start(bf16[256,3072]{1,0:T(8,128)(2,1)S(1)} %broadcast_select_fusion), channel_id=1, source_target_pairs={{0,16},{4,12},{8,24},{12,4},{16,0},{20,28},{24,8},{28,20},{1,17},{... | collective-permute-start | bytes 4718600 | tf_op jit(solution)/shard_map/ppermute | solution.py:359
  263.7 8.4 %collective-permute-start.22 = (bf16[256,3072]{1,0:T(8,128)(2,1)}, bf16[256,3072]{1,0:T(8,128)(2,1)S(1)}, u32[]{:S(2)}, u32[]{:S(2)}) collective-permute-start(bf16[256,3072]{1,0:T(8,128)(2,1)} %collective-permute-done.19.refs_0_), channel_id=1, source_target_pairs={{0,4},{4,0},{8,12},{12,8},{16,20},{20,16},{24,28},{28,24},{1,5},{5... | collective-permute-start | bytes 4718600 | tf_op jit(solution)/shard_map/ppermute | solution.py:331
  264.2 7.9 %collective-permute-start.23 = (f32[2,256]{1,0:T(2,128)S(1)}, f32[2,256]{1,0:T(2,128)S(1)}, u32[]{:S(2)}, u32[]{:S(2)}) collective-permute-start(f32[2,256]{1,0:T(2,128)S(1)} %get-tuple-element.57), channel_id=1, source_target_pairs={{0,1},{1,0},{2,3},{3,2},{4,5},{5,4},{6,7},{7,6},{8,9},{9,8},{10,11... | collective-permute-start | bytes 6152 | tf_op jit(solution)/shard_map/ppermute | solution.py:331
  (30 other events, 120.9 us)
Sparse Core Ops, SparseCore 0:
  10.1 79.0 all-gather.2
  164.9 58.4 reduce-scatter.2
  227.8 58.3 reduce-scatter.4

commit v9 on v8

--- a/solution.py
+++ b/solution.py
@@ -372,6 +372,10 @@
         left = lax.ppermute(left, axis, [(at, at - 1) for at in range(1, count - step + 1)])
         if step == 1:
             right, left, beside = lax.optimization_barrier((right, left, beside))
+        if step == 2:
+            early = [block for _, _, block in blocks[1:]]
+            right, left, early = lax.optimization_barrier((right, left, early))
+            blocks[1:] = [entry[:2] + (block,) for entry, block in zip(blocks[1:], early)]
         over, under = me >= step, me + step < count
         if 2 * step >= count:
             at = jnp.where(over, me - step, jnp.minimum(me + step, count - 1))
@@ -445,6 +449,7 @@
     projected = add_block(None, normed_part, w_t, my_index)
     blocks, (whole_cot, projected) = line_blocks(normed_part, "mp", (whole_cot, projected))
     d_heads = project(whole_cot, w_out_t, jnp.bfloat16)
+    cot_cols = columns_to_owner(whole_cot, "dp")
     normed = jnp.zeros((parts, part_width, group_rows), jnp.bfloat16)
     for order, (at, there, block) in enumerate(blocks):
         if order == len(blocks) - 1:
@@ -453,9 +458,6 @@
             )
         if order > 0:
             projected = add_block(projected, block, w_t, at)
-        if order == 1:
-            projected, late_cot = lax.optimization_barrier((projected, whole_cot))
-            cot_cols = columns_to_owner(late_cot, "dp")
         if there is not None:
             at, block = jnp.where(there, at, my_index), jnp.where(there, block, normed_part)
         normed = lax.dynamic_update_slice(normed, block[None], (at, 0, 0))

time: 297 us -> 291 us (0.980)
  waiting for transfers between devices: 112 us -> 108 us
    ppermute x3, waiting for transfers between devices: 21.3 us -> 12.8 us  [line_blocks(): lax.ppermute(left, axis, [(at, at - 1) for at in range(1, count - step +...]
    reduce_scatter x1, waiting for transfers between devices: 0.67 us -> 3.97 us  [shards(): d_normed = lax.psum_scatter(d_part, 'mp', scatter_dimension=0, tiled=False)]
    unnamed x55 -> x61, local copies, waits for them, and re-layouts: 13.3 us -> 11.7 us
  transfers between devices with their start and end apart: 32 -> 32, of which waited for: 13 -> 13; matrix products, arithmetic and copies ran while one was open for 7% -> 7% of each run, Pallas kernels for 23% -> 26%
where the time goes in v9:
time: 291 us; the launch traced here: 290 us
  waiting for transfers between devices  108 us (37%)
  Pallas kernels  89.8 us (31%)
  starting transfers between devices  46.1 us (16%)
  local copies, waits for them, and re-layouts  16 us (5%)
  between operations  14.4 us (5%)
  other arithmetic  11.8 us (4%)
  matrix products  3.71 us (1%)
    ppermute x19, waiting for transfers between devices, flip(): return lax.ppermute(values, axis, [(at, at ^ bit) for at in range(count)])  35.9 us
    pallas_call x5, Pallas kernels, add_block(): pl.pallas_call(functools.partial(add_block_kernel, total is None), grid_s...  27.9 us
    ppermute x3, waiting for transfers between devices, line_blocks(): lax.ppermute(right, axis, [(at, at + 1) for at in range(step - 1, count -...  27.6 us
    all_to_all x2, waiting for transfers between devices, columns_to_owner(): return lax.all_to_all(cut, axis, 0, 0, tiled=True)  27.2 us
    pallas_call x2, Pallas kernels, weight_grads(): pl.pallas_call(functools.partial(weight_kernel, keys, scale), grid=(4,),...  24 us
    pallas_call x2, Pallas kernels, expand(): pl.pallas_call(functools.partial(expand_kernel, kinds, width), grid=(part...  23.4 us
    ppermute x19, starting transfers between devices, flip(): return lax.ppermute(values, axis, [(at, at ^ bit) for at in range(count)])  21.7 us
    ppermute x3, waiting for transfers between devices, line_blocks(): lax.ppermute(left, axis, [(at, at - 1) for at in range(1, count - step +...  12.8 us
  transfers between devices with their start and end apart: 32, of which 13 were waited for; matrix products, arithmetic and copies ran while one was open for 7% of the time, Pallas kernels for 26%

profile of v9, /device:TPU:0, one launch (start us, length us, event | category | flops | bytes accessed | tf_op | source)
XLA Modules:
  0.0 289.5 jit_solution(9086782538933037483)
XLA Ops:
  12.0 5.1 %collective-permute-start.2 = (f32[2,256]{1,0:T(2,128)S(1)}, f32[2,256]{1,0:T(2,128)S(1)}, u32[]{:S(2)}, u32[]{:S(2)}) collective-permute-start(f32[2,256]{1,0:T(2,128)S(1)} %pad_maximum_fusion.1), channel_id=1, source_target_pairs={{0,3},{1,2},{2,1},{3,0},{4,7},{5,6},{6,5},{7,4},{8,11},{9,10},{10,... | collective-permute-start | bytes 6152 | tf_op jit(solution)/shard_map/ppermute | solution.py:331
  17.8 4.0 %all-to-all-start = ((bf16[8,64,1536]{2,1,0:T(8,128)(2,1)}), bf16[8,64,1536]{2,1,0:T(8,128)(2,1)S(1)}, u32[]{:S(2)}, u32[]{:S(2)}) async-start(bf16[8,64,1536]{2,1,0:T(8,128)(2,1)} %bitcast), calls=%async_computation | async-start | bytes 3145728 | tf_op jit(solution)/shard_map/all_to_all | solution.py:415
  28.8 13.6 %collective-permute-done.9 = f32[3,64]{1,0:T(4,128)S(1)} collective-permute-done((f32[3,64]{1,0:T(4,128)S(1)}, f32[3,64]{1,0:T(4,128)S(1)}, u32[]{:S(2)}, u32[]{:S(2)}) %collective-permute-start.9) | collective-permute-done | bytes 800 | tf_op jit(solution)/shard_map/ppermute | solution.py:331
  49.1 3.2 %collective-permute-start.10 = (bf16[1536,256]{1,0:T(8,128)(2,1)S(1)}, bf16[1536,256]{1,0:T(8,128)(2,1)S(1)}, u32[]{:S(2)}, u32[]{:S(2)}) collective-permute-start(bf16[1536,256]{1,0:T(8,128)(2,1)S(1)} %get-tuple-element.81.x_ref), channel_id=1, source_target_pairs={{0,1},{1,2},{2,3},{4,5},{5,6},{6,7},{8,9},{9,10},{10,11},{12,13},{... | collective-permute-start | bytes 2359304 | tf_op jit(solution)/shard_map/ppermute | solution.py:371
  53.7 5.3 %shard_map.121.refs_0_ = f32[256,2304]{1,0:T(8,128)S(1)} custom-call(s32[1]{0:T(128)} %bitcast.7.at_ref, bf16[1536,256]{1,0:T(8,128)(2,1)S(1)} %get-tuple-element.81.x_ref, bf16[3,6144,768]{2,1,0:T(8,128)(2,1)} %bitcast.72), custom_call_target="tpu_custom_call" | custom-call | flops 1811939328 | bytes 11796480 | tf_op jit(solution)/shard_map/pallas_call | solution.py:55
  58.9 27.6 %collective-permute-done.10.x_ref = bf16[1536,256]{1,0:T(8,128)(2,1)S(1)} collective-permute-done((bf16[1536,256]{1,0:T(8,128)(2,1)S(1)}, bf16[1536,256]{1,0:T(8,128)(2,1)S(1)}, u32[]{:S(2)}, u32[]{:S(2)}) %collective-permute-start.10) | collective-permute-done | bytes 786464 | tf_op jit(solution)/shard_map/ppermute | solution.py:371
  87.4 3.6 %collective-permute-done.11.x_ref = bf16[1536,256]{1,0:T(8,128)(2,1)} collective-permute-done((bf16[1536,256]{1,0:T(8,128)(2,1)S(1)}, bf16[1536,256]{1,0:T(8,128)(2,1)}, u32[]{:S(2)}, u32[]{:S(2)}) %collective-permute-start.11) | collective-permute-done | bytes 786464 | tf_op jit(solution)/shard_map/ppermute | solution.py:372
  93.9 4.5 %all-to-all-start.1 = ((bf16[8,768,256]{2,1,0:T(8,128)(2,1)}), bf16[8,768,256]{2,1,0:T(8,128)(2,1)}, u32[]{:S(2)}, u32[]{:S(2)}) async-start(bf16[8,768,256]{2,1,0:T(8,128)(2,1)} %bitcast.67), calls=%async_computation.1 | async-start | bytes 6291456 | tf_op jit(solution)/shard_map/all_to_all | solution.py:393
  101.2 6.3 %shard_map.122.d_ref = bf16[256,768]{1,0:T(8,128)(2,1)S(1)} custom-call(bf16[4,1536,256]{2,1,0:T(8,128)(2,1)S(1)} %bitcast.68, bf16[1,6144,768]{2,1,0:T(8,128)(2,1)} %bitcast.78), custom_call_target="tpu_custom_call" | custom-call | flops 2415919104 | bytes 12582912 | tf_op jit(solution)/shard_map/pallas_call | solution.py:105
  107.5 9.1 %collective-permute-done.13 = bf16[1536,256]{1,0:T(8,128)(2,1)} collective-permute-done((bf16[1536,256]{1,0:T(8,128)(2,1)}, bf16[1536,256]{1,0:T(8,128)(2,1)}, u32[]{:S(2)}, u32[]{:S(2)}) %collective-permute-start.13) | collective-permute-done | bytes 786464 | tf_op jit(solution)/shard_map/ppermute | solution.py:372
  118.9 5.4 %shard_map.123.refs_0_ = f32[256,2304]{1,0:T(8,128)S(1)} custom-call(s32[1]{0:T(128)} %bitcast.13.at_ref, bf16[1536,256]{1,0:T(8,128)(2,1)S(1)} %copy-done.6, bf16[3,6144,768]{2,1,0:T(8,128)(2,1)} %bitcast.73, f32[256,2304]{1,0:T(8,128)S(1)} %shard_map.121.refs_0_), custom_call_target="tpu_custom_call", output_to_operand_aliasing={{}: (3, {})} | custom-call | flops 1811939328 | bytes 11796480 | tf_op jit(solution)/shard_map/pallas_call | solution.py:55
  125.9 5.5 %shard_map.124.refs_0_ = f32[256,2304]{1,0:T(8,128)S(1)} custom-call(s32[1]{0:T(128)} %bitcast.12.at_ref, bf16[1536,256]{1,0:T(8,128)(2,1)} %collective-permute-done.11.x_ref, bf16[3,6144,768]{2,1,0:T(8,128)(2,1)} %bitcast.74, f32[256,2304]{1,0:T(8,128)S(1)} %shard_map.123.refs_0_), custom_call_target="tpu_custom_call", output_to_operand_aliasing={{}: (3, {})} | custom-call | flops 1811939328 | bytes 11796480 | tf_op jit(solution)/shard_map/pallas_call | solution.py:55
  133.1 6.4 %shard_map.125.refs_0_ = f32[256,2304]{1,0:T(8,128)S(1)} custom-call(s32[1]{0:T(128)} %bitcast.11.at_ref, bf16[1536,256]{1,0:T(8,128)(2,1)S(1)} %get-tuple-element.79.x_ref, bf16[3,6144,768]{2,1,0:T(8,128)(2,1)} %bitcast.75, f32[256,2304]{1,0:T(8,128)S(1)} %shard_map.124.refs_0_), custom_call_target="tpu_custom_call", output_to_operand_aliasing={{}: (3, {})} | custom-call | flops 1811939328 | bytes 11796480 | tf_op jit(solution)/shard_map/pallas_call | solution.py:55
  141.8 5.3 %shard_map.126.proj_ref = f32[256,2304]{1,0:T(8,128)S(1)} custom-call(s32[1]{0:T(128)} %bitcast.5.at_ref, bf16[1536,256]{1,0:T(8,128)(2,1)S(1)} %copy-done.2, bf16[3,6144,768]{2,1,0:T(8,128)(2,1)} %bitcast.76, f32[256,2304]{1,0:T(8,128)S(1)} %shard_map.125.refs_0_), custom_call_target="tpu_custom_call", output_to_operand_aliasing={{}: (3, {})} | custom-call | flops 1811939328 | bytes 11796480 | tf_op jit(solution)/shard_map/pallas_call | solution.py:55
  148.7 6.0 %shard_map.128 = bf16[4,1536,256]{2,1,0:T(8,128)(2,1)S(1)} custom-call(bf16[256,768]{1,0:T(8,128)(2,1)S(1)} %shard_map.127.x_ref, bf16[1,6144,768]{2,1,0:T(8,128)(2,1)} %bitcast.79), custom_call_target="tpu_custom_call" | custom-call | flops 2415919104 | bytes 12582912 | tf_op jit(solution)/shard_map/pallas_call | solution.py:154
  158.6 4.6 %all-to-all-start.2 = ((bf16[8,768,256]{2,1,0:T(8,128)(2,1)}), bf16[8,768,256]{2,1,0:T(8,128)(2,1)}, u32[]{:S(2)}, u32[]{:S(2)}) async-start(bf16[8,768,256]{2,1,0:T(8,128)(2,1)} %bitcast.80), calls=%async_computation.3 | async-start | bytes 6291456 | tf_op jit(solution)/shard_map/all_to_all | solution.py:393
  165.7 5.4 %shard_map.129.x_ref.refs_0_ = bf16[256,3072]{1,0:T(8,128)(2,1)} custom-call(f32[256,2304]{1,0:T(8,128)S(1)} %shard_map.126.proj_ref, s32[256,1]{1,0:T(8,128)S(1)} %copy-done.8, s32[1,256]{1,0:T(1,128)S(1)} %bitcast.71, f32[2,128]{1,0:T(2,128)S(1)} %copy-done.10, bf16[256,768]{1,0:T(8,128)(2,1)S(1)} %shard_map.122.d_ref), custom_call_target="tpu_custom_call" | custom-call | flops 805306368 | bytes 4718592 | tf_op jit(solution)/shard_map/pallas_call | solution.py:246
  174.4 27.2 %all-to-all-done.2.normed_ref = bf16[8,768,256]{2,1,0:T(8,128)(2,1)} async-done(((bf16[8,768,256]{2,1,0:T(8,128)(2,1)}), bf16[8,768,256]{2,1,0:T(8,128)(2,1)}, u32[]{:S(2)}, u32[]{:S(2)}) %all-to-all-start.2) | async-done | bytes 3145760 | tf_op jit(solution)/shard_map/all_to_all | solution.py:393
  201.6 17.4 %shard_map.130 = (bf16[4,1536,256]{2,1,0:T(8,128)(2,1)}, f32[2,256]{1,0:T(2,128)S(1)}) custom-call(bf16[256,3072]{1,0:T(8,128)(2,1)} %shard_map.129.x_ref.refs_0_, bf16[3,6144,768]{2,1,0:T(8,128)(2,1)} %bitcast.77, f32[6144,1]{1,0:T(8,128)} %copy.29.refs_0_, bf16[4,1536,256]{2,1,0:T(8,128)(2,1)} %bitcast_dynamic-update-slice_fusion.refs_1_), custom_call_target="tpu_custom_call" | custom-call | flops 7247757312 | bytes 31457280 | tf_op jit(solution)/shard_map/pallas_call | solution.py:154
  219.1 14.8 %collective-permute-done.17.refs_4_ = bf16[256,3072]{1,0:T(8,128)(2,1)} collective-permute-done((bf16[256,3072]{1,0:T(8,128)(2,1)}, bf16[256,3072]{1,0:T(8,128)(2,1)}, u32[]{:S(2)}, u32[]{:S(2)}) %collective-permute-start.17) | collective-permute-done | bytes 1572896 | tf_op jit(solution)/shard_map/ppermute | solution.py:331
  236.1 3.4 %collective-permute-done.20.refs_3_ = bf16[256,3072]{1,0:T(8,128)(2,1)S(1)} collective-permute-done((bf16[256,3072]{1,0:T(8,128)(2,1)S(1)}, bf16[256,3072]{1,0:T(8,128)(2,1)S(1)}, u32[]{:S(2)}, u32[]{:S(2)}) %collective-permute-start.20) | collective-permute-done | bytes 1572896 | tf_op jit(solution)/shard_map/ppermute | solution.py:331
  241.8 13.5 %shard_map.131.refs_2_ = f32[4,768,768]{2,1,0:T(8,128)} custom-call(bf16[8,768,256]{2,1,0:T(8,128)(2,1)} %all-to-all-done.2.normed_ref, bf16[8,768,256]{2,1,0:T(8,128)(2,1)} %all-to-all-done.1.cot_ref, bf16[256,3072]{1,0:T(8,128)(2,1)} %shard_map.129.x_ref.refs_0_, bf16[256,3072]{1,0:T(8,128)(2,1)} %collective-permute-done.16.refs_1_, ...), custom_call_target="tpu_custom_call" | custom-call | flops 7247757312 | bytes 15728640 | tf_op jit(solution)/shard_map/pallas_call | solution.py:301
  262.6 10.6 %shard_map.132 = (bf16[3,768,768]{2,1,0:T(8,128)(2,1)}, bf16[768,768]{1,0:T(8,128)(2,1)}) custom-call(bf16[8,768,256]{2,1,0:T(8,128)(2,1)} %all-to-all-done.2.normed_ref, bf16[8,768,256]{2,1,0:T(8,128)(2,1)} %all-to-all-done.1.cot_ref, bf16[256,3072]{1,0:T(8,128)(2,1)} %collective-permute-done.19.refs_0_, ...), custom_call_target="tpu_custom_call" | custom-call | flops 2415919104 | bytes 9437184 | tf_op jit(solution)/shard_map/pallas_call | solution.py:301
  276.1 4.0 %reduce-scatter.5.cloned.1.call-done = bf16[1,1536,256]{2,1,0:T(8,128)(2,1)} async-done(((bf16[4,1536,256]{2,1,0:T(8,128)(2,1)}), bf16[1,1536,256]{2,1,0:T(8,128)(2,1)}) %reduce-scatter.5.cloned.1.call-update) | async-done | bytes 786448 | tf_op jit(solution)/shard_map/reduce_scatter | solution.py:475
  (157 shorter events, 63.2 us)
Async XLA Ops:
  7.2 83.9 %all-gather.3.cloned.1.call-start = ((), (), s32[]{:S(2)}) async-start(), calls=%async_computation.7 | async-start | bytes 3932160 | tf_op jit(solution)/shard_map/all_gather | solution.py:407
  12.0 10.0 %collective-permute-start.2 = (f32[2,256]{1,0:T(2,128)S(1)}, f32[2,256]{1,0:T(2,128)S(1)}, u32[]{:S(2)}, u32[]{:S(2)}) collective-permute-start(f32[2,256]{1,0:T(2,128)S(1)} %pad_maximum_fusion.1), channel_id=1, source_target_pairs={{0,3},{1,2},{2,1},{3,0},{4,7},{5,6},{6,5},{7,4},{8,11},{9,10},{10,... | collective-permute-start | bytes 6152 | tf_op jit(solution)/shard_map/ppermute | solution.py:331
  17.8 28.8 %all-to-all-start = ((bf16[8,64,1536]{2,1,0:T(8,128)(2,1)}), bf16[8,64,1536]{2,1,0:T(8,128)(2,1)S(1)}, u32[]{:S(2)}, u32[]{:S(2)}) async-start(bf16[8,64,1536]{2,1,0:T(8,128)(2,1)} %bitcast), calls=%async_computation | async-start | bytes 3145728 | tf_op jit(solution)/shard_map/all_to_all | solution.py:415
  22.5 19.8 %collective-permute-start.9 = (f32[3,64]{1,0:T(4,128)S(1)}, f32[3,64]{1,0:T(4,128)S(1)}, u32[]{:S(2)}, u32[]{:S(2)}) collective-permute-start(f32[3,64]{1,0:T(4,128)S(1)} %bitcast.98), channel_id=1, source_target_pairs={{0,28},{4,24},{8,20},{12,16},{16,12},{20,8},{24,4},{28,0},{1,29},{... | collective-permute-start | bytes 2312 | tf_op jit(solution)/shard_map/ppermute | solution.py:331
  25.3 17.7 %collective-permute-start.8 = (f32[3,64]{1,0:T(4,128)S(1)}, f32[3,64]{1,0:T(4,128)S(1)}, u32[]{:S(2)}, u32[]{:S(2)}) collective-permute-start(f32[3,64]{1,0:T(4,128)S(1)} %bitcast.97), channel_id=1, source_target_pairs={{0,24},{4,28},{8,16},{12,20},{16,8},{20,12},{24,0},{28,4},{1,25},{... | collective-permute-start | bytes 2312 | tf_op jit(solution)/shard_map/ppermute | solution.py:331
  25.6 18.6 %collective-permute-start.7 = (f32[3,64]{1,0:T(4,128)S(1)}, f32[3,64]{1,0:T(4,128)S(1)}, u32[]{:S(2)}, u32[]{:S(2)}) collective-permute-start(f32[3,64]{1,0:T(4,128)S(1)} %bitcast.92), channel_id=1, source_target_pairs={{0,20},{4,16},{8,28},{12,24},{16,4},{20,0},{24,12},{28,8},{1,21},{... | collective-permute-start | bytes 2312 | tf_op jit(solution)/shard_map/ppermute | solution.py:331
  27.0 17.2 %collective-permute-start.6 = (f32[3,64]{1,0:T(4,128)S(1)}, f32[3,64]{1,0:T(4,128)S(1)}, u32[]{:S(2)}, u32[]{:S(2)}) collective-permute-start(f32[3,64]{1,0:T(4,128)S(1)} %bitcast.93), channel_id=1, source_target_pairs={{0,16},{4,20},{8,24},{12,28},{16,0},{20,4},{24,8},{28,12},{1,17},{... | collective-permute-start | bytes 2312 | tf_op jit(solution)/shard_map/ppermute | solution.py:331
  27.3 16.9 %collective-permute-start.5 = (f32[3,64]{1,0:T(4,128)S(1)}, f32[3,64]{1,0:T(4,128)S(1)}, u32[]{:S(2)}, u32[]{:S(2)}) collective-permute-start(f32[3,64]{1,0:T(4,128)S(1)} %bitcast.94), channel_id=1, source_target_pairs={{0,12},{4,8},{8,4},{12,0},{16,28},{20,24},{24,20},{28,16},{1,13},{... | collective-permute-start | bytes 2312 | tf_op jit(solution)/shard_map/ppermute | solution.py:331
  49.1 37.4 %collective-permute-start.10 = (bf16[1536,256]{1,0:T(8,128)(2,1)S(1)}, bf16[1536,256]{1,0:T(8,128)(2,1)S(1)}, u32[]{:S(2)}, u32[]{:S(2)}) collective-permute-start(bf16[1536,256]{1,0:T(8,128)(2,1)S(1)} %get-tuple-element.81.x_ref), channel_id=1, source_target_pairs={{0,1},{1,2},{2,3},{4,5},{5,6},{6,7},{8,9},{9,10},{10,11},{12,13},{... | collective-permute-start | bytes 2359304 | tf_op jit(solution)/shard_map/ppermute | solution.py:371
  52.3 38.7 %collective-permute-start.11 = (bf16[1536,256]{1,0:T(8,128)(2,1)S(1)}, bf16[1536,256]{1,0:T(8,128)(2,1)}, u32[]{:S(2)}, u32[]{:S(2)}) collective-permute-start(bf16[1536,256]{1,0:T(8,128)(2,1)S(1)} %get-tuple-element.81.x_ref), channel_id=1, source_target_pairs={{1,0},{2,1},{3,2},{5,4},{6,5},{7,6},{9,8},{10,9},{11,10},{13,12},{... | collective-permute-start | bytes 2359304 | tf_op jit(solution)/shard_map/ppermute | solution.py:372
  91.1 16.4 %collective-permute-start.12 = (bf16[1536,256]{1,0:T(8,128)(2,1)}, bf16[1536,256]{1,0:T(8,128)(2,1)}, u32[]{:S(2)}, u32[]{:S(2)}) collective-permute-start(bf16[1536,256]{1,0:T(8,128)(2,1)} %copy-done.5), channel_id=1, source_target_pairs={{1,2},{2,3},{5,6},{6,7},{9,10},{10,11},{13,14},{14,15},{17,18},{18... | collective-permute-start | bytes 2359304 | tf_op jit(solution)/shard_map/ppermute | solution.py:371
  92.6 24.1 %collective-permute-start.13 = (bf16[1536,256]{1,0:T(8,128)(2,1)}, bf16[1536,256]{1,0:T(8,128)(2,1)}, u32[]{:S(2)}, u32[]{:S(2)}) collective-permute-start(bf16[1536,256]{1,0:T(8,128)(2,1)} %collective-permute-done.11.x_ref), channel_id=1, source_target_pairs={{1,0},{2,1},{5,4},{6,5},{9,8},{10,9},{13,12},{14,13},{17,16},{18,1... | collective-permute-start | bytes 2359304 | tf_op jit(solution)/shard_map/ppermute | solution.py:372
  93.9 46.7 %all-to-all-start.1 = ((bf16[8,768,256]{2,1,0:T(8,128)(2,1)}), bf16[8,768,256]{2,1,0:T(8,128)(2,1)}, u32[]{:S(2)}, u32[]{:S(2)}) async-start(bf16[8,768,256]{2,1,0:T(8,128)(2,1)} %bitcast.67), calls=%async_computation.1 | async-start | bytes 6291456 | tf_op jit(solution)/shard_map/all_to_all | solution.py:393
  98.4 174.7 %reduce-scatter.3.cloned.1.call-start = ((), (), s32[]{:S(2)}) async-start(), calls=%async_computation.5 | async-start | bytes 3932160 | tf_op jit(solution)/shard_map/reduce_scatter | solution.py:469
  116.7 22.8 %collective-permute-start.14 = (bf16[1536,256]{1,0:T(8,128)(2,1)}, bf16[1536,256]{1,0:T(8,128)(2,1)S(1)}, u32[]{:S(2)}, u32[]{:S(2)}) collective-permute-start(bf16[1536,256]{1,0:T(8,128)(2,1)} %collective-permute-done.12), channel_id=1, source_target_pairs={{2,3},{6,7},{10,11},{14,15},{18,19},{22,23},{26,27},{30,31}} | collective-permute-start | bytes 2359304 | tf_op jit(solution)/shard_map/ppermute | solution.py:371
  117.4 22.1 %collective-permute-start.15 = (bf16[1536,256]{1,0:T(8,128)(2,1)}, bf16[1536,256]{1,0:T(8,128)(2,1)S(1)}, u32[]{:S(2)}, u32[]{:S(2)}) collective-permute-start(bf16[1536,256]{1,0:T(8,128)(2,1)} %collective-permute-done.13), channel_id=1, source_target_pairs={{1,0},{5,4},{9,8},{13,12},{17,16},{21,20},{25,24},{29,28}} | collective-permute-start | bytes 2359304 | tf_op jit(solution)/shard_map/ppermute | solution.py:372
  158.6 43.0 %all-to-all-start.2 = ((bf16[8,768,256]{2,1,0:T(8,128)(2,1)}), bf16[8,768,256]{2,1,0:T(8,128)(2,1)}, u32[]{:S(2)}, u32[]{:S(2)}) async-start(bf16[8,768,256]{2,1,0:T(8,128)(2,1)} %bitcast.80), calls=%async_computation.3 | async-start | bytes 6291456 | tf_op jit(solution)/shard_map/all_to_all | solution.py:393
  163.2 116.9 %reduce-scatter.5.cloned.1.call-start = ((), (), s32[]{:S(2)}) async-start(), calls=%async_computation.6 | async-start | bytes 3932160 | tf_op jit(solution)/shard_map/reduce_scatter | solution.py:475
  171.1 48.0 %collective-permute-start.16 = (bf16[256,3072]{1,0:T(8,128)(2,1)}, bf16[256,3072]{1,0:T(8,128)(2,1)}, u32[]{:S(2)}, u32[]{:S(2)}) collective-permute-start(bf16[256,3072]{1,0:T(8,128)(2,1)} %shard_map.129.x_ref.refs_0_), channel_id=1, source_target_pairs={{0,4},{4,0},{8,12},{12,8},{16,20},{20,16},{24,28},{28,24},{1,5},{5... | collective-permute-start | bytes 4718600 | tf_op jit(solution)/shard_map/ppermute | solution.py:331
  171.2 62.6 %collective-permute-start.17 = (bf16[256,3072]{1,0:T(8,128)(2,1)}, bf16[256,3072]{1,0:T(8,128)(2,1)}, u32[]{:S(2)}, u32[]{:S(2)}) collective-permute-start(bf16[256,3072]{1,0:T(8,128)(2,1)} %shard_map.129.x_ref.refs_0_), channel_id=1, source_target_pairs={{0,16},{4,20},{8,24},{12,28},{16,0},{20,4},{24,8},{28,12},{1,17},{... | collective-permute-start | bytes 4718600 | tf_op jit(solution)/shard_map/ppermute | solution.py:331
  172.9 61.0 %collective-permute-start.18 = (bf16[256,3072]{1,0:T(8,128)(2,1)}, bf16[256,3072]{1,0:T(8,128)(2,1)S(1)}, u32[]{:S(2)}, u32[]{:S(2)}) collective-permute-start(bf16[256,3072]{1,0:T(8,128)(2,1)} %shard_map.129.x_ref.refs_0_), channel_id=1, source_target_pairs={{0,8},{4,12},{8,0},{12,4},{16,24},{20,28},{24,16},{28,20},{1,9},{5... | collective-permute-start | bytes 4718600 | tf_op jit(solution)/shard_map/ppermute | solution.py:331
  234.5 20.7 %collective-permute-start.19 = (bf16[256,3072]{1,0:T(8,128)(2,1)S(1)}, bf16[256,3072]{1,0:T(8,128)(2,1)}, u32[]{:S(2)}, u32[]{:S(2)}) collective-permute-start(bf16[256,3072]{1,0:T(8,128)(2,1)S(1)} %broadcast_select_fusion), channel_id=1, source_target_pairs={{0,16},{4,12},{8,24},{12,4},{16,0},{20,28},{24,8},{28,20},{1,17},{... | collective-permute-start | bytes 4718600 | tf_op jit(solution)/shard_map/ppermute | solution.py:359
  255.2 7.3 %collective-permute-start.22 = (bf16[256,3072]{1,0:T(8,128)(2,1)}, bf16[256,3072]{1,0:T(8,128)(2,1)S(1)}, u32[]{:S(2)}, u32[]{:S(2)}) collective-permute-start(bf16[256,3072]{1,0:T(8,128)(2,1)} %collective-permute-done.19.refs_0_), channel_id=1, source_target_pairs={{0,4},{4,0},{8,12},{12,8},{16,20},{20,16},{24,28},{28,24},{1,5},{5... | collective-permute-start | bytes 4718600 | tf_op jit(solution)/shard_map/ppermute | solution.py:331
  255.7 6.0 %collective-permute-start.24 = (f32[2,256]{1,0:T(2,128)S(1)}, f32[2,256]{1,0:T(2,128)S(1)}, u32[]{:S(2)}, u32[]{:S(2)}) collective-permute-start(f32[2,256]{1,0:T(2,128)S(1)} %get-tuple-element.61), channel_id=1, source_target_pairs={{0,2},{1,3},{2,0},{3,1},{4,6},{5,7},{6,4},{7,5},{8,10},{9,11},{10,... | collective-permute-start | bytes 6152 | tf_op jit(solution)/shard_map/ppermute | solution.py:331
  (33 other events, 151.4 us)
Sparse Core Ops, SparseCore 0:
  10.1 79.0 all-gather.2
  156.5 60.7 reduce-scatter.2
  219.6 60.4 reduce-scatter.4
